TPU v7x, 32 devices: a whole 2x2x4 slice. The times are simulated.
32 devices in a mesh: dp: 4 (over z), expert: 8 (over y, x, core).
Axes of the slice: x: 2, y: 2, z: 4, core: 2. Of those that a mesh axis runs over, the one named last changes fastest.
Arguments:
- tokens: bfloat16 [4096, 1024], P(('dp', 'expert')), may hold values from -6 to 6
- cotangent: bfloat16 [4096, 1024], P(('dp', 'expert')), may hold values from -6 to 6
- expert_ids: int32 [4096, 8], P(('dp', 'expert')), may hold values from 0 to 15, all different within a row; in each aligned block of 128 rows (0 to 127, 128 to 255, ...) at most 80 rows name the same one
- route_weights: float32 [4096, 8], P(('dp', 'expert')), may hold values from 0.05 to 0.25
- weight_in: bfloat16 [1024, 16, 768], P('dp', 'expert'), may hold values from -0.1875 to 0.1875
- weight_down: bfloat16 [384, 16, 1024], P('dp', 'expert'), may hold values from -0.3125 to 0.3125
Outputs:
- token_grad: bfloat16 [4096, 1024], P(('dp', 'expert'))
- grad_in: bfloat16 [1024, 16, 768], P('dp', 'expert')
Inputs may be any that keep to these rules, and one draw needn't show every extreme that they name: `expert_ids`: each token names 8 different experts. Among the 128 tokens of one device at most 80 name the same expert, a bound that some block reaches.
All inputs are finite; a program needn't handle non-finite values.
Results may differ from a plain program's by a relative error of at most 0.018.
Values may be sent and summed in bfloat16 or wider, within the bound.
No kernel may reach another device: no remote copies, remote signals or barrier semaphores. Data moves between devices by JAX's collectives and lax.ppermute only.
A program may use at most 64 MiB of HBM per device.

v0:
```python
import jax
import jax.numpy as jnp
from jax import lax
from jax.sharding import PartitionSpec as P


def on_device(tokens, cotangent, expert_ids, route_weights, weight_in, weight_down):
    token_count = tokens.shape[0]
    width = tokens.shape[1]
    route_count = expert_ids.shape[1]
    peers = lax.axis_size("expert")
    local_experts = weight_in.shape[1]
    experts = local_experts * peers
    capacity = 5 * token_count * route_count // (4 * experts)
    hidden_units = weight_down.shape[0] * lax.axis_size("dp")
    rows_expert = token_count * route_count * lax.axis_size("dp") // local_experts
    grad_scale = float(rows_expert) ** (-0.5)
    flat_ids = expert_ids.reshape(-1)
    one_hot = (flat_ids[:, None] == jnp.arange(experts, dtype=jnp.int32)[None, :]).astype(jnp.int32)
    ranks = jnp.cumsum(one_hot, axis=0) - 1
    slots = jnp.sum(ranks * one_hot, axis=1)
    target = flat_ids * capacity + slots
    sources = jnp.arange(token_count * route_count, dtype=jnp.int32) // route_count
    inverse = jnp.full((experts * capacity,), token_count, jnp.int32).at[target].set(sources)
    blank = jnp.zeros((1, width), jnp.bfloat16)
    send_tokens = jnp.concatenate([tokens, blank], 0)[inverse].reshape(
        peers, local_experts, capacity, width
    )
    send_grads = jnp.concatenate([cotangent, blank], 0)[inverse].reshape(
        peers, local_experts, capacity, width
    )
    arrived_tokens, arrived_grads = (
        lax.all_to_all(send_tokens, "expert", split_axis=0, concat_axis=0, tiled=True),
        lax.all_to_all(send_grads, "expert", split_axis=0, concat_axis=0, tiled=True),
    )
    full_in, full_down = (
        lax.all_gather(weight_in, "dp", axis=0, tiled=True),
        lax.all_gather(weight_down, "dp", axis=0, tiled=True),
    )
    gate_up = jnp.einsum(
        "secd,dei->seci", arrived_tokens, full_in, preferred_element_type=jnp.float32
    )
    hidden_grad = jnp.einsum(
        "secd,fed->secf", arrived_grads, full_down, preferred_element_type=jnp.float32
    )
    gate = gate_up[..., :hidden_units]
    upper = gate_up[..., hidden_units:]
    sigma = jax.nn.sigmoid(gate)
    grad_gate = hidden_grad * upper * sigma * (1.0 + gate * (1.0 - sigma))
    grad_up = hidden_grad * gate * sigma
    grad_mid = jnp.concatenate([grad_gate, grad_up], -1).astype(jnp.bfloat16)
    input_part = jnp.einsum("seci,dei->secd", grad_mid, full_in, preferred_element_type=jnp.float32)
    input_part = input_part.astype(jnp.bfloat16)
    returned = lax.all_to_all(
        input_part, "expert", split_axis=0, concat_axis=0, tiled=True
    ).reshape(experts * capacity, width)
    picked = returned[target].reshape(token_count, route_count, width)
    token_grad = jnp.sum(route_weights[:, :, None] * picked.astype(jnp.float32), axis=1).astype(
        jnp.bfloat16
    )
    grad_in = lax.psum_scatter(
        (
            jnp.einsum(
                "secd,seci->dei", arrived_tokens, grad_mid, preferred_element_type=jnp.float32
            )
            * grad_scale
        ).astype(jnp.bfloat16),
        "dp",
        scatter_dimension=0,
        tiled=True,
    )
    return (token_grad, grad_in)


def solution(mesh):
    placed = (
        P(("dp", "expert"), None),
        P(("dp", "expert"), None),
        P(("dp", "expert"), None),
        P(("dp", "expert"), None),
        P("dp", "expert", None),
        P("dp", "expert", None),
    )
    return jax.shard_map(
        on_device,
        mesh=mesh,
        in_specs=placed,
        out_specs=(P(("dp", "expert"), None), P("dp", "expert", None)),
        check_vma=False,
    )
```

profile of v0, /device:TPU:0, one launch (start us, length us, event | category | flops | bytes accessed | tf_op | source)
XLA Modules:
  0.0 193.4 jit_solution(3487394115446405456)
XLA Ops:
  7.2 0.0 copy-start.3
  7.2 0.0 copy-start.1
  7.2 0.0 all-gather.5.cloned.1.call-start
  7.2 2.1 %copy.34 = bf16[256,2,768]{2,0,1:T(8,128)(2,1)} copy(bf16[256,2,768]{2,1,0:T(2,128)(2,1)} %param.10) | data formatting | bytes 1572864 | tf_op args[4]
  9.4 0.0 all-gather.5.cloned.1.call-update
  9.4 0.8 copy.28
  10.2 0.1 eq.29
  10.3 0.1 eq.25
  10.4 4.5 %reduce-window.6 = s32[16,8,128]{2,1,0:T(8,128)S(1)} reduce-window(s32[16,8,128]{2,1,0:T(8,128)S(1)} %fusion.26, s32[]{:T(128)} %constant.33.clone.1), window={size=1x1x128 pad=0_0x0_0x127_0}, to_apply=%region_0.0 | reduce-window | flops 2080768 | bytes 131076 | tf_op jit(solution)/shard_map/reduce-window
  14.9 0.1 slice.22
  15.0 0.1 copy.30
  15.1 0.1 copy.31
  15.2 0.0 copy-done.3
  15.2 0.1 copy.27
  15.3 0.1 mul.55
  15.5 0.1 add_add_fusion
  15.6 4.3 %scatter_custom_fusion = s32[1280]{0:T(1024)S(1)} fusion(s32[1024]{0:T(1024)S(1)} %bitcast.64, s32[1024]{0:T(1024)S(1)} %add_select_fusion, s32[]{:T(128)} %constant.16.clone.1), kind=kCustom, calls=%fused_computation.45 | custom fusion | bytes 5124 | tf_op jit(solution)/shard_map/scatter | solution.py:24
  20.0 5.1 %gather_fusion.1 = bf16[1280,1024]{1,0:T(8,128)(2,1)} fusion(bf16[129,1024]{1,0:T(8,128)(2,1)S(1)} %concatenate.11, s32[2048]{0:T(1024)S(1)} %pad_clamp_fusion), kind=kCustom, calls=%fused_computation.1 | custom fusion | bytes 5248000 | tf_op jit(solution)/shard_map/gather | solution.py:26
  25.0 5.3 %all-to-all-start.1 = ((bf16[8,2,80,1024]{3,2,1,0:T(8,128)(2,1)}), bf16[8,2,80,1024]{3,2,1,0:T(8,128)(2,1)S(1)}, u32[]{:S(2)}, u32[]{:S(2)}) async-start(bf16[8,2,80,1024]{3,2,1,0:T(8,128)(2,1)} %bitcast.8), calls=%async_computation.1 | async-start | bytes 5242880 | tf_op jit(solution)/shard_map/all_to_all | solution.py:33
  30.3 0.0 all-gather.3.cloned.1.call-start
  30.4 0.0 copy-done
  30.4 0.8 copy.32
  31.2 0.0 all-gather.3.cloned.1.call-update
  31.3 5.1 %gather_fusion = bf16[1280,1024]{1,0:T(8,128)(2,1)} fusion(bf16[129,1024]{1,0:T(8,128)(2,1)S(1)} %concatenate.10, s32[2048]{0:T(1024)S(1)} %pad_clamp_fusion), kind=kCustom, calls=%fused_computation | custom fusion | bytes 5248000 | tf_op jit(solution)/shard_map/gather | solution.py:29
  36.4 26.3 %all-to-all-done.1 = bf16[8,2,80,1024]{3,2,1,0:T(8,128)(2,1)S(1)} async-done(((bf16[8,2,80,1024]{3,2,1,0:T(8,128)(2,1)}), bf16[8,2,80,1024]{3,2,1,0:T(8,128)(2,1)S(1)}, u32[]{:S(2)}, u32[]{:S(2)}) %all-to-all-start.1) | async-done | bytes 2621472 | tf_op jit(solution)/shard_map/all_to_all | solution.py:33
  62.6 4.4 %all-to-all-start = ((bf16[8,2,80,1024]{3,2,1,0:T(8,128)(2,1)}), bf16[8,2,80,1024]{3,2,1,0:T(8,128)(2,1)}, u32[]{:S(2)}, u32[]{:S(2)}) async-start(bf16[8,2,80,1024]{3,2,1,0:T(8,128)(2,1)} %bitcast.4), calls=%async_computation | async-start | bytes 5242880 | tf_op jit(solution)/shard_map/all_to_all | solution.py:34
  67.0 0.0 reduce-scatter.2.cloned.1.call-start
  67.1 9.3 %all-gather.5.cloned.1.call-done = bf16[1024,2,768]{2,0,1:T(8,128)(2,1)} async-done(((bf16[256,2,768]{2,0,1:T(8,128)(2,1)}), bf16[1024,2,768]{2,0,1:T(8,128)(2,1)}) %all-gather.5.cloned.1.call-update) | async-done | bytes 3145744 | tf_op jit(solution)/shard_map/all_gather | solution.py:37
  76.4 6.0 %fusion.11 = f32[8,2,80,768]{3,2,0,1:T(8,128)} fusion(bf16[1024,2,768]{2,0,1:T(8,128)(2,1)} %all-gather.5.cloned.1.call-done, bf16[8,2,80,1024]{3,2,1,0:T(8,128)(2,1)S(1)} %all-to-all-done.1), kind=kOutput, calls=%fused_computation.18 | convolution fusion | flops 2013265920 | bytes 9699328 | tf_op jit(solution)/shard_map/secd,dei->seci/dot_general | solution.py:40
  82.3 17.0 %all-to-all-done = bf16[8,2,80,1024]{3,2,1,0:T(8,128)(2,1)} async-done(((bf16[8,2,80,1024]{3,2,1,0:T(8,128)(2,1)}), bf16[8,2,80,1024]{3,2,1,0:T(8,128)(2,1)}, u32[]{:S(2)}, u32[]{:S(2)}) %all-to-all-start) | async-done | bytes 2621472 | tf_op jit(solution)/shard_map/all_to_all | solution.py:34
  99.3 14.4 %all-gather.3.cloned.1.call-done = bf16[384,2,1024]{2,0,1:T(8,128)(2,1)} async-done(((bf16[96,2,1024]{2,0,1:T(8,128)(2,1)}), bf16[384,2,1024]{2,0,1:T(8,128)(2,1)}) %all-gather.3.cloned.1.call-update) | async-done | bytes 1572880 | tf_op jit(solution)/shard_map/all_gather | solution.py:38
  113.7 5.3 %fusion.20 = (bf16[8,2,80,384]{3,2,0,1:T(8,128)(2,1)S(1)}, bf16[8,2,80,384]{3,2,0,1:T(8,128)(2,1)S(1)}) fusion(f32[8,2,80,768]{3,2,0,1:T(8,128)} %fusion.11, bf16[384,2,1024]{2,0,1:T(8,128)(2,1)} %all-gather.3.cloned.1.call-done, bf16[8,2,80,1024]{3,2,1,0:T(8,128)(2,1)} %all-to-all-done), kind=kOutput, calls=%fused_computation.22 | convolution fusion | flops 1013022720 | bytes 10092544 | tf_op jit(solution)/shard_map/secd,fed->secf/dot_general | solution.py:43
  119.1 0.0 copy-start.6
  119.1 0.0 copy-start.7
  119.1 1.0 copy-done.6
  120.1 0.3 copy-done.7
  120.4 4.1 %fusion.2 = bf16[1024,2,768]{0,2,1:T(8,128)(2,1)} fusion(bf16[8,2,80,1024]{3,2,1,0:T(8,128)(2,1)S(1)} %all-to-all-done.1, bf16[8,2,80,384]{3,2,0,1:T(8,128)(2,1)S(1)} %get-tuple-element.9, bf16[8,2,80,384]{3,2,0,1:T(8,128)(2,1)S(1)} %get-tuple-element.8), kind=kOutput, calls=%fused_computation.8 | convolution fusion | flops 2020343808 | bytes 7733248 | tf_op jit(solution)/shard_map/secd,seci->dei/dot_general | solution.py:63
  124.5 0.0 reduce-scatter.2.cloned.1.call-update
  124.6 1.9 copy-done.5
  126.4 3.7 %convert_bitcast_fusion = bf16[8,2,80,1024]{3,2,0,1:T(8,128)(2,1)S(1)} fusion(bf16[1024,2,768]{2,0,1:T(8,128)(2,1)S(1)} %copy-done.5, bf16[8,2,80,384]{3,2,0,1:T(8,128)(2,1)} %copy-done.7, bf16[8,2,80,384]{3,2,0,1:T(8,128)(2,1)} %copy-done.6), kind=kOutput, calls=%fused_computation.15 | convolution fusion | flops 2018508800 | bytes 7733248 | tf_op jit(solution)/shard_map/seci,dei->secd/dot_general | solution.py:52
  130.2 1.8 copy.36
  131.9 3.8 %all-to-all-start.2 = ((bf16[8,2,80,1024]{3,2,1,0:T(8,128)(2,1)}), bf16[8,2,80,1024]{3,2,1,0:T(8,128)(2,1)S(1)}, u32[]{:S(2)}, u32[]{:S(2)}) async-start(bf16[8,2,80,1024]{3,2,1,0:T(8,128)(2,1)} %copy.36), calls=%async_computation.2 | async-start | bytes 5242880 | tf_op jit(solution)/shard_map/all_to_all | solution.py:54
  135.7 0.1 copy.26
  135.8 32.1 %all-to-all-done.2 = bf16[8,2,80,1024]{3,2,1,0:T(8,128)(2,1)S(1)} async-done(((bf16[8,2,80,1024]{3,2,1,0:T(8,128)(2,1)}), bf16[8,2,80,1024]{3,2,1,0:T(8,128)(2,1)S(1)}, u32[]{:S(2)}, u32[]{:S(2)}) %all-to-all-start.2) | async-done | bytes 2621472 | tf_op jit(solution)/shard_map/all_to_all | solution.py:54
  168.0 5.3 %gather_fusion.2 = bf16[1024,1024]{1,0:T(8,128)(2,1)} fusion(bf16[1280,1024]{1,0:T(8,128)(2,1)S(1)} %bitcast.60, s32[1024]{0:T(1024)S(1)} %broadcast_clamp_fusion), kind=kCustom, calls=%fused_computation.2 | custom fusion | bytes 4198400 | tf_op jit(solution)/shard_map/gather | solution.py:57
  173.3 3.7 %fusion.1 = bf16[128,1024]{1,0:T(8,128)(2,1)} fusion(bf16[1024,1024]{1,0:T(8,128)(2,1)} %gather_fusion.2, f32[128,8]{1,0:T(8,128)S(1)} %copy.26), kind=kLoop, calls=%fused_computation.7 | loop fusion | flops 3014656 | bytes 2363392 | tf_op jit(solution)/shard_map/reduce_sum | solution.py:58
  177.0 6.9 %reduce-scatter.2.cloned.1.call-done = bf16[256,2,768]{0,2,1:T(8,128)(2,1)} async-done(((bf16[1024,2,768]{0,2,1:T(8,128)(2,1)}), bf16[256,2,768]{0,2,1:T(8,128)(2,1)}) %reduce-scatter.2.cloned.1.call-update) | async-done | bytes 786448 | tf_op jit(solution)/shard_map/reduce_scatter | solution.py:61
  183.8 3.0 %copy.38 = bf16[256,2,768]{2,1,0:T(2,128)(2,1)} copy(bf16[256,2,768]{0,2,1:T(8,128)(2,1)} %reduce-scatter.2.cloned.1.call-done) | data formatting | bytes 1572864
  (19 shorter events, 0.2 us)
Async XLA Ops:
  7.2 8.1 %copy-start.3 = (s32[128,8]{0,1:T(8,128)S(1)}, s32[128,8]{0,1:T(8,128)}, u32[]{:S(2)}) copy-start(s32[128,8]{0,1:T(8,128)} %param.8) | copy-start | bytes 12292
  7.2 8.3 %copy-start.1 = (bf16[128,1024]{1,0:T(8,128)(2,1)S(1)}, bf16[128,1024]{1,0:T(8,128)(2,1)}, u32[]{:S(2)}) copy-start(bf16[128,1024]{1,0:T(8,128)(2,1)} %param.6) | copy-start | bytes 786436
  7.2 69.2 %all-gather.5.cloned.1.call-start = ((), (), s32[]{:S(2)}) async-start(), calls=%async_computation.5 | async-start | bytes 3932160 | tf_op jit(solution)/shard_map/all_gather | solution.py:37
  25.0 5.4 %copy-start = (bf16[96,2,1024]{2,1,0:T(2,128)(2,1)S(1)}, bf16[96,2,1024]{2,1,0:T(2,128)(2,1)}, u32[]{:S(2)}) copy-start(bf16[96,2,1024]{2,1,0:T(2,128)(2,1)} %param.11) | copy-start | bytes 1179652
  25.0 6.2 %copy-start.2 = (bf16[128,1024]{1,0:T(8,128)(2,1)S(1)}, bf16[128,1024]{1,0:T(8,128)(2,1)}, u32[]{:S(2)}) copy-start(bf16[128,1024]{1,0:T(8,128)(2,1)} %param.7) | copy-start | bytes 786436
  25.0 37.6 %all-to-all-start.1 = ((bf16[8,2,80,1024]{3,2,1,0:T(8,128)(2,1)}), bf16[8,2,80,1024]{3,2,1,0:T(8,128)(2,1)S(1)}, u32[]{:S(2)}, u32[]{:S(2)}) async-start(bf16[8,2,80,1024]{3,2,1,0:T(8,128)(2,1)} %bitcast.8), calls=%async_computation.1 | async-start | bytes 5242880 | tf_op jit(solution)/shard_map/all_to_all | solution.py:33
  30.3 83.4 %all-gather.3.cloned.1.call-start = ((), (), s32[]{:S(2)}) async-start(), calls=%async_computation.4 | async-start | bytes 1966080 | tf_op jit(solution)/shard_map/all_gather | solution.py:38
  62.6 36.7 %all-to-all-start = ((bf16[8,2,80,1024]{3,2,1,0:T(8,128)(2,1)}), bf16[8,2,80,1024]{3,2,1,0:T(8,128)(2,1)}, u32[]{:S(2)}, u32[]{:S(2)}) async-start(bf16[8,2,80,1024]{3,2,1,0:T(8,128)(2,1)} %bitcast.4), calls=%async_computation | async-start | bytes 5242880 | tf_op jit(solution)/shard_map/all_to_all | solution.py:34
  67.0 116.8 %reduce-scatter.2.cloned.1.call-start = ((), (), s32[]{:S(2)}) async-start(), calls=%async_computation.6 | async-start | bytes 3932160 | tf_op jit(solution)/shard_map/reduce_scatter | solution.py:61
  119.1 1.0 copy-start.6
  119.1 1.3 copy-start.7
  124.5 1.9 copy-start.5
  131.9 3.8 %copy-start.4 = (f32[128,8]{0,1:T(8,128)S(1)}, f32[128,8]{0,1:T(8,128)}, u32[]{:S(2)}) copy-start(f32[128,8]{0,1:T(8,128)} %param.9) | copy-start | bytes 12292
  131.9 36.1 %all-to-all-start.2 = ((bf16[8,2,80,1024]{3,2,1,0:T(8,128)(2,1)}), bf16[8,2,80,1024]{3,2,1,0:T(8,128)(2,1)S(1)}, u32[]{:S(2)}, u32[]{:S(2)}) async-start(bf16[8,2,80,1024]{3,2,1,0:T(8,128)(2,1)} %copy.36), calls=%async_computation.2 | async-start | bytes 5242880 | tf_op jit(solution)/shard_map/all_to_all | solution.py:54
Sparse Core Ops, SparseCore 0:
  10.2 66.1 all-gather.4
  77.9 35.7 all-gather.2
  124.7 59.1 reduce-scatter.1
where the time goes:
time: 194 us; the launch traced here: 193 us
  waiting for transfers between devices  106 us (55%)
  local copies, waits for them, and re-layouts  32.3 us (17%)
  matrix products  19.1 us (10%)
  between operations  13.9 us (7%)
  starting transfers between devices  13.6 us (7%)
  other arithmetic  8.35 us (4%)
    all_to_all x1, waiting for transfers between devices, on_device(): lax.all_to_all(input_part, 'expert', split_axis=0, concat_axis=0, tiled=T...  32.1 us
    all_to_all x1, waiting for transfers between devices, on_device(): lax.all_to_all(send_tokens, 'expert', split_axis=0, concat_axis=0, tiled=...  26.3 us
    all_to_all x1, waiting for transfers between devices, on_device(): lax.all_to_all(send_grads, 'expert', split_axis=0, concat_axis=0, tiled=T...  17 us
    all_gather x1, waiting for transfers between devices, on_device(): lax.all_gather(weight_down, 'dp', axis=0, tiled=True)  14.4 us
    unnamed x21, local copies, waits for them, and re-layouts  10.1 us
    all_gather x1, waiting for transfers between devices, on_device(): lax.all_gather(weight_in, 'dp', axis=0, tiled=True)  9.29 us
    reduce_scatter x1, waiting for transfers between devices, on_device(): lax.psum_scatter((jnp.einsum('secd,seci->dei', arrived_tokens, grad_mid,...  6.87 us
    dot_general x1, matrix products, on_device(): jnp.einsum('secd,dei->seci', arrived_tokens, full_in, preferred_element_t...  5.96 us
  transfers between devices with their start and end apart: 6, of which 6 were waited for; matrix products, arithmetic and copies ran while one was open for 22% of the time, Pallas kernels for 0%

commit v1 on v0

--- a/solution.py
+++ b/solution.py
@@ -1,10 +1,14 @@
+import functools
+
 import jax
 import jax.numpy as jnp
 from jax import lax
+from jax.experimental import pallas as pl
+from jax.experimental.pallas import tpu as pltpu
 from jax.sharding import PartitionSpec as P
 
 
-def on_device(tokens, cotangent, expert_ids, route_weights, weight_in, weight_down):
+def by_routes(tokens, cotangent, expert_ids, route_weights, weight_in, weight_down):
     token_count = tokens.shape[0]
     width = tokens.shape[1]
     route_count = expert_ids.shape[1]
@@ -72,6 +76,293 @@
     return (token_grad, grad_in)
 
 
+LANES = 128
+VMEM = 24 * 2**20
+NT = (((1,), (1,)), ((), ()))
+HIDE = 1 << 34
+TN = (((0,), (0,)), ((), ()))
+
+
+def payload_kernel(tokens, cotangent, ids, weights, out):
+    count, width = tokens.shape
+    out[:, :width] = tokens[...]
+    out[:, width : 2 * width] = cotangent[...]
+    lane = lax.broadcasted_iota(jnp.int32, (LANES, count), 0)
+    n = LANES // 8
+    total = jnp.zeros((LANES, count), jnp.float32)
+    routed = jnp.zeros((LANES, count), jnp.float32)
+    for k in range(ids.shape[0]):
+        here = lane % n == ids[k : k + 1, :]
+        total = total + jnp.where(here, weights[k : k + 1, :], 0.0)
+        routed = routed + jnp.where(here, 1.0, 0.0)
+    top = total.astype(jnp.bfloat16).astype(jnp.float32)
+    rest = jnp.where(lane < 2 * n, total - top, jnp.where(lane < 3 * n, routed, 0.0))
+    out[:, 2 * width :] = jnp.where(lane < n, top, rest).T.astype(jnp.bfloat16)
+
+
+def payload_of(tokens, cotangent, ids, weights):
+    count, width = tokens.shape
+    return pl.pallas_call(
+        payload_kernel,
+        out_shape=jax.ShapeDtypeStruct((count, 2 * width + LANES), jnp.bfloat16),
+        cost_estimate=pl.CostEstimate(flops=1 << 20, bytes_accessed=2 << 20, transcendentals=0),
+        name="payload",
+    )(tokens, cotangent, ids.T, weights.T)
+
+
+def halves_kernel(place, weight, kept, given):
+    quarter = weight.shape[2] // 4
+
+    def part(k, out):
+        for a in range(2):
+            both = [weight[e, :, (2 * a + k) * quarter : (2 * a + k + 1) * quarter] for e in range(2)]
+            out[:, 2 * a * quarter : 2 * (a + 1) * quarter] = jnp.concatenate(both, 1)
+
+    for high in range(2):
+
+        @pl.when(place[0] // 2 == high)
+        def _():
+            part(high, kept)
+            part(1 - high, given)
+
+
+def halves(place, weight):
+    _, rows, cols = weight.shape
+    vmem = pl.BlockSpec(memory_space=pltpu.VMEM)
+    return pl.pallas_call(
+        halves_kernel,
+        in_specs=[pl.BlockSpec(memory_space=pltpu.SMEM), vmem],
+        out_specs=[vmem] * 2,
+        out_shape=[jax.ShapeDtypeStruct((rows, cols), jnp.bfloat16)] * 2,
+        cost_estimate=pl.CostEstimate(flops=HIDE, bytes_accessed=2 << 20, transcendentals=0),
+        name="halves",
+    )(place, weight)
+
+
+def join_kernel(place, own, got, far, out):
+    quarter = own.shape[1] // 4
+    mine = (own[...].astype(jnp.float32) + got[...].astype(jnp.float32)).astype(jnp.bfloat16)
+
+    def put(k, value):
+        for a in range(2):
+            for e in range(2):
+                at = (2 * a + k) * quarter
+                out[e, :, at : at + quarter] = value[:, (2 * a + e) * quarter : (2 * a + e + 1) * quarter]
+
+    for high in range(2):
+
+        @pl.when(place[0] // 2 == high)
+        def _():
+            put(high, mine)
+            put(1 - high, far[...])
+
+
+def join(place, own, got, far):
+    vmem = pl.BlockSpec(memory_space=pltpu.VMEM)
+    return pl.pallas_call(
+        join_kernel,
+        in_specs=[pl.BlockSpec(memory_space=pltpu.SMEM)] + [vmem] * 3,
+        out_specs=vmem,
+        out_shape=jax.ShapeDtypeStruct((2,) + own.shape, jnp.bfloat16),
+        cost_estimate=pl.CostEstimate(flops=1 << 20, bytes_accessed=2 << 20, transcendentals=0),
+        name="join",
+    )(place, own, got, far)
+
+
+def middle_kernel(place, xs, xo, w0, w1, w2, w3, d0, d1, ts, to, gm_ref, w_all, d_all, pick):
+    rows, cols = w0.shape
+    ff = d0.shape[0] // 2
+    count = xs.shape[0] // 2
+    width = ts.shape[1]
+    q, j = place[0], place[1]
+    hidden = cols // 2
+    for k, w in enumerate((w0, w1, w2, w3)):
+        w_all[pl.ds(pl.multiple_of((q ^ k) * rows, rows), rows), :] = w[...]
+    r = q % 2
+    for e in range(2):
+        d_all[pl.ds(pl.multiple_of((2 * e + r) * ff, ff), ff), :] = d0[pl.ds(e * ff, ff), :]
+        d_all[pl.ds(pl.multiple_of((2 * e + 1 - r) * ff, ff), ff), :] = d1[pl.ds(e * ff, ff), :]
+    lane = lax.broadcasted_iota(jnp.int32, (LANES, cols), 0)
+    col = lax.broadcasted_iota(jnp.int32, (LANES, cols), 1)
+    n = LANES // 8
+    expert = 2 * j + jnp.where(col % hidden >= hidden // 2, 1, 0)
+    first = jnp.where(col < hidden, expert, expert + 2 * n)
+    second = jnp.where(col < hidden, expert + n, -1)
+    hit = jnp.where(lane == first, 1.0, 0.0) + jnp.where(lane == second, 1.0, 0.0)
+    pick[...] = hit.astype(jnp.bfloat16)
+
+    for b in range(4):
+        x_ref, t_ref = (xs, ts) if b < 2 else (xo, to)
+        at = pl.ds((b % 2) * count, count)
+        gu = jnp.dot(x_ref[at, :width], w_all[...], preferred_element_type=jnp.float32)
+        dh = lax.dot_general(
+            x_ref[at, width : 2 * width], d_all[...], NT, preferred_element_type=jnp.float32
+        )
+        wm = jnp.dot(x_ref[at, 2 * width :], pick[...], preferred_element_type=jnp.float32)
+        w, on = wm[:, :hidden], wm[:, hidden:]
+        gate, up = gu[:, :hidden], gu[:, hidden:]
+        sg = 0.5 * jnp.tanh(0.5 * gate) + 0.5
+        dhs = dh * on * sg
+        gg = dhs * up * (1.0 + gate * (1.0 - sg))
+        gup = dhs * gate
+        gm_ref[pl.ds(b * count, count), :hidden] = gg.astype(jnp.bfloat16)
+        gm_ref[pl.ds(b * count, count), hidden:] = gup.astype(jnp.bfloat16)
+        gw = jnp.concatenate([(gg * w).astype(jnp.bfloat16), (gup * w).astype(jnp.bfloat16)], 1)
+        t_ref[at, :] = lax.dot_general(
+            gw, w_all[...], NT, preferred_element_type=jnp.float32
+        ).astype(jnp.bfloat16)
+
+
+def middle(place, xs, ws, ds):
+    n, wide = xs[0].shape
+    rows, cols = ws[0].shape
+    ffr, width = ds[0].shape
+    vmem = pl.BlockSpec(memory_space=pltpu.VMEM)
+    return pl.pallas_call(
+        middle_kernel,
+        in_specs=[pl.BlockSpec(memory_space=pltpu.SMEM)] + [vmem] * 8,
+        out_specs=[vmem] * 3,
+        scratch_shapes=[
+            pltpu.VMEM((4 * rows, cols), jnp.bfloat16),
+            pltpu.VMEM((2 * ffr, width), jnp.bfloat16),
+            pltpu.VMEM((LANES, cols), jnp.bfloat16),
+        ],
+        out_shape=[
+            jax.ShapeDtypeStruct((n, width), jnp.bfloat16),
+            jax.ShapeDtypeStruct((n, width), jnp.bfloat16),
+            jax.ShapeDtypeStruct((2 * n, cols), jnp.bfloat16),
+        ],
+        compiler_params=pltpu.CompilerParams(vmem_limit_bytes=VMEM),
+        cost_estimate=pl.CostEstimate(
+            flops=HIDE, bytes_accessed=12 << 20, transcendentals=n * cols
+        ),
+        name="middle",
+    )(place, *xs, *ws, *ds)
+
+
+def outer_kernel(scale, half, count, place, *refs):
+    xs, gs, outs = refs[: 2 * half], refs[2 * half : 3 * half], refs[3 * half :]
+    acc = None
+    for k in range(half):
+        x = jnp.concatenate([x[...] for x in xs[2 * k : 2 * k + 2]], 0)
+        part = lax.dot_general(x, gs[k][...], TN, preferred_element_type=jnp.float32)
+        acc = part if acc is None else acc + part
+    value = (acc * scale).astype(jnp.bfloat16)
+    for k in range(count):
+
+        @pl.when(pl.program_id(0) == k)
+        def _():
+            outs[k][...] = value
+
+
+def outer(place, xs, gs, scale, rows, top, count):
+    cols = gs[0].shape[1]
+    return pl.pallas_call(
+        functools.partial(outer_kernel, scale, len(gs), count),
+        grid_spec=pltpu.PrefetchScalarGridSpec(
+            num_scalar_prefetch=1,
+            grid=(count,),
+            in_specs=[pl.BlockSpec((x.shape[0], rows), lambda i, s: (0, s[0] ^ (top - i))) for x in xs]
+            + [pl.BlockSpec(g.shape, lambda i, s: (0, 0)) for g in gs],
+            out_specs=[pl.BlockSpec((rows, cols), lambda i, s: (0, 0))] * count,
+        ),
+        out_shape=[jax.ShapeDtypeStruct((rows, cols), jnp.bfloat16)] * count,
+        compiler_params=pltpu.CompilerParams(
+            vmem_limit_bytes=VMEM, dimension_semantics=("arbitrary",)
+        ),
+        cost_estimate=pl.CostEstimate(flops=HIDE, bytes_accessed=12 << 20, transcendentals=0),
+        name="outer",
+    )(place, *xs, *gs)
+
+
+def by_tokens(tokens, cotangent, expert_ids, route_weights, weight_in, weight_down):
+    count, width = tokens.shape
+    n_dp = lax.axis_size("dp")
+    peers = lax.axis_size("expert")
+    half = n_dp // 2
+    rows, _, cols = weight_in.shape
+    ff_rows = weight_down.shape[0]
+    grad_scale = float(count * expert_ids.shape[1] * n_dp // weight_in.shape[1]) ** (-0.5)
+    q = lax.axis_index("dp")
+    place = jnp.stack([q, lax.axis_index("expert")]).astype(jnp.int32)
+    across = [(i, (i + half) % n_dp) for i in range(n_dp)]
+    beside = [(i, i ^ 1) for i in range(n_dp)]
+    cores = [(i, i ^ 1) for i in range(peers)]
+    hops = [[(i, i ^ (2 * m)) for i in range(peers)] for m in (1, 2, 3)]
+
+    payload = payload_of(tokens, cotangent, expert_ids, route_weights)
+    far_payload = lax.ppermute(payload, "dp", across)
+
+    def spread(x):
+        return [lax.ppermute(x, "expert", hop) for hop in hops]
+
+    def plus(a, b):
+        return (a.astype(jnp.float32) + b.astype(jnp.float32)).astype(jnp.bfloat16)
+
+    after = lax.optimization_barrier
+
+    near = [payload] + spread(payload)
+    weight_in, weight_down, payload = after((weight_in, weight_down, payload))
+    kept, given = halves(place, weight_in.swapaxes(0, 1))
+    w1 = lax.ppermute(kept, "dp", beside)
+    given, weight_down, w1, far_payload, *near = after((given, weight_down, w1, far_payload, *near))
+    near_own = jnp.concatenate(near, 0)
+    far = [far_payload] + spread(far_payload)
+    w2 = lax.ppermute(given, "dp", across)
+    near_sib = lax.ppermute(near_own, "expert", cores)
+    near_sib, weight_down = after((near_sib, weight_down))
+    down = weight_down.swapaxes(0, 1).reshape(2 * ff_rows, width)
+    down1 = lax.ppermute(down, "dp", beside)
+    w2, down1, *far = after((w2, down1, *far))
+    far_own = jnp.concatenate(far, 0)
+    w3 = lax.ppermute(w2, "dp", beside)
+    far_sib = lax.ppermute(far_own, "expert", cores)
+    ws, ds = (kept, w1, w2, w3), (down, down1)
+
+    def back_sums(own, got):
+        return [plus(own[k * count : (k + 1) * count], got[k * count : (k + 1) * count]) for k in range(4)]
+
+    def back_hops(sums):
+        return [sums[0]] + [lax.ppermute(t, "expert", hop) for t, hop in zip(sums[1:], hops)]
+
+    near_ts, near_to, near_mid = middle(place, (near_sib, near_own), ws, ds)
+    near_got = lax.ppermute(near_ts, "expert", cores)
+    far_sib, near_mid = after((far_sib, near_mid))
+    far_ts, far_to, far_mid = middle(place, (far_sib, far_own), ws, ds)
+    far_got = lax.ppermute(far_ts, "expert", cores)
+    tiles, mids = (far_sib, far_own, near_sib, near_own), (far_mid, near_mid)
+    (g3,) = outer(place, tiles, mids, grad_scale, rows, 3, 1)
+    got3 = lax.ppermute(g3, "dp", beside)
+    far_sums, near_sums = back_sums(far_to, far_got), back_sums(near_to, near_got)
+    far_mid, *sums = after((far_mid, *far_sums, *near_sums))
+    far_sums, near_sums = sums[:4], sums[4:]
+    far_back = back_hops(far_sums)
+    g2, g1, g0 = outer(place, tiles, (far_mid, near_mid), grad_scale, rows, 2, 3)
+    got1 = lax.ppermute(g1, "dp", beside)
+    got3, g2, *near_sums = after((got3, g2, *near_sums))
+    relay = plus(g2, got3)
+    away_half = lax.ppermute(relay, "dp", across)
+    near_back = back_hops(near_sums)
+    away = sum(t.astype(jnp.float32) for t in far_back).astype(jnp.bfloat16)
+    home = lax.ppermute(away, "dp", across)
+    near_total = sum(t.astype(jnp.float32) for t in near_back)
+    token_grad = (near_total + home.astype(jnp.float32)).astype(jnp.bfloat16)
+    grad_in = join(place, g0, got1, away_half).swapaxes(0, 1)
+    return token_grad, grad_in
+
+
+def on_device(tokens, cotangent, expert_ids, route_weights, weight_in, weight_down):
+    peers, n_dp = lax.axis_size("expert"), lax.axis_size("dp")
+    experts = weight_in.shape[1] * peers
+    capacity = 5 * tokens.shape[0] * expert_ids.shape[1] // (4 * experts)
+    dense = weight_in.shape[1] * capacity >= tokens.shape[0]
+    if dense and weight_in.shape[1] == 2 and n_dp == 4 and peers == 8 and experts == 16:
+        form = by_tokens
+    else:
+        form = by_routes
+    return form(tokens, cotangent, expert_ids, route_weights, weight_in, weight_down)
+
+
 def solution(mesh):
     placed = (
         P(("dp", "expert"), None),

time: 194 us -> 145 us (0.75)
  the two profiles are of different devices: /device:TPU:0 before, /device:TPU:25 now
where the time goes in v1:
time: 145 us
  waiting for transfers between devices  93.5 us (64%)
  Pallas kernels  24.7 us (17%)
  starting transfers between devices  16 us (11%)
  local copies, waits for them, and re-layouts  6.93 us (5%)
  other arithmetic  2.65 us (2%)
    ppermute x1, waiting for transfers between devices, by_tokens(): w2 = lax.ppermute(given, 'dp', across)  17.9 us
    ppermute x1, waiting for transfers between devices, by_tokens(): w1 = lax.ppermute(kept, 'dp', beside)  14.1 us
    ppermute x1, waiting for transfers between devices, by_tokens(): got1 = lax.ppermute(g1, 'dp', beside)  14 us
    pallas_call x2, Pallas kernels, middle(): pl.pallas_call(middle_kernel, in_specs=[pl.BlockSpec(memory_space=pltpu.S...  11.6 us
    ppermute x6, waiting for transfers between devices, spread(): return [lax.ppermute(x, 'expert', hop) for hop in hops]  10.9 us
    ppermute x1, waiting for transfers between devices, by_tokens(): away_half = lax.ppermute(relay, 'dp', across)  9.29 us
    ppermute x1, waiting for transfers between devices, by_tokens(): w3 = lax.ppermute(w2, 'dp', beside)  9.23 us
    ppermute x6, waiting for transfers between devices, back_hops(): lax.ppermute(t, 'expert', hop)  6.99 us
  transfers between devices with their start and end apart: 25, of which 14 were waited for; matrix products, arithmetic and copies ran while one was open for 5% of the time, Pallas kernels for 12%

profile of v1, /device:TPU:25, one launch (start us, length us, event | category | flops | bytes accessed | tf_op | source)
XLA Modules:
  0.0 144.7 jit_solution(15138301285945105182)
XLA Ops:
  0.6 2.0 %payload.1 = bf16[128,2176]{1,0:T(8,128)(2,1)} custom-call(bf16[128,1024]{1,0:T(8,128)(2,1)} %tokens.1, bf16[128,1024]{1,0:T(8,128)(2,1)} %cotangent.1, s32[8,128]{1,0:T(8,128)} %bitcast.16, f32[8,128]{1,0:T(8,128)} %bitcast.17), custom_call_target="tpu_custom_call" | custom-call | flops 1048576 | bytes 2097152 | tf_op jit(solution)/shard_map/payload/pallas_call | solution.py:105
  2.6 2.2 %collective-permute-start.4 = (bf16[128,2176]{1,0:T(8,128)(2,1)}, bf16[128,2176]{1,0:T(8,128)(2,1)S(1)}, u32[]{:S(2)}, u32[]{:S(2)}) collective-permute-start(bf16[128,2176]{1,0:T(8,128)(2,1)} %payload.1), channel_id=1, source_target_pairs={{0,6},{1,7},{2,4},{3,5},{4,2},{5,3},{6,0},{7,1},{8,14},{9,15},{10,... | collective-permute-start | bytes 1671176 | tf_op jit(solution)/shard_map/ppermute | solution.py:297
  4.8 0.2 collective-permute-start.3
  5.0 0.3 collective-permute-start.2
  5.3 2.1 %copy.12 = bf16[256,2,768]{2,0,1:T(8,128)(2,1)} copy(bf16[256,2,768]{2,1,0:T(2,128)(2,1)} %param.10) | data formatting | bytes 1572864 | tf_op jit(solution)/shard_map/optimization_barrier | solution.py:305
  7.4 0.7 pad_add_fusion.place
  8.0 2.3 %halves.1 = (bf16[256,768]{1,0:T(8,128)(2,1)}, bf16[256,768]{1,0:T(8,128)(2,1)}) custom-call(s32[2]{0:T(128)} %pad_add_fusion.place, bf16[2,256,768]{2,1,0:T(8,128)(2,1)} %bitcast.14), custom_call_target="tpu_custom_call" | custom-call | flops 17179869184 | bytes 2097152 | tf_op jit(solution)/shard_map/halves/pallas_call | solution.py:132
  10.4 0.1 collective-permute-start
  10.5 14.1 %collective-permute-done.w1 = bf16[256,768]{1,0:T(8,128)(2,1)S(1)} collective-permute-done((bf16[256,768]{1,0:T(8,128)(2,1)}, bf16[256,768]{1,0:T(8,128)(2,1)S(1)}, u32[]{:S(2)}, u32[]{:S(2)}) %collective-permute-start) | collective-permute-done | bytes 393248 | tf_op jit(solution)/shard_map/ppermute | solution.py:307
  24.6 5.6 %collective-permute-done.3 = bf16[128,2176]{1,0:T(8,128)(2,1)S(1)} collective-permute-done((bf16[128,2176]{1,0:T(8,128)(2,1)}, bf16[128,2176]{1,0:T(8,128)(2,1)S(1)}, u32[]{:S(2)}, u32[]{:S(2)}) %collective-permute-start.3) | collective-permute-done | bytes 557088 | tf_op jit(solution)/shard_map/ppermute | solution.py:297
  30.2 2.6 %collective-permute-done.1 = bf16[128,2176]{1,0:T(8,128)(2,1)S(1)} collective-permute-done((bf16[128,2176]{1,0:T(8,128)(2,1)}, bf16[128,2176]{1,0:T(8,128)(2,1)S(1)}, u32[]{:S(2)}, u32[]{:S(2)}) %collective-permute-start.1) | collective-permute-done | bytes 557088 | tf_op jit(solution)/shard_map/ppermute | solution.py:294
  33.0 1.3 collective-permute-start.6
  34.3 2.2 %collective-permute-start.10 = (bf16[128,2176]{1,0:T(8,128)(2,1)S(1)}, bf16[128,2176]{1,0:T(8,128)(2,1)S(1)}, u32[]{:S(2)}, u32[]{:S(2)}) collective-permute-start(bf16[128,2176]{1,0:T(8,128)(2,1)S(1)} %collective-permute-done.1), channel_id=1, source_target_pairs={{0,6},{1,7},{2,4},{3,5},{4,2},{5,3},{6,0},{7,1},{8,14},{9,15},{10,... | collective-permute-start | bytes 1671176 | tf_op jit(solution)/shard_map/ppermute | solution.py:297
  36.5 0.2 collective-permute-start.9
  36.7 0.3 collective-permute-start.8
  37.0 1.3 collective-permute-done.6.xs.refs_2_
  38.4 0.2 collective-permute-start.7
  38.6 17.9 %collective-permute-done.5.w2 = bf16[256,768]{1,0:T(8,128)(2,1)S(1)} collective-permute-done((bf16[256,768]{1,0:T(8,128)(2,1)S(1)}, bf16[256,768]{1,0:T(8,128)(2,1)S(1)}, u32[]{:S(2)}, u32[]{:S(2)}) %collective-permute-start.5) | collective-permute-done | bytes 393248 | tf_op jit(solution)/shard_map/ppermute | solution.py:311
  56.5 5.3 %collective-permute-done.9 = bf16[128,2176]{1,0:T(8,128)(2,1)S(1)} collective-permute-done((bf16[128,2176]{1,0:T(8,128)(2,1)S(1)}, bf16[128,2176]{1,0:T(8,128)(2,1)S(1)}, u32[]{:S(2)}, u32[]{:S(2)}) %collective-permute-start.9) | collective-permute-done | bytes 557088 | tf_op jit(solution)/shard_map/ppermute | solution.py:297
  62.0 0.6 collective-permute-start.11
  62.6 9.2 %collective-permute-done.12.w3 = bf16[256,768]{1,0:T(8,128)(2,1)S(1)} collective-permute-done((bf16[256,768]{1,0:T(8,128)(2,1)S(1)}, bf16[256,768]{1,0:T(8,128)(2,1)S(1)}, u32[]{:S(2)}, u32[]{:S(2)}) %collective-permute-start.12) | collective-permute-done | bytes 393248 | tf_op jit(solution)/shard_map/ppermute | solution.py:318
  71.9 5.8 %middle.2 = (bf16[512,1024]{1,0:T(8,128)(2,1)S(1)}, bf16[512,1024]{1,0:T(8,128)(2,1)S(1)}, bf16[1024,768]{1,0:T(8,128)(2,1)S(1)}) custom-call(s32[2]{0:T(128)S(1)} %copy-done.1, bf16[512,2176]{1,0:T(8,128)(2,1)S(1)} %collective-permute-done.6.xs.refs_2_, bf16[512,2176]{1,0:T(8,128)(2,1)S(1)} %constant_dynamic-update-slice_fusion.xo.refs_3_, ...), custom_call_target="tpu_custom_call" | custom-call | flops 17179869184 | bytes 12582912 | tf_op jit(solution)/shard_map/middle/pallas_call | solution.py:221
  77.7 1.5 %collective-permute-start.15 = (bf16[512,1024]{1,0:T(8,128)(2,1)S(1)}, bf16[512,1024]{1,0:T(8,128)(2,1)S(1)}, u32[]{:S(2)}, u32[]{:S(2)}) collective-permute-start(bf16[512,1024]{1,0:T(8,128)(2,1)S(1)} %get-tuple-element.75), channel_id=1, source_target_pairs={{0,1},{1,0},{2,3},{3,2},{4,5},{5,4},{6,7},{7,6},{8,9},{9,8},{10,11... | collective-permute-start | bytes 3145736 | tf_op jit(solution)/shard_map/ppermute | solution.py:329
  79.1 2.3 %collective-permute-done.15 = bf16[512,1024]{1,0:T(8,128)(2,1)S(1)} collective-permute-done((bf16[512,1024]{1,0:T(8,128)(2,1)S(1)}, bf16[512,1024]{1,0:T(8,128)(2,1)S(1)}, u32[]{:S(2)}, u32[]{:S(2)}) %collective-permute-start.15) | collective-permute-done | bytes 1048608 | tf_op jit(solution)/shard_map/ppermute | solution.py:329
  81.4 0.4 add_convert_fusion.3
  81.9 5.8 %middle.3 = (bf16[512,1024]{1,0:T(8,128)(2,1)S(1)}, bf16[512,1024]{1,0:T(8,128)(2,1)S(1)}, bf16[1024,768]{1,0:T(8,128)(2,1)S(1)}) custom-call(s32[2]{0:T(128)S(1)} %copy-done.1, bf16[512,2176]{1,0:T(8,128)(2,1)S(1)} %collective-permute-done.11.xs.refs_0_, bf16[512,2176]{1,0:T(8,128)(2,1)S(1)} %constant_dynamic-update-slice_fusion.4.xo.refs_1_, ...), custom_call_target="tpu_custom_call" | custom-call | flops 17179869184 | bytes 12582912 | tf_op jit(solution)/shard_map/middle/pallas_call | solution.py:221
  87.7 0.4 collective-permute-start.14
  88.2 1.9 %outer.2 = bf16[256,768]{1,0:T(8,128)(2,1)S(1)} custom-call(s32[2]{0:T(128)S(1)} %copy-done.1, bf16[512,2176]{1,0:T(8,128)(2,1)S(1)} %collective-permute-done.11.xs.refs_0_, bf16[512,2176]{1,0:T(8,128)(2,1)S(1)} %constant_dynamic-update-slice_fusion.4.xo.refs_1_, bf16[512,2176]{1,0:T(8,128)(2,1)S(1)} %collective-permute-done.6.xs.refs_2_, ...), custom_call_target="tpu_custom_call" | custom-call | flops 17179869184 | bytes 12582912 | tf_op jit(solution)/shard_map/outer/pallas_call | solution.py:260
  90.1 0.3 collective-permute-done.14
  90.4 0.4 add_convert_fusion.7
  90.9 4.4 %outer.3 = (bf16[256,768]{1,0:T(8,128)(2,1)S(1)}, bf16[256,768]{1,0:T(8,128)(2,1)S(1)}, bf16[256,768]{1,0:T(8,128)(2,1)S(1)}) custom-call(s32[2]{0:T(128)S(1)} %copy-done.1, bf16[512,2176]{1,0:T(8,128)(2,1)S(1)} %collective-permute-done.11.xs.refs_0_, bf16[512,2176]{1,0:T(8,128)(2,1)S(1)} %constant_dynamic-update-slice_fusion.4.xo.refs_1_, ...), custom_call_target="tpu_custom_call" | custom-call | flops 17179869184 | bytes 12582912 | tf_op jit(solution)/shard_map/outer/pallas_call | solution.py:260
  95.3 0.7 copy-done
  96.0 4.7 %collective-permute-done.13 = bf16[256,768]{1,0:T(8,128)(2,1)S(1)} collective-permute-done((bf16[256,768]{1,0:T(8,128)(2,1)S(1)}, bf16[256,768]{1,0:T(8,128)(2,1)S(1)}, u32[]{:S(2)}, u32[]{:S(2)}) %collective-permute-start.13) | collective-permute-done | bytes 393248 | tf_op jit(solution)/shard_map/ppermute | solution.py:335
  100.7 1.2 collective-permute-start.19
  101.9 1.4 collective-permute-start.21
  103.4 0.1 add_convert_fusion
  103.5 1.3 collective-permute-start.16
  104.8 2.8 %collective-permute-done.19 = bf16[128,1024]{1,0:T(8,128)(2,1)S(1)} collective-permute-done((bf16[128,1024]{1,0:T(8,128)(2,1)S(1)}, bf16[128,1024]{1,0:T(8,128)(2,1)S(1)}, u32[]{:S(2)}, u32[]{:S(2)}) %collective-permute-start.19) | collective-permute-done | bytes 262176 | tf_op jit(solution)/shard_map/ppermute | solution.py:326
  107.6 1.2 collective-permute-start.17
  108.8 1.2 collective-permute-start.18
  110.0 4.2 %collective-permute-done.21 = bf16[128,1024]{1,0:T(8,128)(2,1)S(1)} collective-permute-done((bf16[128,1024]{1,0:T(8,128)(2,1)S(1)}, bf16[128,1024]{1,0:T(8,128)(2,1)S(1)}, u32[]{:S(2)}, u32[]{:S(2)}) %collective-permute-start.21) | collective-permute-done | bytes 262176 | tf_op jit(solution)/shard_map/ppermute | solution.py:326
  114.2 0.2 add_convert_fusion.2
  114.4 9.3 %collective-permute-done.24.far = bf16[256,768]{1,0:T(8,128)(2,1)S(1)} collective-permute-done((bf16[256,768]{1,0:T(8,128)(2,1)S(1)}, bf16[256,768]{1,0:T(8,128)(2,1)S(1)}, u32[]{:S(2)}, u32[]{:S(2)}) %collective-permute-start.24) | collective-permute-done | bytes 393248 | tf_op jit(solution)/shard_map/ppermute | solution.py:344
  123.7 14.0 %collective-permute-done.23.got = bf16[256,768]{1,0:T(8,128)(2,1)S(1)} collective-permute-done((bf16[256,768]{1,0:T(8,128)(2,1)S(1)}, bf16[256,768]{1,0:T(8,128)(2,1)S(1)}, u32[]{:S(2)}, u32[]{:S(2)}) %collective-permute-start.23) | collective-permute-done | bytes 393248 | tf_op jit(solution)/shard_map/ppermute | solution.py:341
  137.7 0.8 copy-done.6
  138.4 2.5 %join.1 = bf16[2,256,768]{2,1,0:T(8,128)(2,1)} custom-call(s32[2]{0:T(128)} %pad_add_fusion.place, bf16[256,768]{1,0:T(8,128)(2,1)} %copy-done, bf16[256,768]{1,0:T(8,128)(2,1)} %copy-done.6, bf16[256,768]{1,0:T(8,128)(2,1)} %copy-done.5), custom_call_target="tpu_custom_call" | custom-call | flops 1048576 | bytes 2097152 | tf_op jit(solution)/shard_map/join/pallas_call | solution.py:162
  140.9 2.8 %copy.10 = bf16[256,2,768]{2,1,0:T(2,128)(2,1)} copy(bf16[256,2,768]{2,0,1:T(8,128)(2,1)} %bitcast.13) | data formatting | bytes 1572864
  143.8 0.9 add_convert_fusion.1
  (42 shorter events, 0.8 us)
Async XLA Ops:
  2.6 22.0 %collective-permute-start.4 = (bf16[128,2176]{1,0:T(8,128)(2,1)}, bf16[128,2176]{1,0:T(8,128)(2,1)S(1)}, u32[]{:S(2)}, u32[]{:S(2)}) collective-permute-start(bf16[128,2176]{1,0:T(8,128)(2,1)} %payload.1), channel_id=1, source_target_pairs={{0,6},{1,7},{2,4},{3,5},{4,2},{5,3},{6,0},{7,1},{8,14},{9,15},{10,... | collective-permute-start | bytes 1671176 | tf_op jit(solution)/shard_map/ppermute | solution.py:297
  4.8 25.4 %collective-permute-start.3 = (bf16[128,2176]{1,0:T(8,128)(2,1)}, bf16[128,2176]{1,0:T(8,128)(2,1)S(1)}, u32[]{:S(2)}, u32[]{:S(2)}) collective-permute-start(bf16[128,2176]{1,0:T(8,128)(2,1)} %payload.1), channel_id=1, source_target_pairs={{0,4},{1,5},{2,6},{3,7},{4,0},{5,1},{6,2},{7,3},{8,12},{9,13},{10,... | collective-permute-start | bytes 1671176 | tf_op jit(solution)/shard_map/ppermute | solution.py:297
  5.0 25.2 %collective-permute-start.2 = (bf16[128,2176]{1,0:T(8,128)(2,1)}, bf16[128,2176]{1,0:T(8,128)(2,1)S(1)}, u32[]{:S(2)}, u32[]{:S(2)}) collective-permute-start(bf16[128,2176]{1,0:T(8,128)(2,1)} %payload.1), channel_id=1, source_target_pairs={{0,2},{1,3},{2,0},{3,1},{4,6},{5,7},{6,4},{7,5},{8,10},{9,11},{10,... | collective-permute-start | bytes 1671176 | tf_op jit(solution)/shard_map/ppermute | solution.py:297
  5.2 27.5 %collective-permute-start.1 = (bf16[128,2176]{1,0:T(8,128)(2,1)}, bf16[128,2176]{1,0:T(8,128)(2,1)S(1)}, u32[]{:S(2)}, u32[]{:S(2)}) collective-permute-start(bf16[128,2176]{1,0:T(8,128)(2,1)} %payload.1), channel_id=1, source_target_pairs={{0,16},{8,24},{16,0},{24,8},{1,17},{9,25},{17,1},{25,9},{2,18},{10... | collective-permute-start | bytes 1671176 | tf_op jit(solution)/shard_map/ppermute | solution.py:294
  8.0 24.7 %copy-start.3 = (bf16[128,2176]{1,0:T(8,128)(2,1)S(1)}, bf16[128,2176]{1,0:T(8,128)(2,1)}, u32[]{:S(2)}) copy-start(bf16[128,2176]{1,0:T(8,128)(2,1)} %payload.1) | copy-start | bytes 1671172
  10.4 14.2 %collective-permute-start = (bf16[256,768]{1,0:T(8,128)(2,1)}, bf16[256,768]{1,0:T(8,128)(2,1)S(1)}, u32[]{:S(2)}, u32[]{:S(2)}) collective-permute-start(bf16[256,768]{1,0:T(8,128)(2,1)} %get-tuple-element.51.w0), channel_id=1, source_target_pairs={{0,8},{8,0},{16,24},{24,16},{1,9},{9,1},{17,25},{25,17},{2,10},{10... | collective-permute-start | bytes 1179656 | tf_op jit(solution)/shard_map/ppermute | solution.py:307
  32.8 4.2 %copy-start.7 = (bf16[256,768]{1,0:T(8,128)(2,1)S(1)}, bf16[256,768]{1,0:T(8,128)(2,1)}, u32[]{:S(2)}) copy-start(bf16[256,768]{1,0:T(8,128)(2,1)} %get-tuple-element.52) | copy-start | bytes 1179652
  32.8 5.5 %copy-start.4 = (bf16[96,2,1024]{2,1,0:T(2,128)(2,1)S(1)}, bf16[96,2,1024]{2,1,0:T(2,128)(2,1)}, u32[]{:S(2)}) copy-start(bf16[96,2,1024]{2,1,0:T(2,128)(2,1)} %param.11) | copy-start | bytes 1179652
  33.0 5.3 %collective-permute-start.6 = (bf16[512,2176]{1,0:T(8,128)(2,1)S(1)}, bf16[512,2176]{1,0:T(8,128)(2,1)S(1)}, u32[]{:S(2)}, u32[]{:S(2)}) collective-permute-start(bf16[512,2176]{1,0:T(8,128)(2,1)S(1)} %constant_dynamic-update-slice_fusion.xo.refs_3_), channel_id=1, source_target_pairs={{0,1},{1,0},{2,3},{3,2},{4,5},{5,4},{6,7},{7,6},{8,9},{9,8},{10,11... | collective-permute-start | bytes 6684680 | tf_op jit(solution)/shard_map/ppermute | solution.py:312
  34.3 22.2 %collective-permute-start.10 = (bf16[128,2176]{1,0:T(8,128)(2,1)S(1)}, bf16[128,2176]{1,0:T(8,128)(2,1)S(1)}, u32[]{:S(2)}, u32[]{:S(2)}) collective-permute-start(bf16[128,2176]{1,0:T(8,128)(2,1)S(1)} %collective-permute-done.1), channel_id=1, source_target_pairs={{0,6},{1,7},{2,4},{3,5},{4,2},{5,3},{6,0},{7,1},{8,14},{9,15},{10,... | collective-permute-start | bytes 1671176 | tf_op jit(solution)/shard_map/ppermute | solution.py:297
  36.5 25.2 %collective-permute-start.9 = (bf16[128,2176]{1,0:T(8,128)(2,1)S(1)}, bf16[128,2176]{1,0:T(8,128)(2,1)S(1)}, u32[]{:S(2)}, u32[]{:S(2)}) collective-permute-start(bf16[128,2176]{1,0:T(8,128)(2,1)S(1)} %collective-permute-done.1), channel_id=1, source_target_pairs={{0,4},{1,5},{2,6},{3,7},{4,0},{5,1},{6,2},{7,3},{8,12},{9,13},{10,... | collective-permute-start | bytes 1671176 | tf_op jit(solution)/shard_map/ppermute | solution.py:297
  36.7 25.0 %collective-permute-start.8 = (bf16[128,2176]{1,0:T(8,128)(2,1)S(1)}, bf16[128,2176]{1,0:T(8,128)(2,1)S(1)}, u32[]{:S(2)}, u32[]{:S(2)}) collective-permute-start(bf16[128,2176]{1,0:T(8,128)(2,1)S(1)} %collective-permute-done.1), channel_id=1, source_target_pairs={{0,2},{1,3},{2,0},{3,1},{4,6},{5,7},{6,4},{7,5},{8,10},{9,11},{10,... | collective-permute-start | bytes 1671176 | tf_op jit(solution)/shard_map/ppermute | solution.py:297
  37.0 19.5 %collective-permute-start.5 = (bf16[256,768]{1,0:T(8,128)(2,1)S(1)}, bf16[256,768]{1,0:T(8,128)(2,1)S(1)}, u32[]{:S(2)}, u32[]{:S(2)}) collective-permute-start(bf16[256,768]{1,0:T(8,128)(2,1)S(1)} %copy-done.7), channel_id=1, source_target_pairs={{0,16},{8,24},{16,0},{24,8},{1,17},{9,25},{17,1},{25,9},{2,18},{10... | collective-permute-start | bytes 1179656 | tf_op jit(solution)/shard_map/ppermute | solution.py:311
  38.4 33.5 %copy-start.1 = (s32[2]{0:T(128)S(1)}, s32[2]{0:T(128)}, u32[]{:S(2)}) copy-start(s32[2]{0:T(128)} %pad_add_fusion.place) | copy-start | bytes 28
  38.4 33.5 %copy-start.2 = (bf16[256,768]{1,0:T(8,128)(2,1)S(1)}, bf16[256,768]{1,0:T(8,128)(2,1)}, u32[]{:S(2)}) copy-start(bf16[256,768]{1,0:T(8,128)(2,1)} %get-tuple-element.51.w0) | copy-start | bytes 1179652
  38.4 23.3 %collective-permute-start.7 = (bf16[192,1024]{1,0:T(8,128)(2,1)S(1)}, bf16[192,1024]{1,0:T(8,128)(2,1)S(1)}, u32[]{:S(2)}, u32[]{:S(2)}) collective-permute-start(bf16[192,1024]{1,0:T(8,128)(2,1)S(1)} %bitcast.10), channel_id=1, source_target_pairs={{0,8},{8,0},{16,24},{24,16},{1,9},{9,1},{17,25},{25,17},{2,10},{10... | collective-permute-start | bytes 1179656 | tf_op jit(solution)/shard_map/ppermute | solution.py:315
  61.8 10.1 %collective-permute-start.12 = (bf16[256,768]{1,0:T(8,128)(2,1)S(1)}, bf16[256,768]{1,0:T(8,128)(2,1)S(1)}, u32[]{:S(2)}, u32[]{:S(2)}) collective-permute-start(bf16[256,768]{1,0:T(8,128)(2,1)S(1)} %collective-permute-done.5.w2), channel_id=1, source_target_pairs={{0,8},{8,0},{16,24},{24,16},{1,9},{9,1},{17,25},{25,17},{2,10},{10... | collective-permute-start | bytes 1179656 | tf_op jit(solution)/shard_map/ppermute | solution.py:318
  62.0 19.8 %collective-permute-start.11 = (bf16[512,2176]{1,0:T(8,128)(2,1)S(1)}, bf16[512,2176]{1,0:T(8,128)(2,1)S(1)}, u32[]{:S(2)}, u32[]{:S(2)}) collective-permute-start(bf16[512,2176]{1,0:T(8,128)(2,1)S(1)} %constant_dynamic-update-slice_fusion.4.xo.refs_1_), channel_id=1, source_target_pairs={{0,1},{1,0},{2,3},{3,2},{4,5},{5,4},{6,7},{7,6},{8,9},{9,8},{10,11... | collective-permute-start | bytes 6684680 | tf_op jit(solution)/shard_map/ppermute | solution.py:319
  77.7 3.8 %collective-permute-start.15 = (bf16[512,1024]{1,0:T(8,128)(2,1)S(1)}, bf16[512,1024]{1,0:T(8,128)(2,1)S(1)}, u32[]{:S(2)}, u32[]{:S(2)}) collective-permute-start(bf16[512,1024]{1,0:T(8,128)(2,1)S(1)} %get-tuple-element.75), channel_id=1, source_target_pairs={{0,1},{1,0},{2,3},{3,2},{4,5},{5,4},{6,7},{7,6},{8,9},{9,8},{10,11... | collective-permute-start | bytes 3145736 | tf_op jit(solution)/shard_map/ppermute | solution.py:329
  87.7 2.7 %collective-permute-start.14 = (bf16[512,1024]{1,0:T(8,128)(2,1)S(1)}, bf16[512,1024]{1,0:T(8,128)(2,1)S(1)}, u32[]{:S(2)}, u32[]{:S(2)}) collective-permute-start(bf16[512,1024]{1,0:T(8,128)(2,1)S(1)} %get-tuple-element.73), channel_id=1, source_target_pairs={{0,1},{1,0},{2,3},{3,2},{4,5},{5,4},{6,7},{7,6},{8,9},{9,8},{10,11... | collective-permute-start | bytes 3145736 | tf_op jit(solution)/shard_map/ppermute | solution.py:332
  90.1 10.6 %collective-permute-start.13 = (bf16[256,768]{1,0:T(8,128)(2,1)S(1)}, bf16[256,768]{1,0:T(8,128)(2,1)S(1)}, u32[]{:S(2)}, u32[]{:S(2)}) collective-permute-start(bf16[256,768]{1,0:T(8,128)(2,1)S(1)} %outer.2), channel_id=1, source_target_pairs={{0,8},{8,0},{16,24},{24,16},{1,9},{9,1},{17,25},{25,17},{2,10},{10... | collective-permute-start | bytes 1179656 | tf_op jit(solution)/shard_map/ppermute | solution.py:335
  95.3 0.7 copy-start
  100.7 6.9 %collective-permute-start.19 = (bf16[128,1024]{1,0:T(8,128)(2,1)S(1)}, bf16[128,1024]{1,0:T(8,128)(2,1)S(1)}, u32[]{:S(2)}, u32[]{:S(2)}) collective-permute-start(bf16[128,1024]{1,0:T(8,128)(2,1)S(1)} %get-tuple-element.87), channel_id=1, source_target_pairs={{0,2},{1,3},{2,0},{3,1},{4,6},{5,7},{6,4},{7,5},{8,10},{9,11},{10,... | collective-permute-start | bytes 786440 | tf_op jit(solution)/shard_map/ppermute | solution.py:326
  101.9 6.9 %collective-permute-start.20 = (bf16[128,1024]{1,0:T(8,128)(2,1)S(1)}, bf16[128,1024]{1,0:T(8,128)(2,1)S(1)}, u32[]{:S(2)}, u32[]{:S(2)}) collective-permute-start(bf16[128,1024]{1,0:T(8,128)(2,1)S(1)} %get-tuple-element.88), channel_id=1, source_target_pairs={{0,4},{1,5},{2,6},{3,7},{4,0},{5,1},{6,2},{7,3},{8,12},{9,13},{10,... | collective-permute-start | bytes 786440 | tf_op jit(solution)/shard_map/ppermute | solution.py:326
  101.9 12.2 %collective-permute-start.21 = (bf16[128,1024]{1,0:T(8,128)(2,1)S(1)}, bf16[128,1024]{1,0:T(8,128)(2,1)S(1)}, u32[]{:S(2)}, u32[]{:S(2)}) collective-permute-start(bf16[128,1024]{1,0:T(8,128)(2,1)S(1)} %get-tuple-element.89), channel_id=1, source_target_pairs={{0,6},{1,7},{2,4},{3,5},{4,2},{5,3},{6,0},{7,1},{8,14},{9,15},{10,... | collective-permute-start | bytes 786440 | tf_op jit(solution)/shard_map/ppermute | solution.py:326
  103.5 20.2 %collective-permute-start.24 = (bf16[256,768]{1,0:T(8,128)(2,1)S(1)}, bf16[256,768]{1,0:T(8,128)(2,1)S(1)}, u32[]{:S(2)}, u32[]{:S(2)}) collective-permute-start(bf16[256,768]{1,0:T(8,128)(2,1)S(1)} %add_convert_fusion), channel_id=1, source_target_pairs={{0,16},{8,24},{16,0},{24,8},{1,17},{9,25},{17,1},{25,9},{2,18},{10... | collective-permute-start | bytes 1179656 | tf_op jit(solution)/shard_map/ppermute | solution.py:344
  103.5 40.2 %collective-permute-start.16 = (bf16[128,1024]{1,0:T(8,128)(2,1)S(1)}, bf16[128,1024]{1,0:T(8,128)(2,1)S(1)}, u32[]{:S(2)}, u32[]{:S(2)}) collective-permute-start(bf16[128,1024]{1,0:T(8,128)(2,1)S(1)} %get-tuple-element.83), channel_id=1, source_target_pairs={{0,2},{1,3},{2,0},{3,1},{4,6},{5,7},{6,4},{7,5},{8,10},{9,11},{10,... | collective-permute-start | bytes 786440 | tf_op jit(solution)/shard_map/ppermute | solution.py:326
  107.6 36.2 %collective-permute-start.17 = (bf16[128,1024]{1,0:T(8,128)(2,1)S(1)}, bf16[128,1024]{1,0:T(8,128)(2,1)S(1)}, u32[]{:S(2)}, u32[]{:S(2)}) collective-permute-start(bf16[128,1024]{1,0:T(8,128)(2,1)S(1)} %get-tuple-element.84), channel_id=1, source_target_pairs={{0,4},{1,5},{2,6},{3,7},{4,0},{5,1},{6,2},{7,3},{8,12},{9,13},{10,... | collective-permute-start | bytes 786440 | tf_op jit(solution)/shard_map/ppermute | solution.py:326
  108.8 35.0 %collective-permute-start.18 = (bf16[128,1024]{1,0:T(8,128)(2,1)S(1)}, bf16[128,1024]{1,0:T(8,128)(2,1)S(1)}, u32[]{:S(2)}, u32[]{:S(2)}) collective-permute-start(bf16[128,1024]{1,0:T(8,128)(2,1)S(1)} %get-tuple-element.85), channel_id=1, source_target_pairs={{0,6},{1,7},{2,4},{3,5},{4,2},{5,3},{6,0},{7,1},{8,14},{9,15},{10,... | collective-permute-start | bytes 786440 | tf_op jit(solution)/shard_map/ppermute | solution.py:326
  114.2 23.5 %collective-permute-start.23 = (bf16[256,768]{1,0:T(8,128)(2,1)S(1)}, bf16[256,768]{1,0:T(8,128)(2,1)S(1)}, u32[]{:S(2)}, u32[]{:S(2)}) collective-permute-start(bf16[256,768]{1,0:T(8,128)(2,1)S(1)} %get-tuple-element.91), channel_id=1, source_target_pairs={{0,8},{8,0},{16,24},{24,16},{1,9},{9,1},{17,25},{25,17},{2,10},{10... | collective-permute-start | bytes 1179656 | tf_op jit(solution)/shard_map/ppermute | solution.py:341
  123.7 14.0 %copy-start.5 = (bf16[256,768]{1,0:T(8,128)(2,1)}, bf16[256,768]{1,0:T(8,128)(2,1)S(1)}, u32[]{:S(2)}) copy-start(bf16[256,768]{1,0:T(8,128)(2,1)S(1)} %collective-permute-done.24.far) | copy-start | bytes 1179652
  123.7 20.1 %collective-permute-start.22 = (bf16[128,1024]{1,0:T(8,128)(2,1)S(1)}, bf16[128,1024]{1,0:T(8,128)(2,1)S(1)}, u32[]{:S(2)}, u32[]{:S(2)}) collective-permute-start(bf16[128,1024]{1,0:T(8,128)(2,1)S(1)} %add_convert_fusion.2), channel_id=1, source_target_pairs={{0,16},{8,24},{16,0},{24,8},{1,17},{9,25},{17,1},{25,9},{2,18},{10... | collective-permute-start | bytes 786440 | tf_op jit(solution)/shard_map/ppermute | solution.py:347
  137.7 0.8 copy-start.6

commit v2 on v1

--- a/solution.py
+++ b/solution.py
@@ -79,7 +79,8 @@
 LANES = 128
 VMEM = 24 * 2**20
 NT = (((1,), (1,)), ((), ()))
-HIDE = 1 << 34
+HIDE = 1 << 36
+SMALL = 8 * 2**20
 TN = (((0,), (0,)), ((), ()))
 
 
@@ -135,6 +136,7 @@
         out_specs=[vmem] * 2,
         out_shape=[jax.ShapeDtypeStruct((rows, cols), jnp.bfloat16)] * 2,
         cost_estimate=pl.CostEstimate(flops=HIDE, bytes_accessed=2 << 20, transcendentals=0),
+        compiler_params=pltpu.CompilerParams(vmem_limit_bytes=SMALL),
         name="halves",
     )(place, weight)
 
@@ -165,23 +167,22 @@
         out_specs=vmem,
         out_shape=jax.ShapeDtypeStruct((2,) + own.shape, jnp.bfloat16),
         cost_estimate=pl.CostEstimate(flops=1 << 20, bytes_accessed=2 << 20, transcendentals=0),
+        compiler_params=pltpu.CompilerParams(vmem_limit_bytes=SMALL),
         name="join",
     )(place, own, got, far)
 
 
-def middle_kernel(place, xs, xo, w0, w1, w2, w3, d0, d1, ts, to, gm_ref, w_all, d_all, pick):
-    rows, cols = w0.shape
-    ff = d0.shape[0] // 2
-    count = xs.shape[0] // 2
-    width = ts.shape[1]
+def gather_weights(place, ws, ds, w_all, d_all, pick):
+    rows, cols = ws[0].shape
+    ff = ds[0].shape[0] // 2
     q, j = place[0], place[1]
     hidden = cols // 2
-    for k, w in enumerate((w0, w1, w2, w3)):
+    for k, w in enumerate(ws):
         w_all[pl.ds(pl.multiple_of((q ^ k) * rows, rows), rows), :] = w[...]
     r = q % 2
     for e in range(2):
-        d_all[pl.ds(pl.multiple_of((2 * e + r) * ff, ff), ff), :] = d0[pl.ds(e * ff, ff), :]
-        d_all[pl.ds(pl.multiple_of((2 * e + 1 - r) * ff, ff), ff), :] = d1[pl.ds(e * ff, ff), :]
+        d_all[pl.ds(pl.multiple_of((2 * e + r) * ff, ff), ff), :] = ds[0][pl.ds(e * ff, ff), :]
+        d_all[pl.ds(pl.multiple_of((2 * e + 1 - r) * ff, ff), ff), :] = ds[1][pl.ds(e * ff, ff), :]
     lane = lax.broadcasted_iota(jnp.int32, (LANES, cols), 0)
     col = lax.broadcasted_iota(jnp.int32, (LANES, cols), 1)
     n = LANES // 8
@@ -191,53 +192,57 @@
     hit = jnp.where(lane == first, 1.0, 0.0) + jnp.where(lane == second, 1.0, 0.0)
     pick[...] = hit.astype(jnp.bfloat16)
 
+
+def grad_mid(xs, xo, w_all, d_all, pick, gm, gw):
+    width, cols = w_all.shape
+    hidden = cols // 2
+    count = xs.shape[0] // 2
     for b in range(4):
-        x_ref, t_ref = (xs, ts) if b < 2 else (xo, to)
-        at = pl.ds((b % 2) * count, count)
-        gu = jnp.dot(x_ref[at, :width], w_all[...], preferred_element_type=jnp.float32)
+        x = xs if b < 2 else xo
+        at, to = pl.ds((b % 2) * count, count), pl.ds(b * count, count)
+        gu = jnp.dot(x[at, :width], w_all[...], preferred_element_type=jnp.float32)
         dh = lax.dot_general(
-            x_ref[at, width : 2 * width], d_all[...], NT, preferred_element_type=jnp.float32
+            x[at, width : 2 * width], d_all[...], NT, preferred_element_type=jnp.float32
         )
-        wm = jnp.dot(x_ref[at, 2 * width :], pick[...], preferred_element_type=jnp.float32)
+        wm = jnp.dot(x[at, 2 * width :], pick[...], preferred_element_type=jnp.float32)
         w, on = wm[:, :hidden], wm[:, hidden:]
         gate, up = gu[:, :hidden], gu[:, hidden:]
         sg = 0.5 * jnp.tanh(0.5 * gate) + 0.5
         dhs = dh * on * sg
         gg = dhs * up * (1.0 + gate * (1.0 - sg))
         gup = dhs * gate
-        gm_ref[pl.ds(b * count, count), :hidden] = gg.astype(jnp.bfloat16)
-        gm_ref[pl.ds(b * count, count), hidden:] = gup.astype(jnp.bfloat16)
-        gw = jnp.concatenate([(gg * w).astype(jnp.bfloat16), (gup * w).astype(jnp.bfloat16)], 1)
-        t_ref[at, :] = lax.dot_general(
-            gw, w_all[...], NT, preferred_element_type=jnp.float32
+        gm[to, :hidden] = gg.astype(jnp.bfloat16)
+        gm[to, hidden:] = gup.astype(jnp.bfloat16)
+        gw[to, :hidden] = (gg * w).astype(jnp.bfloat16)
+        gw[to, hidden:] = (gup * w).astype(jnp.bfloat16)
+
+
+def weights_kernel(place, w0, w1, w2, w3, d0, d1, w_all, d_all, pick):
+    gather_weights(place, (w0, w1, w2, w3), (d0, d1), w_all, d_all, pick)
+
+
+def vmem_call(kernel, name, outs, *args, place=None, flops=HIDE):
+    vmem = pl.BlockSpec(memory_space=pltpu.VMEM)
+    specs = [vmem] * len(args)
+    if place is not None:
+        args, specs = (place, *args), [pl.BlockSpec(memory_space=pltpu.SMEM)] + specs
+    return pl.pallas_call(
+        kernel,
+        in_specs=specs,
+        out_specs=[vmem] * len(outs),
+        out_shape=[jax.ShapeDtypeStruct(o, jnp.bfloat16) for o in outs],
+        compiler_params=pltpu.CompilerParams(vmem_limit_bytes=VMEM),
+        cost_estimate=pl.CostEstimate(flops=flops, bytes_accessed=12 << 20, transcendentals=0),
+        name=name,
+    )(*args)
+
+
+def token_kernel(gw, w_all, ts, to):
+    n = ts.shape[0]
+    for b, out in enumerate((ts, to)):
+        out[...] = lax.dot_general(
+            gw[pl.ds(b * n, n), :], w_all[...], NT, preferred_element_type=jnp.float32
         ).astype(jnp.bfloat16)
-
-
-def middle(place, xs, ws, ds):
-    n, wide = xs[0].shape
-    rows, cols = ws[0].shape
-    ffr, width = ds[0].shape
-    vmem = pl.BlockSpec(memory_space=pltpu.VMEM)
-    return pl.pallas_call(
-        middle_kernel,
-        in_specs=[pl.BlockSpec(memory_space=pltpu.SMEM)] + [vmem] * 8,
-        out_specs=[vmem] * 3,
-        scratch_shapes=[
-            pltpu.VMEM((4 * rows, cols), jnp.bfloat16),
-            pltpu.VMEM((2 * ffr, width), jnp.bfloat16),
-            pltpu.VMEM((LANES, cols), jnp.bfloat16),
-        ],
-        out_shape=[
-            jax.ShapeDtypeStruct((n, width), jnp.bfloat16),
-            jax.ShapeDtypeStruct((n, width), jnp.bfloat16),
-            jax.ShapeDtypeStruct((2 * n, cols), jnp.bfloat16),
-        ],
-        compiler_params=pltpu.CompilerParams(vmem_limit_bytes=VMEM),
-        cost_estimate=pl.CostEstimate(
-            flops=HIDE, bytes_accessed=12 << 20, transcendentals=n * cols
-        ),
-        name="middle",
-    )(place, *xs, *ws, *ds)
 
 
 def outer_kernel(scale, half, count, place, *refs):
@@ -291,7 +296,6 @@
     hops = [[(i, i ^ (2 * m)) for i in range(peers)] for m in (1, 2, 3)]
 
     payload = payload_of(tokens, cotangent, expert_ids, route_weights)
-    far_payload = lax.ppermute(payload, "dp", across)
 
     def spread(x):
         return [lax.ppermute(x, "expert", hop) for hop in hops]
@@ -302,22 +306,32 @@
     after = lax.optimization_barrier
 
     near = [payload] + spread(payload)
-    weight_in, weight_down, payload = after((weight_in, weight_down, payload))
+    far_payload = lax.ppermute(payload, "dp", across)
+    down1 = lax.ppermute(weight_down, "dp", beside)
+    weight_in, payload = after((weight_in, payload))
     kept, given = halves(place, weight_in.swapaxes(0, 1))
-    w1 = lax.ppermute(kept, "dp", beside)
-    given, weight_down, w1, far_payload, *near = after((given, weight_down, w1, far_payload, *near))
-    near_own = jnp.concatenate(near, 0)
+    given, kept, far_payload, down1, *near = after((given, kept, far_payload, down1, *near))
     far = [far_payload] + spread(far_payload)
     w2 = lax.ppermute(given, "dp", across)
+    w1 = lax.ppermute(kept, "dp", beside)
+    downs = [d.swapaxes(0, 1).reshape(2 * ff_rows, width) for d in (weight_down, down1)]
+    w2, w1, far[0] = after((w2, w1, far[0]))
+    w3 = lax.ppermute(w2, "dp", beside)
+    far_own = jnp.concatenate(far, 0)
+    far_sib = lax.ppermute(far_own, "expert", cores)
+    near_own = jnp.concatenate(near, 0)
+    tall, wide = near_own.shape
+    cols = kept.shape[1]
+    mid_shape, token_shape = (2 * tall, cols), (tall, width)
+    w_all, d_all, pick = vmem_call(
+        weights_kernel,
+        "weights",
+        [(width, cols), (4 * ff_rows, width), (LANES, cols)],
+        *(kept, w1, w2, w3, *downs),
+        place=place,
+    )
+    far_sib, w_all, near_own = after((far_sib, w_all, near_own))
     near_sib = lax.ppermute(near_own, "expert", cores)
-    near_sib, weight_down = after((near_sib, weight_down))
-    down = weight_down.swapaxes(0, 1).reshape(2 * ff_rows, width)
-    down1 = lax.ppermute(down, "dp", beside)
-    w2, down1, *far = after((w2, down1, *far))
-    far_own = jnp.concatenate(far, 0)
-    w3 = lax.ppermute(w2, "dp", beside)
-    far_sib = lax.ppermute(far_own, "expert", cores)
-    ws, ds = (kept, w1, w2, w3), (down, down1)
 
     def back_sums(own, got):
         return [plus(own[k * count : (k + 1) * count], got[k * count : (k + 1) * count]) for k in range(4)]
@@ -325,26 +339,43 @@
     def back_hops(sums):
         return [sums[0]] + [lax.ppermute(t, "expert", hop) for t, hop in zip(sums[1:], hops)]
 
-    near_ts, near_to, near_mid = middle(place, (near_sib, near_own), ws, ds)
+    def mids(name, sib, own):
+        return vmem_call(grad_mid, name, [mid_shape, mid_shape], sib, own, w_all, d_all, pick)
+
+    def backs(name, gw):
+        return vmem_call(
+            token_kernel, name, [token_shape] * 2, gw, w_all, flops=4 * tall * cols * width
+        )
+
+    far_mid, far_gw = mids("far", far_sib, far_own)
+    far_ts, far_to = backs("far_tokens", far_gw)
+    far_got = lax.ppermute(far_ts, "expert", cores)
+    near_sib, far_to = after((near_sib, far_to))
+    near_mid, near_gw = mids("near", near_sib, near_own)
+    far_got, near_mid = after((far_got, near_mid))
+    far_sums = back_sums(far_to, far_got)
+    near_mid, *far_sums = after((near_mid, *far_sums))
+    far_back = back_hops(far_sums)
+    tiles = (far_sib, far_own, near_sib, near_own)
+    (g3,) = outer(place, tiles, (far_mid, near_mid), grad_scale, rows, 3, 1)
+    got3 = lax.ppermute(g3, "dp", beside)
+    near_gw, g3 = after((near_gw, g3))
+    near_ts, near_to = backs("near_tokens", near_gw)
     near_got = lax.ppermute(near_ts, "expert", cores)
-    far_sib, near_mid = after((far_sib, near_mid))
-    far_ts, far_to, far_mid = middle(place, (far_sib, far_own), ws, ds)
-    far_got = lax.ppermute(far_ts, "expert", cores)
-    tiles, mids = (far_sib, far_own, near_sib, near_own), (far_mid, near_mid)
-    (g3,) = outer(place, tiles, mids, grad_scale, rows, 3, 1)
-    got3 = lax.ppermute(g3, "dp", beside)
-    far_sums, near_sums = back_sums(far_to, far_got), back_sums(near_to, near_got)
-    far_mid, *sums = after((far_mid, *far_sums, *near_sums))
-    far_sums, near_sums = sums[:4], sums[4:]
-    far_back = back_hops(far_sums)
-    g2, g1, g0 = outer(place, tiles, (far_mid, near_mid), grad_scale, rows, 2, 3)
+    near_mid, near_to = after((near_mid, near_to))
+    g2, g1 = outer(place, tiles, (far_mid, near_mid), grad_scale, rows, 2, 2)
+    near_got, g1 = after((near_got, g1))
     got1 = lax.ppermute(g1, "dp", beside)
-    got3, g2, *near_sums = after((got3, g2, *near_sums))
+    near_sums = back_sums(near_to, near_got)
+    near_mid, g1 = after((near_mid, g1))
+    (g0,) = outer(place, tiles, (far_mid, near_mid), grad_scale, rows, 0, 1)
+    got3, g0, *far_back = after((got3, g0, *far_back))
     relay = plus(g2, got3)
     away_half = lax.ppermute(relay, "dp", across)
-    near_back = back_hops(near_sums)
     away = sum(t.astype(jnp.float32) for t in far_back).astype(jnp.bfloat16)
     home = lax.ppermute(away, "dp", across)
+    *near_sums, got1 = after((*near_sums, got1))
+    near_back = back_hops(near_sums)
     near_total = sum(t.astype(jnp.float32) for t in near_back)
     token_grad = (near_total + home.astype(jnp.float32)).astype(jnp.bfloat16)
     grad_in = join(place, g0, got1, away_half).swapaxes(0, 1)

time: 145 us -> 128 us (0.88)
  the two profiles are of different devices: /device:TPU:25 before, /device:TPU:0 now
where the time goes in v2:
time: 128 us
  waiting for transfers between devices  68.1 us (53%)
  starting transfers between devices  29.7 us (23%)
  Pallas kernels  21.8 us (17%)
  other arithmetic  4.14 us (3%)
  local copies, waits for them, and re-layouts  3.49 us (3%)
    ppermute x1, waiting for transfers between devices, by_tokens(): down1 = lax.ppermute(weight_down, 'dp', beside)  15.9 us
    ppermute x1, waiting for transfers between devices, by_tokens(): w2 = lax.ppermute(given, 'dp', across)  14.2 us
    ppermute x1, waiting for transfers between devices, by_tokens(): away_half = lax.ppermute(relay, 'dp', across)  13.6 us
    pallas_call x5, Pallas kernels, vmem_call(): pl.pallas_call(kernel, in_specs=specs, out_specs=[vmem] * len(outs), out_...  11.4 us
    ppermute x1, waiting for transfers between devices, by_tokens(): got1 = lax.ppermute(g1, 'dp', beside)  9.71 us
    ppermute x6, starting transfers between devices, spread(): return [lax.ppermute(x, 'expert', hop) for hop in hops]  7.95 us
    ppermute x6, starting transfers between devices, back_hops(): lax.ppermute(t, 'expert', hop)  6.98 us
    pallas_call x3, Pallas kernels, outer(): pl.pallas_call(functools.partial(outer_kernel, scale, len(gs), count), gr...  6.69 us
  transfers between devices with their start and end apart: 25, of which 12 were waited for; matrix products, arithmetic and copies ran while one was open for 4% of the time, Pallas kernels for 16%

profile of v2, /device:TPU:0, one launch (start us, length us, event | category | flops | bytes accessed | tf_op | source)
XLA Modules:
  0.0 128.2 jit_solution(6866303778374256294)
XLA Ops:
  0.6 2.0 %payload.1 = bf16[128,2176]{1,0:T(8,128)(2,1)} custom-call(bf16[128,1024]{1,0:T(8,128)(2,1)} %tokens.1, bf16[128,1024]{1,0:T(8,128)(2,1)} %cotangent.1, s32[8,128]{1,0:T(8,128)} %bitcast.18, f32[8,128]{1,0:T(8,128)} %bitcast.19), custom_call_target="tpu_custom_call" | custom-call | flops 1048576 | bytes 2097152 | tf_op jit(solution)/shard_map/payload/pallas_call | solution.py:106
  2.6 3.9 %collective-permute-start.4 = (bf16[128,2176]{1,0:T(8,128)(2,1)}, bf16[128,2176]{1,0:T(8,128)(2,1)S(1)}, u32[]{:S(2)}, u32[]{:S(2)}) collective-permute-start(bf16[128,2176]{1,0:T(8,128)(2,1)} %payload.1), channel_id=1, source_target_pairs={{0,6},{1,7},{2,4},{3,5},{4,2},{5,3},{6,0},{7,1},{8,14},{9,15},{10,... | collective-permute-start | bytes 1671176 | tf_op jit(solution)/shard_map/ppermute | solution.py:301
  6.5 0.5 collective-permute-start.3
  7.0 3.1 %collective-permute-start = (bf16[128,2176]{1,0:T(8,128)(2,1)}, bf16[128,2176]{1,0:T(8,128)(2,1)S(1)}, u32[]{:S(2)}, u32[]{:S(2)}) collective-permute-start(bf16[128,2176]{1,0:T(8,128)(2,1)} %payload.1), channel_id=1, source_target_pairs={{0,16},{8,24},{16,0},{24,8},{1,17},{9,25},{17,1},{25,9},{2,18},{10... | collective-permute-start | bytes 1671176 | tf_op jit(solution)/shard_map/ppermute | solution.py:309
  10.1 1.6 %collective-permute-start.1 = (bf16[96,2,1024]{2,1,0:T(2,128)(2,1)}, bf16[96,2,1024]{2,1,0:T(2,128)(2,1)S(1)}, u32[]{:S(2)}, u32[]{:S(2)}) collective-permute-start(bf16[96,2,1024]{2,1,0:T(2,128)(2,1)} %param.11), channel_id=1, source_target_pairs={{0,8},{8,0},{16,24},{24,16},{1,9},{9,1},{17,25},{25,17},{2,10},{10... | collective-permute-start | bytes 1179656 | tf_op jit(solution)/shard_map/ppermute | solution.py:310
  11.7 1.2 copy.13
  13.0 0.8 halves.1
  13.8 0.2 copy-done.2
  14.1 15.9 %collective-permute-done.1 = bf16[96,2,1024]{2,1,0:T(2,128)(2,1)S(1)} collective-permute-done((bf16[96,2,1024]{2,1,0:T(2,128)(2,1)}, bf16[96,2,1024]{2,1,0:T(2,128)(2,1)S(1)}, u32[]{:S(2)}, u32[]{:S(2)}) %collective-permute-start.1) | collective-permute-done | bytes 393248 | tf_op jit(solution)/shard_map/ppermute | solution.py:310
  29.9 1.3 %collective-permute-done.3 = bf16[128,2176]{1,0:T(8,128)(2,1)S(1)} collective-permute-done((bf16[128,2176]{1,0:T(8,128)(2,1)}, bf16[128,2176]{1,0:T(8,128)(2,1)S(1)}, u32[]{:S(2)}, u32[]{:S(2)}) %collective-permute-start.3) | collective-permute-done | bytes 557088 | tf_op jit(solution)/shard_map/ppermute | solution.py:301
  31.3 0.3 collective-permute-done.2
  31.5 2.5 %collective-permute-done = bf16[128,2176]{1,0:T(8,128)(2,1)S(1)} collective-permute-done((bf16[128,2176]{1,0:T(8,128)(2,1)}, bf16[128,2176]{1,0:T(8,128)(2,1)S(1)}, u32[]{:S(2)}, u32[]{:S(2)}) %collective-permute-start) | collective-permute-done | bytes 557088 | tf_op jit(solution)/shard_map/ppermute | solution.py:309
  34.1 2.5 %collective-permute-start.9 = (bf16[128,2176]{1,0:T(8,128)(2,1)S(1)}, bf16[128,2176]{1,0:T(8,128)(2,1)S(1)}, u32[]{:S(2)}, u32[]{:S(2)}) collective-permute-start(bf16[128,2176]{1,0:T(8,128)(2,1)S(1)} %collective-permute-done), channel_id=1, source_target_pairs={{0,6},{1,7},{2,4},{3,5},{4,2},{5,3},{6,0},{7,1},{8,14},{9,15},{10,... | collective-permute-start | bytes 1671176 | tf_op jit(solution)/shard_map/ppermute | solution.py:301
  36.6 0.5 collective-permute-start.8
  37.1 0.5 collective-permute-start.7
  37.6 4.0 %collective-permute-start.6 = (bf16[256,768]{1,0:T(8,128)(2,1)S(1)}, bf16[256,768]{1,0:T(8,128)(2,1)S(1)}, u32[]{:S(2)}, u32[]{:S(2)}) collective-permute-start(bf16[256,768]{1,0:T(8,128)(2,1)S(1)} %get-tuple-element.62.w0), channel_id=1, source_target_pairs={{0,8},{8,0},{16,24},{24,16},{1,9},{9,1},{17,25},{25,17},{2,10},{10... | collective-permute-start | bytes 1179656 | tf_op jit(solution)/shard_map/ppermute | solution.py:316
  41.6 0.2 pad_maximum_fusion.xo.refs_3_
  41.9 14.2 %collective-permute-done.5.w2 = bf16[256,768]{1,0:T(8,128)(2,1)S(1)} collective-permute-done((bf16[256,768]{1,0:T(8,128)(2,1)S(1)}, bf16[256,768]{1,0:T(8,128)(2,1)S(1)}, u32[]{:S(2)}, u32[]{:S(2)}) %collective-permute-start.5) | collective-permute-done | bytes 393248 | tf_op jit(solution)/shard_map/ppermute | solution.py:315
  56.2 4.3 %collective-permute-done.7 = bf16[128,2176]{1,0:T(8,128)(2,1)S(1)} collective-permute-done((bf16[128,2176]{1,0:T(8,128)(2,1)S(1)}, bf16[128,2176]{1,0:T(8,128)(2,1)S(1)}, u32[]{:S(2)}, u32[]{:S(2)}) %collective-permute-start.7) | collective-permute-done | bytes 557088 | tf_op jit(solution)/shard_map/ppermute | solution.py:301
  60.8 4.2 %collective-permute-done.11.w3 = bf16[256,768]{1,0:T(8,128)(2,1)S(1)} collective-permute-done((bf16[256,768]{1,0:T(8,128)(2,1)S(1)}, bf16[256,768]{1,0:T(8,128)(2,1)S(1)}, u32[]{:S(2)}, u32[]{:S(2)}) %collective-permute-start.11) | collective-permute-done | bytes 393248 | tf_op jit(solution)/shard_map/ppermute | solution.py:319
  65.0 0.7 weights.1
  65.8 3.6 %far.1 = (bf16[1024,768]{1,0:T(8,128)(2,1)S(1)}, bf16[1024,768]{1,0:T(8,128)(2,1)S(1)}) custom-call(bf16[512,2176]{1,0:T(8,128)(2,1)S(1)} %collective-permute-done.10.xs.refs_0_, bf16[512,2176]{1,0:T(8,128)(2,1)S(1)} %constant_dynamic-update-slice_fusion.xo.refs_1_, bf16[1024,768]{1,0:T(8,128)(2,1)S(1)} %get-tuple-element.74.w_all, ...), custom_call_target="tpu_custom_call" | custom-call | flops 68719476736 | bytes 12582912 | tf_op jit(solution)/shard_map/far/pallas_call | solution.py:229
  69.4 1.8 %far_tokens.1 = (bf16[512,1024]{1,0:T(8,128)(2,1)S(1)}, bf16[512,1024]{1,0:T(8,128)(2,1)S(1)}) custom-call(bf16[1024,768]{1,0:T(8,128)(2,1)S(1)} %get-tuple-element.77.gw, bf16[1024,768]{1,0:T(8,128)(2,1)S(1)} %get-tuple-element.74.w_all), custom_call_target="tpu_custom_call" | custom-call | flops 1610612736 | bytes 12582912 | tf_op jit(solution)/shard_map/far_tokens/pallas_call | solution.py:229
  71.3 0.6 collective-permute-start.12
  71.8 3.5 %near.1 = (bf16[1024,768]{1,0:T(8,128)(2,1)S(1)}, bf16[1024,768]{1,0:T(8,128)(2,1)S(1)}) custom-call(bf16[512,2176]{1,0:T(8,128)(2,1)S(1)} %collective-permute-done.13.xs.refs_2_, bf16[512,2176]{1,0:T(8,128)(2,1)S(1)} %pad_maximum_fusion.xo.refs_3_, bf16[1024,768]{1,0:T(8,128)(2,1)S(1)} %get-tuple-element.74.w_all, ...), custom_call_target="tpu_custom_call" | custom-call | flops 68719476736 | bytes 12582912 | tf_op jit(solution)/shard_map/near/pallas_call | solution.py:229
  75.3 1.2 add_convert_fusion.7
  76.6 1.6 %collective-permute-start.20 = (bf16[128,1024]{1,0:T(8,128)(2,1)}, bf16[128,1024]{1,0:T(8,128)(2,1)}, u32[]{:S(2)}, u32[]{:S(2)}) collective-permute-start(bf16[128,1024]{1,0:T(8,128)(2,1)} %get-tuple-element.103), channel_id=1, source_target_pairs={{0,2},{1,3},{2,0},{3,1},{4,6},{5,7},{6,4},{7,5},{8,10},{9,11},{10,... | collective-permute-start | bytes 786440 | tf_op jit(solution)/shard_map/ppermute | solution.py:340
  78.2 1.5 %collective-permute-start.21 = (bf16[128,1024]{1,0:T(8,128)(2,1)}, bf16[128,1024]{1,0:T(8,128)(2,1)}, u32[]{:S(2)}, u32[]{:S(2)}) collective-permute-start(bf16[128,1024]{1,0:T(8,128)(2,1)} %get-tuple-element.104), channel_id=1, source_target_pairs={{0,4},{1,5},{2,6},{3,7},{4,0},{5,1},{6,2},{7,3},{8,12},{9,13},{10,... | collective-permute-start | bytes 786440 | tf_op jit(solution)/shard_map/ppermute | solution.py:340
  79.7 0.3 collective-permute-start.22
  80.0 1.9 %outer.3 = bf16[256,768]{1,0:T(8,128)(2,1)S(1)} custom-call(s32[2]{0:T(128)S(1)} %pad_add_fusion.place, bf16[512,2176]{1,0:T(8,128)(2,1)S(1)} %collective-permute-done.10.xs.refs_0_, bf16[512,2176]{1,0:T(8,128)(2,1)S(1)} %constant_dynamic-update-slice_fusion.xo.refs_1_, bf16[512,2176]{1,0:T(8,128)(2,1)S(1)} %collective-permute-done.13.xs.refs_2_, ...), custom_call_target="tpu_custom_call" | custom-call | flops 68719476736 | bytes 12582912 | tf_op jit(solution)/shard_map/outer/pallas_call | solution.py:265
  81.9 1.3 %collective-permute-start.19 = (bf16[256,768]{1,0:T(8,128)(2,1)S(1)}, bf16[256,768]{1,0:T(8,128)(2,1)S(1)}, u32[]{:S(2)}, u32[]{:S(2)}) collective-permute-start(bf16[256,768]{1,0:T(8,128)(2,1)S(1)} %outer.3), channel_id=1, source_target_pairs={{0,8},{8,0},{16,24},{24,16},{1,9},{9,1},{17,25},{25,17},{2,10},{10... | collective-permute-start | bytes 1179656 | tf_op jit(solution)/shard_map/ppermute | solution.py:361
  83.2 1.8 %near_tokens.1 = (bf16[512,1024]{1,0:T(8,128)(2,1)S(1)}, bf16[512,1024]{1,0:T(8,128)(2,1)S(1)}) custom-call(bf16[1024,768]{1,0:T(8,128)(2,1)S(1)} %get-tuple-element.89.gw, bf16[1024,768]{1,0:T(8,128)(2,1)S(1)} %get-tuple-element.74.w_all), custom_call_target="tpu_custom_call" | custom-call | flops 1610612736 | bytes 12582912 | tf_op jit(solution)/shard_map/near_tokens/pallas_call | solution.py:229
  85.1 3.1 %outer.4 = (bf16[256,768]{1,0:T(8,128)(2,1)S(1)}, bf16[256,768]{1,0:T(8,128)(2,1)S(1)}) custom-call(s32[2]{0:T(128)S(1)} %pad_add_fusion.place, bf16[512,2176]{1,0:T(8,128)(2,1)S(1)} %collective-permute-done.10.xs.refs_0_, bf16[512,2176]{1,0:T(8,128)(2,1)S(1)} %constant_dynamic-update-slice_fusion.xo.refs_1_, ...), custom_call_target="tpu_custom_call" | custom-call | flops 68719476736 | bytes 12582912 | tf_op jit(solution)/shard_map/outer/pallas_call | solution.py:265
  88.3 0.9 collective-permute-start.15
  89.1 1.7 %outer.5.own = bf16[256,768]{1,0:T(8,128)(2,1)S(1)} custom-call(s32[2]{0:T(128)S(1)} %pad_add_fusion.place, bf16[512,2176]{1,0:T(8,128)(2,1)S(1)} %collective-permute-done.10.xs.refs_0_, bf16[512,2176]{1,0:T(8,128)(2,1)S(1)} %constant_dynamic-update-slice_fusion.xo.refs_1_, bf16[512,2176]{1,0:T(8,128)(2,1)S(1)} %collective-permute-done.13.xs.refs_2_, ...), custom_call_target="tpu_custom_call" | custom-call | flops 68719476736 | bytes 12582912 | tf_op jit(solution)/shard_map/outer/pallas_call | solution.py:265
  90.9 1.2 collective-permute-done.21
  92.1 0.8 collective-permute-done.19
  92.9 1.2 add_convert_fusion.2
  94.2 3.0 %collective-permute-start.23 = (bf16[128,1024]{1,0:T(8,128)(2,1)S(1)}, bf16[128,1024]{1,0:T(8,128)(2,1)S(1)}, u32[]{:S(2)}, u32[]{:S(2)}) collective-permute-start(bf16[128,1024]{1,0:T(8,128)(2,1)S(1)} %add_convert_fusion.2), channel_id=1, source_target_pairs={{0,16},{8,24},{16,0},{24,8},{1,17},{9,25},{17,1},{25,9},{2,18},{10... | collective-permute-start | bytes 786440 | tf_op jit(solution)/shard_map/ppermute | solution.py:376
  97.4 0.4 add_convert_fusion.3
  97.8 9.7 %collective-permute-done.15.got = bf16[256,768]{1,0:T(8,128)(2,1)S(1)} collective-permute-done((bf16[256,768]{1,0:T(8,128)(2,1)S(1)}, bf16[256,768]{1,0:T(8,128)(2,1)S(1)}, u32[]{:S(2)}, u32[]{:S(2)}) %collective-permute-start.15) | collective-permute-done | bytes 393248 | tf_op jit(solution)/shard_map/ppermute | solution.py:368
  107.5 1.6 %collective-permute-start.16 = (bf16[128,1024]{1,0:T(8,128)(2,1)S(1)}, bf16[128,1024]{1,0:T(8,128)(2,1)S(1)}, u32[]{:S(2)}, u32[]{:S(2)}) collective-permute-start(bf16[128,1024]{1,0:T(8,128)(2,1)S(1)} %get-tuple-element.98), channel_id=1, source_target_pairs={{0,2},{1,3},{2,0},{3,1},{4,6},{5,7},{6,4},{7,5},{8,10},{9,11},{10,... | collective-permute-start | bytes 786440 | tf_op jit(solution)/shard_map/ppermute | solution.py:340
  109.1 1.5 %collective-permute-start.17 = (bf16[128,1024]{1,0:T(8,128)(2,1)S(1)}, bf16[128,1024]{1,0:T(8,128)(2,1)S(1)}, u32[]{:S(2)}, u32[]{:S(2)}) collective-permute-start(bf16[128,1024]{1,0:T(8,128)(2,1)S(1)} %get-tuple-element.99), channel_id=1, source_target_pairs={{0,4},{1,5},{2,6},{3,7},{4,0},{5,1},{6,2},{7,3},{8,12},{9,13},{10,... | collective-permute-start | bytes 786440 | tf_op jit(solution)/shard_map/ppermute | solution.py:340
  110.7 0.3 collective-permute-start.18
  111.0 13.6 %collective-permute-done.24.far = bf16[256,768]{1,0:T(8,128)(2,1)S(1)} collective-permute-done((bf16[256,768]{1,0:T(8,128)(2,1)S(1)}, bf16[256,768]{1,0:T(8,128)(2,1)S(1)}, u32[]{:S(2)}, u32[]{:S(2)}) %collective-permute-start.24) | collective-permute-done | bytes 393248 | tf_op jit(solution)/shard_map/ppermute | solution.py:374
  124.6 1.0 join.1
  125.6 1.7 %copy.11 = bf16[256,2,768]{2,1,0:T(2,128)(2,1)} copy(bf16[256,2,768]{2,0,1:T(8,128)(2,1)S(1)} %bitcast.12) | data formatting | bytes 1572864
  127.3 0.9 add_convert_fusion.1
  (34 shorter events, 1.1 us)
Async XLA Ops:
  2.6 27.4 %collective-permute-start.4 = (bf16[128,2176]{1,0:T(8,128)(2,1)}, bf16[128,2176]{1,0:T(8,128)(2,1)S(1)}, u32[]{:S(2)}, u32[]{:S(2)}) collective-permute-start(bf16[128,2176]{1,0:T(8,128)(2,1)} %payload.1), channel_id=1, source_target_pairs={{0,6},{1,7},{2,4},{3,5},{4,2},{5,3},{6,0},{7,1},{8,14},{9,15},{10,... | collective-permute-start | bytes 1671176 | tf_op jit(solution)/shard_map/ppermute | solution.py:301
  6.5 24.8 %collective-permute-start.3 = (bf16[128,2176]{1,0:T(8,128)(2,1)}, bf16[128,2176]{1,0:T(8,128)(2,1)S(1)}, u32[]{:S(2)}, u32[]{:S(2)}) collective-permute-start(bf16[128,2176]{1,0:T(8,128)(2,1)} %payload.1), channel_id=1, source_target_pairs={{0,4},{1,5},{2,6},{3,7},{4,0},{5,1},{6,2},{7,3},{8,12},{9,13},{10,... | collective-permute-start | bytes 1671176 | tf_op jit(solution)/shard_map/ppermute | solution.py:301
  7.0 24.6 %collective-permute-start.2 = (bf16[128,2176]{1,0:T(8,128)(2,1)}, bf16[128,2176]{1,0:T(8,128)(2,1)S(1)}, u32[]{:S(2)}, u32[]{:S(2)}) collective-permute-start(bf16[128,2176]{1,0:T(8,128)(2,1)} %payload.1), channel_id=1, source_target_pairs={{0,2},{1,3},{2,0},{3,1},{4,6},{5,7},{6,4},{7,5},{8,10},{9,11},{10,... | collective-permute-start | bytes 1671176 | tf_op jit(solution)/shard_map/ppermute | solution.py:301
  7.0 27.0 %collective-permute-start = (bf16[128,2176]{1,0:T(8,128)(2,1)}, bf16[128,2176]{1,0:T(8,128)(2,1)S(1)}, u32[]{:S(2)}, u32[]{:S(2)}) collective-permute-start(bf16[128,2176]{1,0:T(8,128)(2,1)} %payload.1), channel_id=1, source_target_pairs={{0,16},{8,24},{16,0},{24,8},{1,17},{9,25},{17,1},{25,9},{2,18},{10... | collective-permute-start | bytes 1671176 | tf_op jit(solution)/shard_map/ppermute | solution.py:309
  10.1 19.8 %collective-permute-start.1 = (bf16[96,2,1024]{2,1,0:T(2,128)(2,1)}, bf16[96,2,1024]{2,1,0:T(2,128)(2,1)S(1)}, u32[]{:S(2)}, u32[]{:S(2)}) collective-permute-start(bf16[96,2,1024]{2,1,0:T(2,128)(2,1)} %param.11), channel_id=1, source_target_pairs={{0,8},{8,0},{16,24},{24,16},{1,9},{9,1},{17,25},{25,17},{2,10},{10... | collective-permute-start | bytes 1179656 | tf_op jit(solution)/shard_map/ppermute | solution.py:310
  13.0 1.0 copy-start.2
  13.0 28.7 %copy-start = (bf16[128,2176]{1,0:T(8,128)(2,1)S(1)}, bf16[128,2176]{1,0:T(8,128)(2,1)}, u32[]{:S(2)}) copy-start(bf16[128,2176]{1,0:T(8,128)(2,1)} %payload.1) | copy-start | bytes 1671172
  34.1 26.6 %collective-permute-start.9 = (bf16[128,2176]{1,0:T(8,128)(2,1)S(1)}, bf16[128,2176]{1,0:T(8,128)(2,1)S(1)}, u32[]{:S(2)}, u32[]{:S(2)}) collective-permute-start(bf16[128,2176]{1,0:T(8,128)(2,1)S(1)} %collective-permute-done), channel_id=1, source_target_pairs={{0,6},{1,7},{2,4},{3,5},{4,2},{5,3},{6,0},{7,1},{8,14},{9,15},{10,... | collective-permute-start | bytes 1671176 | tf_op jit(solution)/shard_map/ppermute | solution.py:301
  36.6 24.0 %collective-permute-start.8 = (bf16[128,2176]{1,0:T(8,128)(2,1)S(1)}, bf16[128,2176]{1,0:T(8,128)(2,1)S(1)}, u32[]{:S(2)}, u32[]{:S(2)}) collective-permute-start(bf16[128,2176]{1,0:T(8,128)(2,1)S(1)} %collective-permute-done), channel_id=1, source_target_pairs={{0,4},{1,5},{2,6},{3,7},{4,0},{5,1},{6,2},{7,3},{8,12},{9,13},{10,... | collective-permute-start | bytes 1671176 | tf_op jit(solution)/shard_map/ppermute | solution.py:301
  37.1 23.4 %collective-permute-start.7 = (bf16[128,2176]{1,0:T(8,128)(2,1)S(1)}, bf16[128,2176]{1,0:T(8,128)(2,1)S(1)}, u32[]{:S(2)}, u32[]{:S(2)}) collective-permute-start(bf16[128,2176]{1,0:T(8,128)(2,1)S(1)} %collective-permute-done), channel_id=1, source_target_pairs={{0,2},{1,3},{2,0},{3,1},{4,6},{5,7},{6,4},{7,5},{8,10},{9,11},{10,... | collective-permute-start | bytes 1671176 | tf_op jit(solution)/shard_map/ppermute | solution.py:301
  37.6 18.5 %collective-permute-start.5 = (bf16[256,768]{1,0:T(8,128)(2,1)S(1)}, bf16[256,768]{1,0:T(8,128)(2,1)S(1)}, u32[]{:S(2)}, u32[]{:S(2)}) collective-permute-start(bf16[256,768]{1,0:T(8,128)(2,1)S(1)} %get-tuple-element.61), channel_id=1, source_target_pairs={{0,16},{8,24},{16,0},{24,8},{1,17},{9,25},{17,1},{25,9},{2,18},{10... | collective-permute-start | bytes 1179656 | tf_op jit(solution)/shard_map/ppermute | solution.py:315
  37.6 18.5 %collective-permute-start.6 = (bf16[256,768]{1,0:T(8,128)(2,1)S(1)}, bf16[256,768]{1,0:T(8,128)(2,1)S(1)}, u32[]{:S(2)}, u32[]{:S(2)}) collective-permute-start(bf16[256,768]{1,0:T(8,128)(2,1)S(1)} %get-tuple-element.62.w0), channel_id=1, source_target_pairs={{0,8},{8,0},{16,24},{24,16},{1,9},{9,1},{17,25},{25,17},{2,10},{10... | collective-permute-start | bytes 1179656 | tf_op jit(solution)/shard_map/ppermute | solution.py:316
  56.2 8.9 %collective-permute-start.11 = (bf16[256,768]{1,0:T(8,128)(2,1)S(1)}, bf16[256,768]{1,0:T(8,128)(2,1)S(1)}, u32[]{:S(2)}, u32[]{:S(2)}) collective-permute-start(bf16[256,768]{1,0:T(8,128)(2,1)S(1)} %collective-permute-done.5.w2), channel_id=1, source_target_pairs={{0,8},{8,0},{16,24},{24,16},{1,9},{9,1},{17,25},{25,17},{2,10},{10... | collective-permute-start | bytes 1179656 | tf_op jit(solution)/shard_map/ppermute | solution.py:319
  60.7 5.0 %collective-permute-start.10 = (bf16[512,2176]{1,0:T(8,128)(2,1)S(1)}, bf16[512,2176]{1,0:T(8,128)(2,1)S(1)}, u32[]{:S(2)}, u32[]{:S(2)}) collective-permute-start(bf16[512,2176]{1,0:T(8,128)(2,1)S(1)} %constant_dynamic-update-slice_fusion.xo.refs_1_), channel_id=1, source_target_pairs={{0,1},{1,0},{2,3},{3,2},{4,5},{5,4},{6,7},{7,6},{8,9},{9,8},{10,11... | collective-permute-start | bytes 6684680 | tf_op jit(solution)/shard_map/ppermute | solution.py:321
  65.7 6.1 %collective-permute-start.13 = (bf16[512,2176]{1,0:T(8,128)(2,1)S(1)}, bf16[512,2176]{1,0:T(8,128)(2,1)S(1)}, u32[]{:S(2)}, u32[]{:S(2)}) collective-permute-start(bf16[512,2176]{1,0:T(8,128)(2,1)S(1)} %pad_maximum_fusion.xo.refs_3_), channel_id=1, source_target_pairs={{0,1},{1,0},{2,3},{3,2},{4,5},{5,4},{6,7},{7,6},{8,9},{9,8},{10,11... | collective-permute-start | bytes 6684680 | tf_op jit(solution)/shard_map/ppermute | solution.py:334
  71.3 4.0 %collective-permute-start.12 = (bf16[512,1024]{1,0:T(8,128)(2,1)S(1)}, bf16[512,1024]{1,0:T(8,128)(2,1)S(1)}, u32[]{:S(2)}, u32[]{:S(2)}) collective-permute-start(bf16[512,1024]{1,0:T(8,128)(2,1)S(1)} %get-tuple-element.78), channel_id=1, source_target_pairs={{0,1},{1,0},{2,3},{3,2},{4,5},{5,4},{6,7},{7,6},{8,9},{9,8},{10,11... | collective-permute-start | bytes 3145736 | tf_op jit(solution)/shard_map/ppermute | solution.py:352
  76.6 14.3 %collective-permute-start.20 = (bf16[128,1024]{1,0:T(8,128)(2,1)}, bf16[128,1024]{1,0:T(8,128)(2,1)}, u32[]{:S(2)}, u32[]{:S(2)}) collective-permute-start(bf16[128,1024]{1,0:T(8,128)(2,1)} %get-tuple-element.103), channel_id=1, source_target_pairs={{0,2},{1,3},{2,0},{3,1},{4,6},{5,7},{6,4},{7,5},{8,10},{9,11},{10,... | collective-permute-start | bytes 786440 | tf_op jit(solution)/shard_map/ppermute | solution.py:340
  78.2 13.9 %collective-permute-start.21 = (bf16[128,1024]{1,0:T(8,128)(2,1)}, bf16[128,1024]{1,0:T(8,128)(2,1)}, u32[]{:S(2)}, u32[]{:S(2)}) collective-permute-start(bf16[128,1024]{1,0:T(8,128)(2,1)} %get-tuple-element.104), channel_id=1, source_target_pairs={{0,4},{1,5},{2,6},{3,7},{4,0},{5,1},{6,2},{7,3},{8,12},{9,13},{10,... | collective-permute-start | bytes 786440 | tf_op jit(solution)/shard_map/ppermute | solution.py:340
  79.7 12.4 %collective-permute-start.22 = (bf16[128,1024]{1,0:T(8,128)(2,1)}, bf16[128,1024]{1,0:T(8,128)(2,1)}, u32[]{:S(2)}, u32[]{:S(2)}) collective-permute-start(bf16[128,1024]{1,0:T(8,128)(2,1)} %get-tuple-element.105), channel_id=1, source_target_pairs={{0,6},{1,7},{2,4},{3,5},{4,2},{5,3},{6,0},{7,1},{8,14},{9,15},{10,... | collective-permute-start | bytes 786440 | tf_op jit(solution)/shard_map/ppermute | solution.py:340
  81.9 11.0 %collective-permute-start.19 = (bf16[256,768]{1,0:T(8,128)(2,1)S(1)}, bf16[256,768]{1,0:T(8,128)(2,1)S(1)}, u32[]{:S(2)}, u32[]{:S(2)}) collective-permute-start(bf16[256,768]{1,0:T(8,128)(2,1)S(1)} %outer.3), channel_id=1, source_target_pairs={{0,8},{8,0},{16,24},{24,16},{1,9},{9,1},{17,25},{25,17},{2,10},{10... | collective-permute-start | bytes 1179656 | tf_op jit(solution)/shard_map/ppermute | solution.py:361
  85.1 3.2 %collective-permute-start.14 = (bf16[512,1024]{1,0:T(8,128)(2,1)S(1)}, bf16[512,1024]{1,0:T(8,128)(2,1)S(1)}, u32[]{:S(2)}, u32[]{:S(2)}) collective-permute-start(bf16[512,1024]{1,0:T(8,128)(2,1)S(1)} %get-tuple-element.92), channel_id=1, source_target_pairs={{0,1},{1,0},{2,3},{3,2},{4,5},{5,4},{6,7},{7,6},{8,9},{9,8},{10,11... | collective-permute-start | bytes 3145736 | tf_op jit(solution)/shard_map/ppermute | solution.py:364
  88.3 4.7 %copy-start.1 = (bf16[128,1024]{1,0:T(8,128)(2,1)S(1)}, bf16[128,1024]{1,0:T(8,128)(2,1)}, u32[]{:S(2)}) copy-start(bf16[128,1024]{1,0:T(8,128)(2,1)} %get-tuple-element.106) | copy-start | bytes 786436
  88.3 19.2 %collective-permute-start.15 = (bf16[256,768]{1,0:T(8,128)(2,1)S(1)}, bf16[256,768]{1,0:T(8,128)(2,1)S(1)}, u32[]{:S(2)}, u32[]{:S(2)}) collective-permute-start(bf16[256,768]{1,0:T(8,128)(2,1)S(1)} %get-tuple-element.96), channel_id=1, source_target_pairs={{0,8},{8,0},{16,24},{24,16},{1,9},{9,1},{17,25},{25,17},{2,10},{10... | collective-permute-start | bytes 1179656 | tf_op jit(solution)/shard_map/ppermute | solution.py:368
  94.2 33.1 %collective-permute-start.23 = (bf16[128,1024]{1,0:T(8,128)(2,1)S(1)}, bf16[128,1024]{1,0:T(8,128)(2,1)S(1)}, u32[]{:S(2)}, u32[]{:S(2)}) collective-permute-start(bf16[128,1024]{1,0:T(8,128)(2,1)S(1)} %add_convert_fusion.2), channel_id=1, source_target_pairs={{0,16},{8,24},{16,0},{24,8},{1,17},{9,25},{17,1},{25,9},{2,18},{10... | collective-permute-start | bytes 786440 | tf_op jit(solution)/shard_map/ppermute | solution.py:376
  97.3 27.3 %collective-permute-start.24 = (bf16[256,768]{1,0:T(8,128)(2,1)S(1)}, bf16[256,768]{1,0:T(8,128)(2,1)S(1)}, u32[]{:S(2)}, u32[]{:S(2)}) collective-permute-start(bf16[256,768]{1,0:T(8,128)(2,1)S(1)} %add_convert_fusion), channel_id=1, source_target_pairs={{0,16},{8,24},{16,0},{24,8},{1,17},{9,25},{17,1},{25,9},{2,18},{10... | collective-permute-start | bytes 1179656 | tf_op jit(solution)/shard_map/ppermute | solution.py:374
  107.5 19.8 %collective-permute-start.16 = (bf16[128,1024]{1,0:T(8,128)(2,1)S(1)}, bf16[128,1024]{1,0:T(8,128)(2,1)S(1)}, u32[]{:S(2)}, u32[]{:S(2)}) collective-permute-start(bf16[128,1024]{1,0:T(8,128)(2,1)S(1)} %get-tuple-element.98), channel_id=1, source_target_pairs={{0,2},{1,3},{2,0},{3,1},{4,6},{5,7},{6,4},{7,5},{8,10},{9,11},{10,... | collective-permute-start | bytes 786440 | tf_op jit(solution)/shard_map/ppermute | solution.py:340
  109.1 18.1 %collective-permute-start.17 = (bf16[128,1024]{1,0:T(8,128)(2,1)S(1)}, bf16[128,1024]{1,0:T(8,128)(2,1)S(1)}, u32[]{:S(2)}, u32[]{:S(2)}) collective-permute-start(bf16[128,1024]{1,0:T(8,128)(2,1)S(1)} %get-tuple-element.99), channel_id=1, source_target_pairs={{0,4},{1,5},{2,6},{3,7},{4,0},{5,1},{6,2},{7,3},{8,12},{9,13},{10,... | collective-permute-start | bytes 786440 | tf_op jit(solution)/shard_map/ppermute | solution.py:340
  110.7 16.6 %collective-permute-start.18 = (bf16[128,1024]{1,0:T(8,128)(2,1)S(1)}, bf16[128,1024]{1,0:T(8,128)(2,1)S(1)}, u32[]{:S(2)}, u32[]{:S(2)}) collective-permute-start(bf16[128,1024]{1,0:T(8,128)(2,1)S(1)} %get-tuple-element.100), channel_id=1, source_target_pairs={{0,6},{1,7},{2,4},{3,5},{4,2},{5,3},{6,0},{7,1},{8,14},{9,15},{10,... | collective-permute-start | bytes 786440 | tf_op jit(solution)/shard_map/ppermute | solution.py:340

commit v3 on v2

--- a/solution.py
+++ b/solution.py
@@ -135,7 +135,7 @@
         in_specs=[pl.BlockSpec(memory_space=pltpu.SMEM), vmem],
         out_specs=[vmem] * 2,
         out_shape=[jax.ShapeDtypeStruct((rows, cols), jnp.bfloat16)] * 2,
-        cost_estimate=pl.CostEstimate(flops=HIDE, bytes_accessed=2 << 20, transcendentals=0),
+        cost_estimate=pl.CostEstimate(flops=1 << 20, bytes_accessed=2 << 20, transcendentals=0),
         compiler_params=pltpu.CompilerParams(vmem_limit_bytes=SMALL),
         name="halves",
     )(place, weight)
@@ -260,7 +260,7 @@
             outs[k][...] = value
 
 
-def outer(place, xs, gs, scale, rows, top, count):
+def outer(place, xs, gs, scale, rows, top, count, flops=HIDE):
     cols = gs[0].shape[1]
     return pl.pallas_call(
         functools.partial(outer_kernel, scale, len(gs), count),
@@ -275,7 +275,7 @@
         compiler_params=pltpu.CompilerParams(
             vmem_limit_bytes=VMEM, dimension_semantics=("arbitrary",)
         ),
-        cost_estimate=pl.CostEstimate(flops=HIDE, bytes_accessed=12 << 20, transcendentals=0),
+        cost_estimate=pl.CostEstimate(flops=flops, bytes_accessed=12 << 20, transcendentals=0),
         name="outer",
     )(place, *xs, *gs)
 
@@ -310,7 +310,7 @@
     down1 = lax.ppermute(weight_down, "dp", beside)
     weight_in, payload = after((weight_in, payload))
     kept, given = halves(place, weight_in.swapaxes(0, 1))
-    given, kept, far_payload, down1, *near = after((given, kept, far_payload, down1, *near))
+    given, kept, far_payload = after((given, kept, far_payload))
     far = [far_payload] + spread(far_payload)
     w2 = lax.ppermute(given, "dp", across)
     w1 = lax.ppermute(kept, "dp", beside)
@@ -348,37 +348,38 @@
         )
 
     far_mid, far_gw = mids("far", far_sib, far_own)
-    far_ts, far_to = backs("far_tokens", far_gw)
-    far_got = lax.ppermute(far_ts, "expert", cores)
-    near_sib, far_to = after((near_sib, far_to))
+    near_sib, far_mid = after((near_sib, far_mid))
     near_mid, near_gw = mids("near", near_sib, near_own)
-    far_got, near_mid = after((far_got, near_mid))
-    far_sums = back_sums(far_to, far_got)
-    near_mid, *far_sums = after((near_mid, *far_sums))
-    far_back = back_hops(far_sums)
     tiles = (far_sib, far_own, near_sib, near_own)
     (g3,) = outer(place, tiles, (far_mid, near_mid), grad_scale, rows, 3, 1)
     got3 = lax.ppermute(g3, "dp", beside)
     near_gw, g3 = after((near_gw, g3))
     near_ts, near_to = backs("near_tokens", near_gw)
     near_got = lax.ppermute(near_ts, "expert", cores)
-    near_mid, near_to = after((near_mid, near_to))
+    far_gw, near_to = after((far_gw, near_to))
+    far_ts, far_to = backs("far_tokens", far_gw)
+    far_got = lax.ppermute(far_ts, "expert", cores)
+    near_mid, far_to = after((near_mid, far_to))
     g2, g1 = outer(place, tiles, (far_mid, near_mid), grad_scale, rows, 2, 2)
-    near_got, g1 = after((near_got, g1))
     got1 = lax.ppermute(g1, "dp", beside)
-    near_sums = back_sums(near_to, near_got)
-    near_mid, g1 = after((near_mid, g1))
-    (g0,) = outer(place, tiles, (far_mid, near_mid), grad_scale, rows, 0, 1)
-    got3, g0, *far_back = after((got3, g0, *far_back))
+    far_got, near_got, g2 = after((far_got, near_got, g2))
+    far_sums, near_sums = back_sums(far_to, far_got), back_sums(near_to, near_got)
+    got3, *near_sums = after((got3, *near_sums))
     relay = plus(g2, got3)
     away_half = lax.ppermute(relay, "dp", across)
+    near_mid, relay = after((near_mid, relay))
+    (g0,) = outer(place, tiles, (far_mid, near_mid), grad_scale, rows, 0, 1, HIDE)
+    g0, *far_sums = after((g0, *far_sums))
+    far_back = back_hops(far_sums)
+    away_half, got1, *far_back = after((away_half, got1, *far_back))
     away = sum(t.astype(jnp.float32) for t in far_back).astype(jnp.bfloat16)
+    away, *near_sums = after((away, *near_sums))
     home = lax.ppermute(away, "dp", across)
-    *near_sums, got1 = after((*near_sums, got1))
     near_back = back_hops(near_sums)
-    near_total = sum(t.astype(jnp.float32) for t in near_back)
-    token_grad = (near_total + home.astype(jnp.float32)).astype(jnp.bfloat16)
     grad_in = join(place, g0, got1, away_half).swapaxes(0, 1)
+    total = near_back[0].astype(jnp.float32) + home.astype(jnp.float32)
+    total, *near_back = after((total, *near_back[1:]))
+    token_grad = sum((t.astype(jnp.float32) for t in near_back), total).astype(jnp.bfloat16)
     return token_grad, grad_in
 
 

time: 128 us -> 124 us (0.969)
  the two profiles are of different devices: /device:TPU:0 before, /device:TPU:12 now
where the time goes in v3:
time: 124 us
  waiting for transfers between devices  56 us (45%)
  starting transfers between devices  39 us (31%)
  Pallas kernels  21.9 us (18%)
  local copies, waits for them, and re-layouts  4.21 us (3%)
  other arithmetic  2.24 us (2%)
    ppermute x1, waiting for transfers between devices, by_tokens(): down1 = lax.ppermute(weight_down, 'dp', beside)  15.5 us
    ppermute x1, waiting for transfers between devices, by_tokens(): w2 = lax.ppermute(given, 'dp', across)  13.4 us
    ppermute x6, starting transfers between devices, back_hops(): lax.ppermute(t, 'expert', hop)  13.1 us
    pallas_call x5, Pallas kernels, vmem_call(): pl.pallas_call(kernel, in_specs=specs, out_specs=[vmem] * len(outs), out_...  11.4 us
    ppermute x6, waiting for transfers between devices, back_hops(): lax.ppermute(t, 'expert', hop)  9.58 us
    ppermute x6, starting transfers between devices, spread(): return [lax.ppermute(x, 'expert', hop) for hop in hops]  6.98 us
    pallas_call x3, Pallas kernels, outer(): pl.pallas_call(functools.partial(outer_kernel, scale, len(gs), count), gr...  6.67 us
    ppermute x1, waiting for transfers between devices, by_tokens(): got1 = lax.ppermute(g1, 'dp', beside)  5.53 us
  transfers between devices with their start and end apart: 25, of which 15 were waited for; matrix products, arithmetic and copies ran while one was open for 4% of the time, Pallas kernels for 12%

profile of v3, /device:TPU:12, one launch (start us, length us, event | category | flops | bytes accessed | tf_op | source)
XLA Modules:
  0.0 124.2 jit_solution(822588603045857041)
XLA Ops:
  0.6 2.0 %payload.1 = bf16[128,2176]{1,0:T(8,128)(2,1)} custom-call(bf16[128,1024]{1,0:T(8,128)(2,1)} %tokens.1, bf16[128,1024]{1,0:T(8,128)(2,1)} %cotangent.1, s32[8,128]{1,0:T(8,128)} %bitcast.18, f32[8,128]{1,0:T(8,128)} %bitcast.19), custom_call_target="tpu_custom_call" | custom-call | flops 1048576 | bytes 2097152 | tf_op jit(solution)/shard_map/payload/pallas_call | solution.py:106
  2.7 2.6 %collective-permute-start = (bf16[128,2176]{1,0:T(8,128)(2,1)}, bf16[128,2176]{1,0:T(8,128)(2,1)}, u32[]{:S(2)}, u32[]{:S(2)}) collective-permute-start(bf16[128,2176]{1,0:T(8,128)(2,1)} %payload.1), channel_id=1, source_target_pairs={{0,16},{8,24},{16,0},{24,8},{1,17},{9,25},{17,1},{25,9},{2,18},{10... | collective-permute-start | bytes 1671176 | tf_op jit(solution)/shard_map/ppermute | solution.py:309
  5.3 1.4 %collective-permute-start.11 = (bf16[128,2176]{1,0:T(8,128)(2,1)}, bf16[128,2176]{1,0:T(8,128)(2,1)S(1)}, u32[]{:S(2)}, u32[]{:S(2)}) collective-permute-start(bf16[128,2176]{1,0:T(8,128)(2,1)} %payload.1), channel_id=1, source_target_pairs={{0,6},{1,7},{2,4},{3,5},{4,2},{5,3},{6,0},{7,1},{8,14},{9,15},{10,... | collective-permute-start | bytes 1671176 | tf_op jit(solution)/shard_map/ppermute | solution.py:301
  6.7 1.5 %collective-permute-start.10 = (bf16[128,2176]{1,0:T(8,128)(2,1)}, bf16[128,2176]{1,0:T(8,128)(2,1)S(1)}, u32[]{:S(2)}, u32[]{:S(2)}) collective-permute-start(bf16[128,2176]{1,0:T(8,128)(2,1)} %payload.1), channel_id=1, source_target_pairs={{0,4},{1,5},{2,6},{3,7},{4,0},{5,1},{6,2},{7,3},{8,12},{9,13},{10,... | collective-permute-start | bytes 1671176 | tf_op jit(solution)/shard_map/ppermute | solution.py:301
  8.2 0.5 collective-permute-start.9
  8.8 0.4 collective-permute-start.8
  9.2 1.1 copy.9
  10.5 0.8 halves.1
  11.3 15.5 %collective-permute-done.8 = bf16[96,2,1024]{2,1,0:T(2,128)(2,1)S(1)} collective-permute-done((bf16[96,2,1024]{2,1,0:T(2,128)(2,1)}, bf16[96,2,1024]{2,1,0:T(2,128)(2,1)S(1)}, u32[]{:S(2)}, u32[]{:S(2)}) %collective-permute-start.8) | collective-permute-done | bytes 393248 | tf_op jit(solution)/shard_map/ppermute | solution.py:310
  26.8 2.5 %collective-permute-done = bf16[128,2176]{1,0:T(8,128)(2,1)} collective-permute-done((bf16[128,2176]{1,0:T(8,128)(2,1)}, bf16[128,2176]{1,0:T(8,128)(2,1)}, u32[]{:S(2)}, u32[]{:S(2)}) %collective-permute-start) | collective-permute-done | bytes 557088 | tf_op jit(solution)/shard_map/ppermute | solution.py:309
  29.3 1.4 %collective-permute-start.5 = (bf16[128,2176]{1,0:T(8,128)(2,1)}, bf16[128,2176]{1,0:T(8,128)(2,1)S(1)}, u32[]{:S(2)}, u32[]{:S(2)}) collective-permute-start(bf16[128,2176]{1,0:T(8,128)(2,1)} %collective-permute-done), channel_id=1, source_target_pairs={{0,6},{1,7},{2,4},{3,5},{4,2},{5,3},{6,0},{7,1},{8,14},{9,15},{10,... | collective-permute-start | bytes 1671176 | tf_op jit(solution)/shard_map/ppermute | solution.py:301
  30.7 1.5 %collective-permute-start.4 = (bf16[128,2176]{1,0:T(8,128)(2,1)}, bf16[128,2176]{1,0:T(8,128)(2,1)S(1)}, u32[]{:S(2)}, u32[]{:S(2)}) collective-permute-start(bf16[128,2176]{1,0:T(8,128)(2,1)} %collective-permute-done), channel_id=1, source_target_pairs={{0,4},{1,5},{2,6},{3,7},{4,0},{5,1},{6,2},{7,3},{8,12},{9,13},{10,... | collective-permute-start | bytes 1671176 | tf_op jit(solution)/shard_map/ppermute | solution.py:301
  32.2 0.5 collective-permute-start.3
  32.8 3.4 %collective-permute-start.1 = (bf16[256,768]{1,0:T(8,128)(2,1)S(1)}, bf16[256,768]{1,0:T(8,128)(2,1)S(1)}, u32[]{:S(2)}, u32[]{:S(2)}) collective-permute-start(bf16[256,768]{1,0:T(8,128)(2,1)S(1)} %get-tuple-element.66), channel_id=1, source_target_pairs={{0,16},{8,24},{16,0},{24,8},{1,17},{9,25},{17,1},{25,9},{2,18},{10... | collective-permute-start | bytes 1179656 | tf_op jit(solution)/shard_map/ppermute | solution.py:315
  36.3 13.4 %collective-permute-done.1.w2 = bf16[256,768]{1,0:T(8,128)(2,1)S(1)} collective-permute-done((bf16[256,768]{1,0:T(8,128)(2,1)S(1)}, bf16[256,768]{1,0:T(8,128)(2,1)S(1)}, u32[]{:S(2)}, u32[]{:S(2)}) %collective-permute-start.1) | collective-permute-done | bytes 393248 | tf_op jit(solution)/shard_map/ppermute | solution.py:315
  49.8 1.0 collective-permute-done.2.w1
  50.8 2.6 %collective-permute-start.7 = (bf16[256,768]{1,0:T(8,128)(2,1)S(1)}, bf16[256,768]{1,0:T(8,128)(2,1)S(1)}, u32[]{:S(2)}, u32[]{:S(2)}) collective-permute-start(bf16[256,768]{1,0:T(8,128)(2,1)S(1)} %collective-permute-done.1.w2), channel_id=1, source_target_pairs={{0,8},{8,0},{16,24},{24,16},{1,9},{9,1},{17,25},{25,17},{2,10},{10... | collective-permute-start | bytes 1179656 | tf_op jit(solution)/shard_map/ppermute | solution.py:319
  53.4 1.1 constant_dynamic-update-slice_fusion.3
  54.5 1.5 %collective-permute-done.3 = bf16[128,2176]{1,0:T(8,128)(2,1)S(1)} collective-permute-done((bf16[128,2176]{1,0:T(8,128)(2,1)}, bf16[128,2176]{1,0:T(8,128)(2,1)S(1)}, u32[]{:S(2)}, u32[]{:S(2)}) %collective-permute-start.3) | collective-permute-done | bytes 557088 | tf_op jit(solution)/shard_map/ppermute | solution.py:301
  56.0 0.9 collective-permute-done.4
  57.1 4.1 %collective-permute-done.7.w3 = bf16[256,768]{1,0:T(8,128)(2,1)S(1)} collective-permute-done((bf16[256,768]{1,0:T(8,128)(2,1)S(1)}, bf16[256,768]{1,0:T(8,128)(2,1)S(1)}, u32[]{:S(2)}, u32[]{:S(2)}) %collective-permute-start.7) | collective-permute-done | bytes 393248 | tf_op jit(solution)/shard_map/ppermute | solution.py:319
  61.2 0.7 weights.1
  62.0 3.6 %far.1 = (bf16[1024,768]{1,0:T(8,128)(2,1)S(1)}, bf16[1024,768]{1,0:T(8,128)(2,1)S(1)}) custom-call(bf16[512,2176]{1,0:T(8,128)(2,1)S(1)} %collective-permute-done.6.xs.refs_0_, bf16[512,2176]{1,0:T(8,128)(2,1)S(1)} %constant_dynamic-update-slice_fusion.xo.refs_1_, bf16[1024,768]{1,0:T(8,128)(2,1)S(1)} %get-tuple-element.74.w_all, ...), custom_call_target="tpu_custom_call" | custom-call | flops 68719476736 | bytes 12582912 | tf_op jit(solution)/shard_map/far/pallas_call | solution.py:229
  65.6 0.7 collective-permute-done.12.xs.refs_2_
  66.3 3.5 %near.1 = (bf16[1024,768]{1,0:T(8,128)(2,1)S(1)}, bf16[1024,768]{1,0:T(8,128)(2,1)S(1)}) custom-call(bf16[512,2176]{1,0:T(8,128)(2,1)S(1)} %collective-permute-done.12.xs.refs_2_, bf16[512,2176]{1,0:T(8,128)(2,1)S(1)} %pad_maximum_fusion.xo.refs_3_, bf16[1024,768]{1,0:T(8,128)(2,1)S(1)} %get-tuple-element.74.w_all, ...), custom_call_target="tpu_custom_call" | custom-call | flops 68719476736 | bytes 12582912 | tf_op jit(solution)/shard_map/near/pallas_call | solution.py:229
  69.8 1.9 %outer.3 = bf16[256,768]{1,0:T(8,128)(2,1)S(1)} custom-call(s32[2]{0:T(128)S(1)} %pad_add_fusion.place, bf16[512,2176]{1,0:T(8,128)(2,1)S(1)} %collective-permute-done.6.xs.refs_0_, bf16[512,2176]{1,0:T(8,128)(2,1)S(1)} %constant_dynamic-update-slice_fusion.xo.refs_1_, bf16[512,2176]{1,0:T(8,128)(2,1)S(1)} %collective-permute-done.12.xs.refs_2_, ...), custom_call_target="tpu_custom_call" | custom-call | flops 68719476736 | bytes 12582912 | tf_op jit(solution)/shard_map/outer/pallas_call | solution.py:265
  71.7 1.8 %collective-permute-start.15 = (bf16[256,768]{1,0:T(8,128)(2,1)S(1)}, bf16[256,768]{1,0:T(8,128)(2,1)S(1)}, u32[]{:S(2)}, u32[]{:S(2)}) collective-permute-start(bf16[256,768]{1,0:T(8,128)(2,1)S(1)} %outer.3), channel_id=1, source_target_pairs={{0,8},{8,0},{16,24},{24,16},{1,9},{9,1},{17,25},{25,17},{2,10},{10... | collective-permute-start | bytes 1179656 | tf_op jit(solution)/shard_map/ppermute | solution.py:355
  73.5 1.8 %near_tokens.1 = (bf16[512,1024]{1,0:T(8,128)(2,1)S(1)}, bf16[512,1024]{1,0:T(8,128)(2,1)S(1)}) custom-call(bf16[1024,768]{1,0:T(8,128)(2,1)S(1)} %get-tuple-element.84.gw, bf16[1024,768]{1,0:T(8,128)(2,1)S(1)} %get-tuple-element.74.w_all), custom_call_target="tpu_custom_call" | custom-call | flops 1610612736 | bytes 12582912 | tf_op jit(solution)/shard_map/near_tokens/pallas_call | solution.py:229
  75.3 1.8 %far_tokens.1 = (bf16[512,1024]{1,0:T(8,128)(2,1)S(1)}, bf16[512,1024]{1,0:T(8,128)(2,1)S(1)}) custom-call(bf16[1024,768]{1,0:T(8,128)(2,1)S(1)} %get-tuple-element.86.gw, bf16[1024,768]{1,0:T(8,128)(2,1)S(1)} %get-tuple-element.74.w_all), custom_call_target="tpu_custom_call" | custom-call | flops 1610612736 | bytes 12582912 | tf_op jit(solution)/shard_map/far_tokens/pallas_call | solution.py:229
  77.2 0.5 collective-permute-start.14
  77.7 3.1 %outer.4 = (bf16[256,768]{1,0:T(8,128)(2,1)S(1)}, bf16[256,768]{1,0:T(8,128)(2,1)S(1)}) custom-call(s32[2]{0:T(128)S(1)} %pad_add_fusion.place, bf16[512,2176]{1,0:T(8,128)(2,1)S(1)} %collective-permute-done.6.xs.refs_0_, bf16[512,2176]{1,0:T(8,128)(2,1)S(1)} %constant_dynamic-update-slice_fusion.xo.refs_1_, ...), custom_call_target="tpu_custom_call" | custom-call | flops 68719476736 | bytes 12582912 | tf_op jit(solution)/shard_map/outer/pallas_call | solution.py:265
  81.4 0.4 add_convert_fusion.7
  81.8 1.1 collective-permute-done.15
  83.0 3.5 %collective-permute-start.16 = (bf16[256,768]{1,0:T(8,128)(2,1)S(1)}, bf16[256,768]{1,0:T(8,128)(2,1)S(1)}, u32[]{:S(2)}, u32[]{:S(2)}) collective-permute-start(bf16[256,768]{1,0:T(8,128)(2,1)S(1)} %add_convert_fusion), channel_id=1, source_target_pairs={{0,16},{8,24},{16,0},{24,8},{1,17},{9,25},{17,1},{25,9},{2,18},{10... | collective-permute-start | bytes 1179656 | tf_op jit(solution)/shard_map/ppermute | solution.py:369
  86.6 1.7 %outer.5.own = bf16[256,768]{1,0:T(8,128)(2,1)S(1)} custom-call(s32[2]{0:T(128)S(1)} %pad_add_fusion.place, bf16[512,2176]{1,0:T(8,128)(2,1)S(1)} %collective-permute-done.6.xs.refs_0_, bf16[512,2176]{1,0:T(8,128)(2,1)S(1)} %constant_dynamic-update-slice_fusion.xo.refs_1_, bf16[512,2176]{1,0:T(8,128)(2,1)S(1)} %collective-permute-done.12.xs.refs_2_, ...), custom_call_target="tpu_custom_call" | custom-call | flops 68719476736 | bytes 12582912 | tf_op jit(solution)/shard_map/outer/pallas_call | solution.py:265
  88.3 0.4 add_convert_fusion.3
  88.7 1.6 %collective-permute-start.18 = (bf16[128,1024]{1,0:T(8,128)(2,1)S(1)}, bf16[128,1024]{1,0:T(8,128)(2,1)S(1)}, u32[]{:S(2)}, u32[]{:S(2)}) collective-permute-start(bf16[128,1024]{1,0:T(8,128)(2,1)S(1)} %get-tuple-element.101), channel_id=1, source_target_pairs={{0,2},{1,3},{2,0},{3,1},{4,6},{5,7},{6,4},{7,5},{8,10},{9,11},{10,... | collective-permute-start | bytes 786440 | tf_op jit(solution)/shard_map/ppermute | solution.py:340
  90.3 0.4 collective-permute-start.19
  90.7 1.5 %collective-permute-start.20 = (bf16[128,1024]{1,0:T(8,128)(2,1)S(1)}, bf16[128,1024]{1,0:T(8,128)(2,1)S(1)}, u32[]{:S(2)}, u32[]{:S(2)}) collective-permute-start(bf16[128,1024]{1,0:T(8,128)(2,1)S(1)} %get-tuple-element.103), channel_id=1, source_target_pairs={{0,6},{1,7},{2,4},{3,5},{4,2},{5,3},{6,0},{7,1},{8,14},{9,15},{10,... | collective-permute-start | bytes 786440 | tf_op jit(solution)/shard_map/ppermute | solution.py:340
  92.2 5.5 %collective-permute-done.17.got = bf16[256,768]{1,0:T(8,128)(2,1)S(1)} collective-permute-done((bf16[256,768]{1,0:T(8,128)(2,1)S(1)}, bf16[256,768]{1,0:T(8,128)(2,1)S(1)}, u32[]{:S(2)}, u32[]{:S(2)}) %collective-permute-start.17) | collective-permute-done | bytes 393248 | tf_op jit(solution)/shard_map/ppermute | solution.py:364
  98.0 4.4 %collective-permute-done.19 = bf16[128,1024]{1,0:T(8,128)(2,1)S(1)} collective-permute-done((bf16[128,1024]{1,0:T(8,128)(2,1)S(1)}, bf16[128,1024]{1,0:T(8,128)(2,1)S(1)}, u32[]{:S(2)}, u32[]{:S(2)}) %collective-permute-start.19) | collective-permute-done | bytes 262176 | tf_op jit(solution)/shard_map/ppermute | solution.py:340
  102.6 3.4 %collective-permute-start.21 = (bf16[128,1024]{1,0:T(8,128)(2,1)S(1)}, bf16[128,1024]{1,0:T(8,128)(2,1)S(1)}, u32[]{:S(2)}, u32[]{:S(2)}) collective-permute-start(bf16[128,1024]{1,0:T(8,128)(2,1)S(1)} %add_convert_fusion.2), channel_id=1, source_target_pairs={{0,16},{8,24},{16,0},{24,8},{1,17},{9,25},{17,1},{25,9},{2,18},{10... | collective-permute-start | bytes 786440 | tf_op jit(solution)/shard_map/ppermute | solution.py:377
  106.0 8.1 %collective-permute-start.22 = (bf16[128,1024]{1,0:T(8,128)(2,1)S(1)}, bf16[128,1024]{1,0:T(8,128)(2,1)S(1)}, u32[]{:S(2)}, u32[]{:S(2)}) collective-permute-start(bf16[128,1024]{1,0:T(8,128)(2,1)S(1)} %get-tuple-element.114), channel_id=1, source_target_pairs={{0,2},{1,3},{2,0},{3,1},{4,6},{5,7},{6,4},{7,5},{8,10},{9,11},{10,... | collective-permute-start | bytes 786440 | tf_op jit(solution)/shard_map/ppermute | solution.py:340
  114.1 1.5 %collective-permute-start.24 = (bf16[128,1024]{1,0:T(8,128)(2,1)S(1)}, bf16[128,1024]{1,0:T(8,128)(2,1)S(1)}, u32[]{:S(2)}, u32[]{:S(2)}) collective-permute-start(bf16[128,1024]{1,0:T(8,128)(2,1)S(1)} %get-tuple-element.116), channel_id=1, source_target_pairs={{0,6},{1,7},{2,4},{3,5},{4,2},{5,3},{6,0},{7,1},{8,14},{9,15},{10,... | collective-permute-start | bytes 786440 | tf_op jit(solution)/shard_map/ppermute | solution.py:340
  115.6 1.0 join.1
  116.6 1.7 %copy.11 = bf16[256,2,768]{2,1,0:T(2,128)(2,1)} copy(bf16[256,2,768]{2,0,1:T(8,128)(2,1)S(1)} %bitcast.13) | data formatting | bytes 1572864
  118.5 4.8 %collective-permute-done.23 = bf16[128,1024]{1,0:T(8,128)(2,1)S(1)} collective-permute-done((bf16[128,1024]{1,0:T(8,128)(2,1)S(1)}, bf16[128,1024]{1,0:T(8,128)(2,1)S(1)}, u32[]{:S(2)}, u32[]{:S(2)}) %collective-permute-start.23) | collective-permute-done | bytes 262176 | tf_op jit(solution)/shard_map/ppermute | solution.py:340
  123.3 0.9 add_convert_fusion.1
  (33 shorter events, 2.0 us)
Async XLA Ops:
  0.6 9.7 %copy-start.1 = (bf16[256,2,768]{2,1,0:T(2,128)(2,1)S(1)}, bf16[256,2,768]{2,1,0:T(2,128)(2,1)}, u32[]{:S(2)}) copy-start(bf16[256,2,768]{2,1,0:T(2,128)(2,1)} %param.10) | copy-start | bytes 2359300
  2.7 33.5 %copy-start = (bf16[128,2176]{1,0:T(8,128)(2,1)S(1)}, bf16[128,2176]{1,0:T(8,128)(2,1)}, u32[]{:S(2)}) copy-start(bf16[128,2176]{1,0:T(8,128)(2,1)} %payload.1) | copy-start | bytes 1671172
  2.7 26.6 %collective-permute-start = (bf16[128,2176]{1,0:T(8,128)(2,1)}, bf16[128,2176]{1,0:T(8,128)(2,1)}, u32[]{:S(2)}, u32[]{:S(2)}) collective-permute-start(bf16[128,2176]{1,0:T(8,128)(2,1)} %payload.1), channel_id=1, source_target_pairs={{0,16},{8,24},{16,0},{24,8},{1,17},{9,25},{17,1},{25,9},{2,18},{10... | collective-permute-start | bytes 1671176 | tf_op jit(solution)/shard_map/ppermute | solution.py:309
  5.3 27.0 %collective-permute-start.11 = (bf16[128,2176]{1,0:T(8,128)(2,1)}, bf16[128,2176]{1,0:T(8,128)(2,1)S(1)}, u32[]{:S(2)}, u32[]{:S(2)}) collective-permute-start(bf16[128,2176]{1,0:T(8,128)(2,1)} %payload.1), channel_id=1, source_target_pairs={{0,6},{1,7},{2,4},{3,5},{4,2},{5,3},{6,0},{7,1},{8,14},{9,15},{10,... | collective-permute-start | bytes 1671176 | tf_op jit(solution)/shard_map/ppermute | solution.py:301
  6.7 26.1 %collective-permute-start.10 = (bf16[128,2176]{1,0:T(8,128)(2,1)}, bf16[128,2176]{1,0:T(8,128)(2,1)S(1)}, u32[]{:S(2)}, u32[]{:S(2)}) collective-permute-start(bf16[128,2176]{1,0:T(8,128)(2,1)} %payload.1), channel_id=1, source_target_pairs={{0,4},{1,5},{2,6},{3,7},{4,0},{5,1},{6,2},{7,3},{8,12},{9,13},{10,... | collective-permute-start | bytes 1671176 | tf_op jit(solution)/shard_map/ppermute | solution.py:301
  8.2 28.0 %collective-permute-start.9 = (bf16[128,2176]{1,0:T(8,128)(2,1)}, bf16[128,2176]{1,0:T(8,128)(2,1)S(1)}, u32[]{:S(2)}, u32[]{:S(2)}) collective-permute-start(bf16[128,2176]{1,0:T(8,128)(2,1)} %payload.1), channel_id=1, source_target_pairs={{0,2},{1,3},{2,0},{3,1},{4,6},{5,7},{6,4},{7,5},{8,10},{9,11},{10,... | collective-permute-start | bytes 1671176 | tf_op jit(solution)/shard_map/ppermute | solution.py:301
  8.8 18.0 %collective-permute-start.8 = (bf16[96,2,1024]{2,1,0:T(2,128)(2,1)}, bf16[96,2,1024]{2,1,0:T(2,128)(2,1)S(1)}, u32[]{:S(2)}, u32[]{:S(2)}) collective-permute-start(bf16[96,2,1024]{2,1,0:T(2,128)(2,1)} %param.11), channel_id=1, source_target_pairs={{0,8},{8,0},{16,24},{24,16},{1,9},{9,1},{17,25},{25,17},{2,10},{10... | collective-permute-start | bytes 1179656 | tf_op jit(solution)/shard_map/ppermute | solution.py:310
  29.3 27.7 %collective-permute-start.5 = (bf16[128,2176]{1,0:T(8,128)(2,1)}, bf16[128,2176]{1,0:T(8,128)(2,1)S(1)}, u32[]{:S(2)}, u32[]{:S(2)}) collective-permute-start(bf16[128,2176]{1,0:T(8,128)(2,1)} %collective-permute-done), channel_id=1, source_target_pairs={{0,6},{1,7},{2,4},{3,5},{4,2},{5,3},{6,0},{7,1},{8,14},{9,15},{10,... | collective-permute-start | bytes 1671176 | tf_op jit(solution)/shard_map/ppermute | solution.py:301
  30.7 26.2 %collective-permute-start.4 = (bf16[128,2176]{1,0:T(8,128)(2,1)}, bf16[128,2176]{1,0:T(8,128)(2,1)S(1)}, u32[]{:S(2)}, u32[]{:S(2)}) collective-permute-start(bf16[128,2176]{1,0:T(8,128)(2,1)} %collective-permute-done), channel_id=1, source_target_pairs={{0,4},{1,5},{2,6},{3,7},{4,0},{5,1},{6,2},{7,3},{8,12},{9,13},{10,... | collective-permute-start | bytes 1671176 | tf_op jit(solution)/shard_map/ppermute | solution.py:301
  32.2 23.7 %collective-permute-start.3 = (bf16[128,2176]{1,0:T(8,128)(2,1)}, bf16[128,2176]{1,0:T(8,128)(2,1)S(1)}, u32[]{:S(2)}, u32[]{:S(2)}) collective-permute-start(bf16[128,2176]{1,0:T(8,128)(2,1)} %collective-permute-done), channel_id=1, source_target_pairs={{0,2},{1,3},{2,0},{3,1},{4,6},{5,7},{6,4},{7,5},{8,10},{9,11},{10,... | collective-permute-start | bytes 1671176 | tf_op jit(solution)/shard_map/ppermute | solution.py:301
  32.8 17.0 %collective-permute-start.1 = (bf16[256,768]{1,0:T(8,128)(2,1)S(1)}, bf16[256,768]{1,0:T(8,128)(2,1)S(1)}, u32[]{:S(2)}, u32[]{:S(2)}) collective-permute-start(bf16[256,768]{1,0:T(8,128)(2,1)S(1)} %get-tuple-element.66), channel_id=1, source_target_pairs={{0,16},{8,24},{16,0},{24,8},{1,17},{9,25},{17,1},{25,9},{2,18},{10... | collective-permute-start | bytes 1179656 | tf_op jit(solution)/shard_map/ppermute | solution.py:315
  36.2 14.6 %collective-permute-start.2 = (bf16[256,768]{1,0:T(8,128)(2,1)S(1)}, bf16[256,768]{1,0:T(8,128)(2,1)S(1)}, u32[]{:S(2)}, u32[]{:S(2)}) collective-permute-start(bf16[256,768]{1,0:T(8,128)(2,1)S(1)} %get-tuple-element.67.w0), channel_id=1, source_target_pairs={{0,8},{8,0},{16,24},{24,16},{1,9},{9,1},{17,25},{25,17},{2,10},{10... | collective-permute-start | bytes 1179656 | tf_op jit(solution)/shard_map/ppermute | solution.py:316
  50.8 10.4 %collective-permute-start.7 = (bf16[256,768]{1,0:T(8,128)(2,1)S(1)}, bf16[256,768]{1,0:T(8,128)(2,1)S(1)}, u32[]{:S(2)}, u32[]{:S(2)}) collective-permute-start(bf16[256,768]{1,0:T(8,128)(2,1)S(1)} %collective-permute-done.1.w2), channel_id=1, source_target_pairs={{0,8},{8,0},{16,24},{24,16},{1,9},{9,1},{17,25},{25,17},{2,10},{10... | collective-permute-start | bytes 1179656 | tf_op jit(solution)/shard_map/ppermute | solution.py:319
  57.0 4.9 %collective-permute-start.6 = (bf16[512,2176]{1,0:T(8,128)(2,1)S(1)}, bf16[512,2176]{1,0:T(8,128)(2,1)S(1)}, u32[]{:S(2)}, u32[]{:S(2)}) collective-permute-start(bf16[512,2176]{1,0:T(8,128)(2,1)S(1)} %constant_dynamic-update-slice_fusion.xo.refs_1_), channel_id=1, source_target_pairs={{0,1},{1,0},{2,3},{3,2},{4,5},{5,4},{6,7},{7,6},{8,9},{9,8},{10,11... | collective-permute-start | bytes 6684680 | tf_op jit(solution)/shard_map/ppermute | solution.py:321
  61.9 4.4 %collective-permute-start.12 = (bf16[512,2176]{1,0:T(8,128)(2,1)S(1)}, bf16[512,2176]{1,0:T(8,128)(2,1)S(1)}, u32[]{:S(2)}, u32[]{:S(2)}) collective-permute-start(bf16[512,2176]{1,0:T(8,128)(2,1)S(1)} %pad_maximum_fusion.xo.refs_3_), channel_id=1, source_target_pairs={{0,1},{1,0},{2,3},{3,2},{4,5},{5,4},{6,7},{7,6},{8,9},{9,8},{10,11... | collective-permute-start | bytes 6684680 | tf_op jit(solution)/shard_map/ppermute | solution.py:334
  71.7 11.2 %collective-permute-start.15 = (bf16[256,768]{1,0:T(8,128)(2,1)S(1)}, bf16[256,768]{1,0:T(8,128)(2,1)S(1)}, u32[]{:S(2)}, u32[]{:S(2)}) collective-permute-start(bf16[256,768]{1,0:T(8,128)(2,1)S(1)} %outer.3), channel_id=1, source_target_pairs={{0,8},{8,0},{16,24},{24,16},{1,9},{9,1},{17,25},{25,17},{2,10},{10... | collective-permute-start | bytes 1179656 | tf_op jit(solution)/shard_map/ppermute | solution.py:355
  77.2 4.0 %collective-permute-start.13 = (bf16[512,1024]{1,0:T(8,128)(2,1)S(1)}, bf16[512,1024]{1,0:T(8,128)(2,1)S(1)}, u32[]{:S(2)}, u32[]{:S(2)}) collective-permute-start(bf16[512,1024]{1,0:T(8,128)(2,1)S(1)} %get-tuple-element.87), channel_id=1, source_target_pairs={{0,1},{1,0},{2,3},{3,2},{4,5},{5,4},{6,7},{7,6},{8,9},{9,8},{10,11... | collective-permute-start | bytes 3145736 | tf_op jit(solution)/shard_map/ppermute | solution.py:361
  77.2 4.1 %collective-permute-start.14 = (bf16[512,1024]{1,0:T(8,128)(2,1)S(1)}, bf16[512,1024]{1,0:T(8,128)(2,1)S(1)}, u32[]{:S(2)}, u32[]{:S(2)}) collective-permute-start(bf16[512,1024]{1,0:T(8,128)(2,1)S(1)} %get-tuple-element.88), channel_id=1, source_target_pairs={{0,1},{1,0},{2,3},{3,2},{4,5},{5,4},{6,7},{7,6},{8,9},{9,8},{10,11... | collective-permute-start | bytes 3145736 | tf_op jit(solution)/shard_map/ppermute | solution.py:358
  80.8 16.9 %collective-permute-start.17 = (bf16[256,768]{1,0:T(8,128)(2,1)S(1)}, bf16[256,768]{1,0:T(8,128)(2,1)S(1)}, u32[]{:S(2)}, u32[]{:S(2)}) collective-permute-start(bf16[256,768]{1,0:T(8,128)(2,1)S(1)} %get-tuple-element.96), channel_id=1, source_target_pairs={{0,8},{8,0},{16,24},{24,16},{1,9},{9,1},{17,25},{25,17},{2,10},{10... | collective-permute-start | bytes 1179656 | tf_op jit(solution)/shard_map/ppermute | solution.py:364
  83.0 19.4 %collective-permute-start.16 = (bf16[256,768]{1,0:T(8,128)(2,1)S(1)}, bf16[256,768]{1,0:T(8,128)(2,1)S(1)}, u32[]{:S(2)}, u32[]{:S(2)}) collective-permute-start(bf16[256,768]{1,0:T(8,128)(2,1)S(1)} %add_convert_fusion), channel_id=1, source_target_pairs={{0,16},{8,24},{16,0},{24,8},{1,17},{9,25},{17,1},{25,9},{2,18},{10... | collective-permute-start | bytes 1179656 | tf_op jit(solution)/shard_map/ppermute | solution.py:369
  88.7 9.3 %collective-permute-start.18 = (bf16[128,1024]{1,0:T(8,128)(2,1)S(1)}, bf16[128,1024]{1,0:T(8,128)(2,1)S(1)}, u32[]{:S(2)}, u32[]{:S(2)}) collective-permute-start(bf16[128,1024]{1,0:T(8,128)(2,1)S(1)} %get-tuple-element.101), channel_id=1, source_target_pairs={{0,2},{1,3},{2,0},{3,1},{4,6},{5,7},{6,4},{7,5},{8,10},{9,11},{10,... | collective-permute-start | bytes 786440 | tf_op jit(solution)/shard_map/ppermute | solution.py:340
  90.3 12.1 %collective-permute-start.19 = (bf16[128,1024]{1,0:T(8,128)(2,1)S(1)}, bf16[128,1024]{1,0:T(8,128)(2,1)S(1)}, u32[]{:S(2)}, u32[]{:S(2)}) collective-permute-start(bf16[128,1024]{1,0:T(8,128)(2,1)S(1)} %get-tuple-element.102), channel_id=1, source_target_pairs={{0,4},{1,5},{2,6},{3,7},{4,0},{5,1},{6,2},{7,3},{8,12},{9,13},{10,... | collective-permute-start | bytes 786440 | tf_op jit(solution)/shard_map/ppermute | solution.py:340
  90.7 11.6 %collective-permute-start.20 = (bf16[128,1024]{1,0:T(8,128)(2,1)S(1)}, bf16[128,1024]{1,0:T(8,128)(2,1)S(1)}, u32[]{:S(2)}, u32[]{:S(2)}) collective-permute-start(bf16[128,1024]{1,0:T(8,128)(2,1)S(1)} %get-tuple-element.103), channel_id=1, source_target_pairs={{0,6},{1,7},{2,4},{3,5},{4,2},{5,3},{6,0},{7,1},{8,14},{9,15},{10,... | collective-permute-start | bytes 786440 | tf_op jit(solution)/shard_map/ppermute | solution.py:340
  102.6 15.7 %collective-permute-start.21 = (bf16[128,1024]{1,0:T(8,128)(2,1)S(1)}, bf16[128,1024]{1,0:T(8,128)(2,1)S(1)}, u32[]{:S(2)}, u32[]{:S(2)}) collective-permute-start(bf16[128,1024]{1,0:T(8,128)(2,1)S(1)} %add_convert_fusion.2), channel_id=1, source_target_pairs={{0,16},{8,24},{16,0},{24,8},{1,17},{9,25},{17,1},{25,9},{2,18},{10... | collective-permute-start | bytes 786440 | tf_op jit(solution)/shard_map/ppermute | solution.py:377
  106.0 12.5 %collective-permute-start.22 = (bf16[128,1024]{1,0:T(8,128)(2,1)S(1)}, bf16[128,1024]{1,0:T(8,128)(2,1)S(1)}, u32[]{:S(2)}, u32[]{:S(2)}) collective-permute-start(bf16[128,1024]{1,0:T(8,128)(2,1)S(1)} %get-tuple-element.114), channel_id=1, source_target_pairs={{0,2},{1,3},{2,0},{3,1},{4,6},{5,7},{6,4},{7,5},{8,10},{9,11},{10,... | collective-permute-start | bytes 786440 | tf_op jit(solution)/shard_map/ppermute | solution.py:340
  114.1 9.2 %collective-permute-start.23 = (bf16[128,1024]{1,0:T(8,128)(2,1)S(1)}, bf16[128,1024]{1,0:T(8,128)(2,1)S(1)}, u32[]{:S(2)}, u32[]{:S(2)}) collective-permute-start(bf16[128,1024]{1,0:T(8,128)(2,1)S(1)} %get-tuple-element.115), channel_id=1, source_target_pairs={{0,4},{1,5},{2,6},{3,7},{4,0},{5,1},{6,2},{7,3},{8,12},{9,13},{10,... | collective-permute-start | bytes 786440 | tf_op jit(solution)/shard_map/ppermute | solution.py:340
  114.1 9.2 %collective-permute-start.24 = (bf16[128,1024]{1,0:T(8,128)(2,1)S(1)}, bf16[128,1024]{1,0:T(8,128)(2,1)S(1)}, u32[]{:S(2)}, u32[]{:S(2)}) collective-permute-start(bf16[128,1024]{1,0:T(8,128)(2,1)S(1)} %get-tuple-element.116), channel_id=1, source_target_pairs={{0,6},{1,7},{2,4},{3,5},{4,2},{5,3},{6,0},{7,1},{8,14},{9,15},{10,... | collective-permute-start | bytes 786440 | tf_op jit(solution)/shard_map/ppermute | solution.py:340

commit v4 on v3

--- a/solution.py
+++ b/solution.py
@@ -377,9 +377,9 @@
     home = lax.ppermute(away, "dp", across)
     near_back = back_hops(near_sums)
     grad_in = join(place, g0, got1, away_half).swapaxes(0, 1)
-    total = near_back[0].astype(jnp.float32) + home.astype(jnp.float32)
-    total, *near_back = after((total, *near_back[1:]))
-    token_grad = sum((t.astype(jnp.float32) for t in near_back), total).astype(jnp.bfloat16)
+    near_total = sum(t.astype(jnp.float32) for t in near_back)
+    near_total, home = after((near_total, home))
+    token_grad = (near_total + home.astype(jnp.float32)).astype(jnp.bfloat16)
     return token_grad, grad_in
 
 

time: 124 us -> 120 us (0.968)
  the two profiles are of different devices: /device:TPU:12 before, /device:TPU:0 now
where the time goes in v4:
time: 120 us
  waiting for transfers between devices  63.2 us (53%)
  starting transfers between devices  27.8 us (23%)
  Pallas kernels  21.9 us (18%)
  local copies, waits for them, and re-layouts  4.21 us (4%)
  other arithmetic  2.25 us (2%)
    ppermute x1, waiting for transfers between devices, by_tokens(): w2 = lax.ppermute(given, 'dp', across)  15 us
    ppermute x1, waiting for transfers between devices, by_tokens(): down1 = lax.ppermute(weight_down, 'dp', beside)  13.5 us
    pallas_call x5, Pallas kernels, vmem_call(): pl.pallas_call(kernel, in_specs=specs, out_specs=[vmem] * len(outs), out_...  11.4 us
    ppermute x1, waiting for transfers between devices, by_tokens(): got1 = lax.ppermute(g1, 'dp', beside)  8.02 us
    ppermute x6, waiting for transfers between devices, back_hops(): lax.ppermute(t, 'expert', hop)  7.62 us
    ppermute x6, starting transfers between devices, back_hops(): lax.ppermute(t, 'expert', hop)  7.11 us
    ppermute x6, starting transfers between devices, spread(): return [lax.ppermute(x, 'expert', hop) for hop in hops]  6.98 us
    pallas_call x3, Pallas kernels, outer(): pl.pallas_call(functools.partial(outer_kernel, scale, len(gs), count), gr...  6.67 us
  transfers between devices with their start and end apart: 25, of which 15 were waited for; matrix products, arithmetic and copies ran while one was open for 5% of the time, Pallas kernels for 12%

profile of v4, /device:TPU:0, one launch (start us, length us, event | category | flops | bytes accessed | tf_op | source)
XLA Modules:
  0.0 120.1 jit_solution(5421558601095460382)
XLA Ops:
  0.6 2.0 %payload.1 = bf16[128,2176]{1,0:T(8,128)(2,1)} custom-call(bf16[128,1024]{1,0:T(8,128)(2,1)} %tokens.1, bf16[128,1024]{1,0:T(8,128)(2,1)} %cotangent.1, s32[8,128]{1,0:T(8,128)} %bitcast.18, f32[8,128]{1,0:T(8,128)} %bitcast.19), custom_call_target="tpu_custom_call" | custom-call | flops 1048576 | bytes 2097152 | tf_op jit(solution)/shard_map/payload/pallas_call | solution.py:106
  2.7 4.0 %collective-permute-start = (bf16[128,2176]{1,0:T(8,128)(2,1)}, bf16[128,2176]{1,0:T(8,128)(2,1)}, u32[]{:S(2)}, u32[]{:S(2)}) collective-permute-start(bf16[128,2176]{1,0:T(8,128)(2,1)} %payload.1), channel_id=1, source_target_pairs={{0,16},{8,24},{16,0},{24,8},{1,17},{9,25},{17,1},{25,9},{2,18},{10... | collective-permute-start | bytes 1671176 | tf_op jit(solution)/shard_map/ppermute | solution.py:309
  6.7 2.4 %collective-permute-start.11 = (bf16[128,2176]{1,0:T(8,128)(2,1)}, bf16[128,2176]{1,0:T(8,128)(2,1)S(1)}, u32[]{:S(2)}, u32[]{:S(2)}) collective-permute-start(bf16[128,2176]{1,0:T(8,128)(2,1)} %payload.1), channel_id=1, source_target_pairs={{0,6},{1,7},{2,4},{3,5},{4,2},{5,3},{6,0},{7,1},{8,14},{9,15},{10,... | collective-permute-start | bytes 1671176 | tf_op jit(solution)/shard_map/ppermute | solution.py:301
  9.2 0.5 collective-permute-start.10
  9.7 0.5 collective-permute-start.9
  10.2 1.6 %collective-permute-start.8 = (bf16[96,2,1024]{2,1,0:T(2,128)(2,1)}, bf16[96,2,1024]{2,1,0:T(2,128)(2,1)S(1)}, u32[]{:S(2)}, u32[]{:S(2)}) collective-permute-start(bf16[96,2,1024]{2,1,0:T(2,128)(2,1)} %param.11), channel_id=1, source_target_pairs={{0,8},{8,0},{16,24},{24,16},{1,9},{9,1},{17,25},{25,17},{2,10},{10... | collective-permute-start | bytes 1179656 | tf_op jit(solution)/shard_map/ppermute | solution.py:310
  11.8 1.1 copy.9
  13.1 0.8 halves.1
  13.8 13.5 %collective-permute-done.8 = bf16[96,2,1024]{2,1,0:T(2,128)(2,1)S(1)} collective-permute-done((bf16[96,2,1024]{2,1,0:T(2,128)(2,1)}, bf16[96,2,1024]{2,1,0:T(2,128)(2,1)S(1)}, u32[]{:S(2)}, u32[]{:S(2)}) %collective-permute-start.8) | collective-permute-done | bytes 393248 | tf_op jit(solution)/shard_map/ppermute | solution.py:310
  27.5 4.2 %collective-permute-done = bf16[128,2176]{1,0:T(8,128)(2,1)} collective-permute-done((bf16[128,2176]{1,0:T(8,128)(2,1)}, bf16[128,2176]{1,0:T(8,128)(2,1)}, u32[]{:S(2)}, u32[]{:S(2)}) %collective-permute-start) | collective-permute-done | bytes 557088 | tf_op jit(solution)/shard_map/ppermute | solution.py:309
  31.7 2.4 %collective-permute-start.5 = (bf16[128,2176]{1,0:T(8,128)(2,1)}, bf16[128,2176]{1,0:T(8,128)(2,1)S(1)}, u32[]{:S(2)}, u32[]{:S(2)}) collective-permute-start(bf16[128,2176]{1,0:T(8,128)(2,1)} %collective-permute-done), channel_id=1, source_target_pairs={{0,6},{1,7},{2,4},{3,5},{4,2},{5,3},{6,0},{7,1},{8,14},{9,15},{10,... | collective-permute-start | bytes 1671176 | tf_op jit(solution)/shard_map/ppermute | solution.py:301
  34.1 0.5 collective-permute-start.4
  34.6 0.5 collective-permute-start.3
  35.2 4.0 %collective-permute-start.2 = (bf16[256,768]{1,0:T(8,128)(2,1)S(1)}, bf16[256,768]{1,0:T(8,128)(2,1)S(1)}, u32[]{:S(2)}, u32[]{:S(2)}) collective-permute-start(bf16[256,768]{1,0:T(8,128)(2,1)S(1)} %get-tuple-element.65.w0), channel_id=1, source_target_pairs={{0,8},{8,0},{16,24},{24,16},{1,9},{9,1},{17,25},{25,17},{2,10},{10... | collective-permute-start | bytes 1179656 | tf_op jit(solution)/shard_map/ppermute | solution.py:316
  39.4 15.0 %collective-permute-done.1.w2 = bf16[256,768]{1,0:T(8,128)(2,1)S(1)} collective-permute-done((bf16[256,768]{1,0:T(8,128)(2,1)S(1)}, bf16[256,768]{1,0:T(8,128)(2,1)S(1)}, u32[]{:S(2)}, u32[]{:S(2)}) %collective-permute-start.1) | collective-permute-done | bytes 393248 | tf_op jit(solution)/shard_map/ppermute | solution.py:315
  54.4 1.1 constant_dynamic-update-slice_fusion.3
  55.5 2.8 %collective-permute-done.3 = bf16[128,2176]{1,0:T(8,128)(2,1)S(1)} collective-permute-done((bf16[128,2176]{1,0:T(8,128)(2,1)}, bf16[128,2176]{1,0:T(8,128)(2,1)S(1)}, u32[]{:S(2)}, u32[]{:S(2)}) %collective-permute-start.3) | collective-permute-done | bytes 557088 | tf_op jit(solution)/shard_map/ppermute | solution.py:301
  58.7 5.2 %collective-permute-done.7.w3 = bf16[256,768]{1,0:T(8,128)(2,1)S(1)} collective-permute-done((bf16[256,768]{1,0:T(8,128)(2,1)S(1)}, bf16[256,768]{1,0:T(8,128)(2,1)S(1)}, u32[]{:S(2)}, u32[]{:S(2)}) %collective-permute-start.7) | collective-permute-done | bytes 393248 | tf_op jit(solution)/shard_map/ppermute | solution.py:319
  63.9 0.7 weights.1
  64.7 3.6 %far.1 = (bf16[1024,768]{1,0:T(8,128)(2,1)S(1)}, bf16[1024,768]{1,0:T(8,128)(2,1)S(1)}) custom-call(bf16[512,2176]{1,0:T(8,128)(2,1)S(1)} %collective-permute-done.6.xs.refs_0_, bf16[512,2176]{1,0:T(8,128)(2,1)S(1)} %constant_dynamic-update-slice_fusion.xo.refs_1_, bf16[1024,768]{1,0:T(8,128)(2,1)S(1)} %get-tuple-element.72.w_all, ...), custom_call_target="tpu_custom_call" | custom-call | flops 68719476736 | bytes 12582912 | tf_op jit(solution)/shard_map/far/pallas_call | solution.py:229
  68.4 0.7 collective-permute-done.12.xs.refs_2_
  69.1 3.5 %near.1 = (bf16[1024,768]{1,0:T(8,128)(2,1)S(1)}, bf16[1024,768]{1,0:T(8,128)(2,1)S(1)}) custom-call(bf16[512,2176]{1,0:T(8,128)(2,1)S(1)} %collective-permute-done.12.xs.refs_2_, bf16[512,2176]{1,0:T(8,128)(2,1)S(1)} %pad_maximum_fusion.xo.refs_3_, bf16[1024,768]{1,0:T(8,128)(2,1)S(1)} %get-tuple-element.72.w_all, ...), custom_call_target="tpu_custom_call" | custom-call | flops 68719476736 | bytes 12582912 | tf_op jit(solution)/shard_map/near/pallas_call | solution.py:229
  72.5 1.9 %outer.3 = bf16[256,768]{1,0:T(8,128)(2,1)S(1)} custom-call(s32[2]{0:T(128)S(1)} %pad_add_fusion.place, bf16[512,2176]{1,0:T(8,128)(2,1)S(1)} %collective-permute-done.6.xs.refs_0_, bf16[512,2176]{1,0:T(8,128)(2,1)S(1)} %constant_dynamic-update-slice_fusion.xo.refs_1_, bf16[512,2176]{1,0:T(8,128)(2,1)S(1)} %collective-permute-done.12.xs.refs_2_, ...), custom_call_target="tpu_custom_call" | custom-call | flops 68719476736 | bytes 12582912 | tf_op jit(solution)/shard_map/outer/pallas_call | solution.py:265
  74.8 1.8 %near_tokens.1 = (bf16[512,1024]{1,0:T(8,128)(2,1)S(1)}, bf16[512,1024]{1,0:T(8,128)(2,1)S(1)}) custom-call(bf16[1024,768]{1,0:T(8,128)(2,1)S(1)} %get-tuple-element.82.gw, bf16[1024,768]{1,0:T(8,128)(2,1)S(1)} %get-tuple-element.72.w_all), custom_call_target="tpu_custom_call" | custom-call | flops 1610612736 | bytes 12582912 | tf_op jit(solution)/shard_map/near_tokens/pallas_call | solution.py:229
  76.6 1.8 %far_tokens.1 = (bf16[512,1024]{1,0:T(8,128)(2,1)S(1)}, bf16[512,1024]{1,0:T(8,128)(2,1)S(1)}) custom-call(bf16[1024,768]{1,0:T(8,128)(2,1)S(1)} %get-tuple-element.84.gw, bf16[1024,768]{1,0:T(8,128)(2,1)S(1)} %get-tuple-element.72.w_all), custom_call_target="tpu_custom_call" | custom-call | flops 1610612736 | bytes 12582912 | tf_op jit(solution)/shard_map/far_tokens/pallas_call | solution.py:229
  78.5 0.5 collective-permute-start.14
  79.0 3.1 %outer.4 = (bf16[256,768]{1,0:T(8,128)(2,1)S(1)}, bf16[256,768]{1,0:T(8,128)(2,1)S(1)}) custom-call(s32[2]{0:T(128)S(1)} %pad_add_fusion.place, bf16[512,2176]{1,0:T(8,128)(2,1)S(1)} %collective-permute-done.6.xs.refs_0_, bf16[512,2176]{1,0:T(8,128)(2,1)S(1)} %constant_dynamic-update-slice_fusion.xo.refs_1_, ...), custom_call_target="tpu_custom_call" | custom-call | flops 68719476736 | bytes 12582912 | tf_op jit(solution)/shard_map/outer/pallas_call | solution.py:265
  82.1 1.8 %collective-permute-start.17 = (bf16[256,768]{1,0:T(8,128)(2,1)S(1)}, bf16[256,768]{1,0:T(8,128)(2,1)S(1)}, u32[]{:S(2)}, u32[]{:S(2)}) collective-permute-start(bf16[256,768]{1,0:T(8,128)(2,1)S(1)} %get-tuple-element.94), channel_id=1, source_target_pairs={{0,8},{8,0},{16,24},{24,16},{1,9},{9,1},{17,25},{25,17},{2,10},{10... | collective-permute-start | bytes 1179656 | tf_op jit(solution)/shard_map/ppermute | solution.py:364
  83.9 0.4 add_convert_fusion.7
  84.4 2.0 %collective-permute-done.15 = bf16[256,768]{1,0:T(8,128)(2,1)S(1)} collective-permute-done((bf16[256,768]{1,0:T(8,128)(2,1)S(1)}, bf16[256,768]{1,0:T(8,128)(2,1)S(1)}, u32[]{:S(2)}, u32[]{:S(2)}) %collective-permute-start.15) | collective-permute-done | bytes 393248 | tf_op jit(solution)/shard_map/ppermute | solution.py:355
  86.5 1.1 collective-permute-start.16
  87.6 1.7 %outer.5.own = bf16[256,768]{1,0:T(8,128)(2,1)S(1)} custom-call(s32[2]{0:T(128)S(1)} %pad_add_fusion.place, bf16[512,2176]{1,0:T(8,128)(2,1)S(1)} %collective-permute-done.6.xs.refs_0_, bf16[512,2176]{1,0:T(8,128)(2,1)S(1)} %constant_dynamic-update-slice_fusion.xo.refs_1_, bf16[512,2176]{1,0:T(8,128)(2,1)S(1)} %collective-permute-done.12.xs.refs_2_, ...), custom_call_target="tpu_custom_call" | custom-call | flops 68719476736 | bytes 12582912 | tf_op jit(solution)/shard_map/outer/pallas_call | solution.py:265
  89.3 0.4 add_convert_fusion.3
  89.7 1.6 %collective-permute-start.18 = (bf16[128,1024]{1,0:T(8,128)(2,1)S(1)}, bf16[128,1024]{1,0:T(8,128)(2,1)S(1)}, u32[]{:S(2)}, u32[]{:S(2)}) collective-permute-start(bf16[128,1024]{1,0:T(8,128)(2,1)S(1)} %get-tuple-element.99), channel_id=1, source_target_pairs={{0,2},{1,3},{2,0},{3,1},{4,6},{5,7},{6,4},{7,5},{8,10},{9,11},{10,... | collective-permute-start | bytes 786440 | tf_op jit(solution)/shard_map/ppermute | solution.py:340
  91.3 1.5 %collective-permute-start.19 = (bf16[128,1024]{1,0:T(8,128)(2,1)S(1)}, bf16[128,1024]{1,0:T(8,128)(2,1)S(1)}, u32[]{:S(2)}, u32[]{:S(2)}) collective-permute-start(bf16[128,1024]{1,0:T(8,128)(2,1)S(1)} %get-tuple-element.100), channel_id=1, source_target_pairs={{0,4},{1,5},{2,6},{3,7},{4,0},{5,1},{6,2},{7,3},{8,12},{9,13},{10,... | collective-permute-start | bytes 786440 | tf_op jit(solution)/shard_map/ppermute | solution.py:340
  92.8 0.5 collective-permute-start.20
  93.3 8.0 %collective-permute-done.17.got = bf16[256,768]{1,0:T(8,128)(2,1)S(1)} collective-permute-done((bf16[256,768]{1,0:T(8,128)(2,1)S(1)}, bf16[256,768]{1,0:T(8,128)(2,1)S(1)}, u32[]{:S(2)}, u32[]{:S(2)}) %collective-permute-start.17) | collective-permute-done | bytes 393248 | tf_op jit(solution)/shard_map/ppermute | solution.py:364
  101.3 2.6 %collective-permute-done.19 = bf16[128,1024]{1,0:T(8,128)(2,1)S(1)} collective-permute-done((bf16[128,1024]{1,0:T(8,128)(2,1)S(1)}, bf16[128,1024]{1,0:T(8,128)(2,1)S(1)}, u32[]{:S(2)}, u32[]{:S(2)}) %collective-permute-start.19) | collective-permute-done | bytes 262176 | tf_op jit(solution)/shard_map/ppermute | solution.py:340
  103.9 1.7 %collective-permute-done.16.far = bf16[256,768]{1,0:T(8,128)(2,1)S(1)} collective-permute-done((bf16[256,768]{1,0:T(8,128)(2,1)S(1)}, bf16[256,768]{1,0:T(8,128)(2,1)S(1)}, u32[]{:S(2)}, u32[]{:S(2)}) %collective-permute-start.16) | collective-permute-done | bytes 393248 | tf_op jit(solution)/shard_map/ppermute | solution.py:369
  105.7 1.6 %collective-permute-start.21 = (bf16[128,1024]{1,0:T(8,128)(2,1)S(1)}, bf16[128,1024]{1,0:T(8,128)(2,1)S(1)}, u32[]{:S(2)}, u32[]{:S(2)}) collective-permute-start(bf16[128,1024]{1,0:T(8,128)(2,1)S(1)} %get-tuple-element.111), channel_id=1, source_target_pairs={{0,2},{1,3},{2,0},{3,1},{4,6},{5,7},{6,4},{7,5},{8,10},{9,11},{10,... | collective-permute-start | bytes 786440 | tf_op jit(solution)/shard_map/ppermute | solution.py:340
  107.3 0.7 collective-permute-start.22
  107.9 1.3 %collective-permute-start.23 = (bf16[128,1024]{1,0:T(8,128)(2,1)S(1)}, bf16[128,1024]{1,0:T(8,128)(2,1)S(1)}, u32[]{:S(2)}, u32[]{:S(2)}) collective-permute-start(bf16[128,1024]{1,0:T(8,128)(2,1)S(1)} %get-tuple-element.113), channel_id=1, source_target_pairs={{0,6},{1,7},{2,4},{3,5},{4,2},{5,3},{6,0},{7,1},{8,14},{9,15},{10,... | collective-permute-start | bytes 786440 | tf_op jit(solution)/shard_map/ppermute | solution.py:340
  109.2 1.0 join.1
  110.2 1.7 %copy.11 = bf16[256,2,768]{2,1,0:T(2,128)(2,1)} copy(bf16[256,2,768]{2,0,1:T(8,128)(2,1)S(1)} %bitcast.13) | data formatting | bytes 1572864
  111.9 1.1 collective-permute-done.21
  113.1 3.9 %collective-permute-done.22 = bf16[128,1024]{1,0:T(8,128)(2,1)S(1)} collective-permute-done((bf16[128,1024]{1,0:T(8,128)(2,1)S(1)}, bf16[128,1024]{1,0:T(8,128)(2,1)S(1)}, u32[]{:S(2)}, u32[]{:S(2)}) %collective-permute-start.22) | collective-permute-done | bytes 262176 | tf_op jit(solution)/shard_map/ppermute | solution.py:340
  117.2 2.2 %collective-permute-done.24 = bf16[128,1024]{1,0:T(8,128)(2,1)S(1)} collective-permute-done((bf16[128,1024]{1,0:T(8,128)(2,1)S(1)}, bf16[128,1024]{1,0:T(8,128)(2,1)S(1)}, u32[]{:S(2)}, u32[]{:S(2)}) %collective-permute-start.24) | collective-permute-done | bytes 262176 | tf_op jit(solution)/shard_map/ppermute | solution.py:377
  119.4 0.8 add_convert_fusion.1
  (33 shorter events, 1.8 us)
Async XLA Ops:
  0.6 12.3 %copy-start.1 = (bf16[256,2,768]{2,1,0:T(2,128)(2,1)S(1)}, bf16[256,2,768]{2,1,0:T(2,128)(2,1)}, u32[]{:S(2)}) copy-start(bf16[256,2,768]{2,1,0:T(2,128)(2,1)} %param.10) | copy-start | bytes 2359300
  2.7 36.5 %copy-start = (bf16[128,2176]{1,0:T(8,128)(2,1)S(1)}, bf16[128,2176]{1,0:T(8,128)(2,1)}, u32[]{:S(2)}) copy-start(bf16[128,2176]{1,0:T(8,128)(2,1)} %payload.1) | copy-start | bytes 1671172
  2.7 29.0 %collective-permute-start = (bf16[128,2176]{1,0:T(8,128)(2,1)}, bf16[128,2176]{1,0:T(8,128)(2,1)}, u32[]{:S(2)}, u32[]{:S(2)}) collective-permute-start(bf16[128,2176]{1,0:T(8,128)(2,1)} %payload.1), channel_id=1, source_target_pairs={{0,16},{8,24},{16,0},{24,8},{1,17},{9,25},{17,1},{25,9},{2,18},{10... | collective-permute-start | bytes 1671176 | tf_op jit(solution)/shard_map/ppermute | solution.py:309
  6.7 27.9 %collective-permute-start.11 = (bf16[128,2176]{1,0:T(8,128)(2,1)}, bf16[128,2176]{1,0:T(8,128)(2,1)S(1)}, u32[]{:S(2)}, u32[]{:S(2)}) collective-permute-start(bf16[128,2176]{1,0:T(8,128)(2,1)} %payload.1), channel_id=1, source_target_pairs={{0,6},{1,7},{2,4},{3,5},{4,2},{5,3},{6,0},{7,1},{8,14},{9,15},{10,... | collective-permute-start | bytes 1671176 | tf_op jit(solution)/shard_map/ppermute | solution.py:301
  9.2 26.0 %collective-permute-start.10 = (bf16[128,2176]{1,0:T(8,128)(2,1)}, bf16[128,2176]{1,0:T(8,128)(2,1)S(1)}, u32[]{:S(2)}, u32[]{:S(2)}) collective-permute-start(bf16[128,2176]{1,0:T(8,128)(2,1)} %payload.1), channel_id=1, source_target_pairs={{0,4},{1,5},{2,6},{3,7},{4,0},{5,1},{6,2},{7,3},{8,12},{9,13},{10,... | collective-permute-start | bytes 1671176 | tf_op jit(solution)/shard_map/ppermute | solution.py:301
  9.7 25.5 %collective-permute-start.9 = (bf16[128,2176]{1,0:T(8,128)(2,1)}, bf16[128,2176]{1,0:T(8,128)(2,1)S(1)}, u32[]{:S(2)}, u32[]{:S(2)}) collective-permute-start(bf16[128,2176]{1,0:T(8,128)(2,1)} %payload.1), channel_id=1, source_target_pairs={{0,2},{1,3},{2,0},{3,1},{4,6},{5,7},{6,4},{7,5},{8,10},{9,11},{10,... | collective-permute-start | bytes 1671176 | tf_op jit(solution)/shard_map/ppermute | solution.py:301
  10.2 17.2 %collective-permute-start.8 = (bf16[96,2,1024]{2,1,0:T(2,128)(2,1)}, bf16[96,2,1024]{2,1,0:T(2,128)(2,1)S(1)}, u32[]{:S(2)}, u32[]{:S(2)}) collective-permute-start(bf16[96,2,1024]{2,1,0:T(2,128)(2,1)} %param.11), channel_id=1, source_target_pairs={{0,8},{8,0},{16,24},{24,16},{1,9},{9,1},{17,25},{25,17},{2,10},{10... | collective-permute-start | bytes 1179656 | tf_op jit(solution)/shard_map/ppermute | solution.py:310
  31.7 26.9 %collective-permute-start.5 = (bf16[128,2176]{1,0:T(8,128)(2,1)}, bf16[128,2176]{1,0:T(8,128)(2,1)S(1)}, u32[]{:S(2)}, u32[]{:S(2)}) collective-permute-start(bf16[128,2176]{1,0:T(8,128)(2,1)} %collective-permute-done), channel_id=1, source_target_pairs={{0,6},{1,7},{2,4},{3,5},{4,2},{5,3},{6,0},{7,1},{8,14},{9,15},{10,... | collective-permute-start | bytes 1671176 | tf_op jit(solution)/shard_map/ppermute | solution.py:301
  34.1 24.4 %collective-permute-start.4 = (bf16[128,2176]{1,0:T(8,128)(2,1)}, bf16[128,2176]{1,0:T(8,128)(2,1)S(1)}, u32[]{:S(2)}, u32[]{:S(2)}) collective-permute-start(bf16[128,2176]{1,0:T(8,128)(2,1)} %collective-permute-done), channel_id=1, source_target_pairs={{0,4},{1,5},{2,6},{3,7},{4,0},{5,1},{6,2},{7,3},{8,12},{9,13},{10,... | collective-permute-start | bytes 1671176 | tf_op jit(solution)/shard_map/ppermute | solution.py:301
  34.6 23.7 %collective-permute-start.3 = (bf16[128,2176]{1,0:T(8,128)(2,1)}, bf16[128,2176]{1,0:T(8,128)(2,1)S(1)}, u32[]{:S(2)}, u32[]{:S(2)}) collective-permute-start(bf16[128,2176]{1,0:T(8,128)(2,1)} %collective-permute-done), channel_id=1, source_target_pairs={{0,2},{1,3},{2,0},{3,1},{4,6},{5,7},{6,4},{7,5},{8,10},{9,11},{10,... | collective-permute-start | bytes 1671176 | tf_op jit(solution)/shard_map/ppermute | solution.py:301
  35.2 19.2 %collective-permute-start.1 = (bf16[256,768]{1,0:T(8,128)(2,1)S(1)}, bf16[256,768]{1,0:T(8,128)(2,1)S(1)}, u32[]{:S(2)}, u32[]{:S(2)}) collective-permute-start(bf16[256,768]{1,0:T(8,128)(2,1)S(1)} %get-tuple-element.64), channel_id=1, source_target_pairs={{0,16},{8,24},{16,0},{24,8},{1,17},{9,25},{17,1},{25,9},{2,18},{10... | collective-permute-start | bytes 1179656 | tf_op jit(solution)/shard_map/ppermute | solution.py:315
  35.2 19.2 %collective-permute-start.2 = (bf16[256,768]{1,0:T(8,128)(2,1)S(1)}, bf16[256,768]{1,0:T(8,128)(2,1)S(1)}, u32[]{:S(2)}, u32[]{:S(2)}) collective-permute-start(bf16[256,768]{1,0:T(8,128)(2,1)S(1)} %get-tuple-element.65.w0), channel_id=1, source_target_pairs={{0,8},{8,0},{16,24},{24,16},{1,9},{9,1},{17,25},{25,17},{2,10},{10... | collective-permute-start | bytes 1179656 | tf_op jit(solution)/shard_map/ppermute | solution.py:316
  54.4 9.5 %collective-permute-start.7 = (bf16[256,768]{1,0:T(8,128)(2,1)S(1)}, bf16[256,768]{1,0:T(8,128)(2,1)S(1)}, u32[]{:S(2)}, u32[]{:S(2)}) collective-permute-start(bf16[256,768]{1,0:T(8,128)(2,1)S(1)} %collective-permute-done.1.w2), channel_id=1, source_target_pairs={{0,8},{8,0},{16,24},{24,16},{1,9},{9,1},{17,25},{25,17},{2,10},{10... | collective-permute-start | bytes 1179656 | tf_op jit(solution)/shard_map/ppermute | solution.py:319
  58.6 6.0 %collective-permute-start.6 = (bf16[512,2176]{1,0:T(8,128)(2,1)S(1)}, bf16[512,2176]{1,0:T(8,128)(2,1)S(1)}, u32[]{:S(2)}, u32[]{:S(2)}) collective-permute-start(bf16[512,2176]{1,0:T(8,128)(2,1)S(1)} %constant_dynamic-update-slice_fusion.xo.refs_1_), channel_id=1, source_target_pairs={{0,1},{1,0},{2,3},{3,2},{4,5},{5,4},{6,7},{7,6},{8,9},{9,8},{10,11... | collective-permute-start | bytes 6684680 | tf_op jit(solution)/shard_map/ppermute | solution.py:321
  64.7 4.4 %collective-permute-start.12 = (bf16[512,2176]{1,0:T(8,128)(2,1)S(1)}, bf16[512,2176]{1,0:T(8,128)(2,1)S(1)}, u32[]{:S(2)}, u32[]{:S(2)}) collective-permute-start(bf16[512,2176]{1,0:T(8,128)(2,1)S(1)} %pad_maximum_fusion.xo.refs_3_), channel_id=1, source_target_pairs={{0,1},{1,0},{2,3},{3,2},{4,5},{5,4},{6,7},{7,6},{8,9},{9,8},{10,11... | collective-permute-start | bytes 6684680 | tf_op jit(solution)/shard_map/ppermute | solution.py:334
  74.4 11.9 %collective-permute-start.15 = (bf16[256,768]{1,0:T(8,128)(2,1)S(1)}, bf16[256,768]{1,0:T(8,128)(2,1)S(1)}, u32[]{:S(2)}, u32[]{:S(2)}) collective-permute-start(bf16[256,768]{1,0:T(8,128)(2,1)S(1)} %outer.3), channel_id=1, source_target_pairs={{0,8},{8,0},{16,24},{24,16},{1,9},{9,1},{17,25},{25,17},{2,10},{10... | collective-permute-start | bytes 1179656 | tf_op jit(solution)/shard_map/ppermute | solution.py:355
  78.4 5.5 %collective-permute-start.13 = (bf16[512,1024]{1,0:T(8,128)(2,1)S(1)}, bf16[512,1024]{1,0:T(8,128)(2,1)S(1)}, u32[]{:S(2)}, u32[]{:S(2)}) collective-permute-start(bf16[512,1024]{1,0:T(8,128)(2,1)S(1)} %get-tuple-element.85), channel_id=1, source_target_pairs={{0,1},{1,0},{2,3},{3,2},{4,5},{5,4},{6,7},{7,6},{8,9},{9,8},{10,11... | collective-permute-start | bytes 3145736 | tf_op jit(solution)/shard_map/ppermute | solution.py:361
  78.5 5.4 %collective-permute-start.14 = (bf16[512,1024]{1,0:T(8,128)(2,1)S(1)}, bf16[512,1024]{1,0:T(8,128)(2,1)S(1)}, u32[]{:S(2)}, u32[]{:S(2)}) collective-permute-start(bf16[512,1024]{1,0:T(8,128)(2,1)S(1)} %get-tuple-element.86), channel_id=1, source_target_pairs={{0,1},{1,0},{2,3},{3,2},{4,5},{5,4},{6,7},{7,6},{8,9},{9,8},{10,11... | collective-permute-start | bytes 3145736 | tf_op jit(solution)/shard_map/ppermute | solution.py:358
  82.1 19.2 %collective-permute-start.17 = (bf16[256,768]{1,0:T(8,128)(2,1)S(1)}, bf16[256,768]{1,0:T(8,128)(2,1)S(1)}, u32[]{:S(2)}, u32[]{:S(2)}) collective-permute-start(bf16[256,768]{1,0:T(8,128)(2,1)S(1)} %get-tuple-element.94), channel_id=1, source_target_pairs={{0,8},{8,0},{16,24},{24,16},{1,9},{9,1},{17,25},{25,17},{2,10},{10... | collective-permute-start | bytes 1179656 | tf_op jit(solution)/shard_map/ppermute | solution.py:364
  86.5 19.0 %collective-permute-start.16 = (bf16[256,768]{1,0:T(8,128)(2,1)S(1)}, bf16[256,768]{1,0:T(8,128)(2,1)S(1)}, u32[]{:S(2)}, u32[]{:S(2)}) collective-permute-start(bf16[256,768]{1,0:T(8,128)(2,1)S(1)} %add_convert_fusion), channel_id=1, source_target_pairs={{0,16},{8,24},{16,0},{24,8},{1,17},{9,25},{17,1},{25,9},{2,18},{10... | collective-permute-start | bytes 1179656 | tf_op jit(solution)/shard_map/ppermute | solution.py:369
  89.7 11.6 %collective-permute-start.18 = (bf16[128,1024]{1,0:T(8,128)(2,1)S(1)}, bf16[128,1024]{1,0:T(8,128)(2,1)S(1)}, u32[]{:S(2)}, u32[]{:S(2)}) collective-permute-start(bf16[128,1024]{1,0:T(8,128)(2,1)S(1)} %get-tuple-element.99), channel_id=1, source_target_pairs={{0,2},{1,3},{2,0},{3,1},{4,6},{5,7},{6,4},{7,5},{8,10},{9,11},{10,... | collective-permute-start | bytes 786440 | tf_op jit(solution)/shard_map/ppermute | solution.py:340
  91.3 12.6 %collective-permute-start.19 = (bf16[128,1024]{1,0:T(8,128)(2,1)S(1)}, bf16[128,1024]{1,0:T(8,128)(2,1)S(1)}, u32[]{:S(2)}, u32[]{:S(2)}) collective-permute-start(bf16[128,1024]{1,0:T(8,128)(2,1)S(1)} %get-tuple-element.100), channel_id=1, source_target_pairs={{0,4},{1,5},{2,6},{3,7},{4,0},{5,1},{6,2},{7,3},{8,12},{9,13},{10,... | collective-permute-start | bytes 786440 | tf_op jit(solution)/shard_map/ppermute | solution.py:340
  92.8 11.1 %collective-permute-start.20 = (bf16[128,1024]{1,0:T(8,128)(2,1)S(1)}, bf16[128,1024]{1,0:T(8,128)(2,1)S(1)}, u32[]{:S(2)}, u32[]{:S(2)}) collective-permute-start(bf16[128,1024]{1,0:T(8,128)(2,1)S(1)} %get-tuple-element.101), channel_id=1, source_target_pairs={{0,6},{1,7},{2,4},{3,5},{4,2},{5,3},{6,0},{7,1},{8,14},{9,15},{10,... | collective-permute-start | bytes 786440 | tf_op jit(solution)/shard_map/ppermute | solution.py:340
  105.7 7.4 %collective-permute-start.21 = (bf16[128,1024]{1,0:T(8,128)(2,1)S(1)}, bf16[128,1024]{1,0:T(8,128)(2,1)S(1)}, u32[]{:S(2)}, u32[]{:S(2)}) collective-permute-start(bf16[128,1024]{1,0:T(8,128)(2,1)S(1)} %get-tuple-element.111), channel_id=1, source_target_pairs={{0,2},{1,3},{2,0},{3,1},{4,6},{5,7},{6,4},{7,5},{8,10},{9,11},{10,... | collective-permute-start | bytes 786440 | tf_op jit(solution)/shard_map/ppermute | solution.py:340
  107.3 9.7 %collective-permute-start.22 = (bf16[128,1024]{1,0:T(8,128)(2,1)S(1)}, bf16[128,1024]{1,0:T(8,128)(2,1)S(1)}, u32[]{:S(2)}, u32[]{:S(2)}) collective-permute-start(bf16[128,1024]{1,0:T(8,128)(2,1)S(1)} %get-tuple-element.112), channel_id=1, source_target_pairs={{0,4},{1,5},{2,6},{3,7},{4,0},{5,1},{6,2},{7,3},{8,12},{9,13},{10,... | collective-permute-start | bytes 786440 | tf_op jit(solution)/shard_map/ppermute | solution.py:340
  107.9 9.1 %collective-permute-start.23 = (bf16[128,1024]{1,0:T(8,128)(2,1)S(1)}, bf16[128,1024]{1,0:T(8,128)(2,1)S(1)}, u32[]{:S(2)}, u32[]{:S(2)}) collective-permute-start(bf16[128,1024]{1,0:T(8,128)(2,1)S(1)} %get-tuple-element.113), channel_id=1, source_target_pairs={{0,6},{1,7},{2,4},{3,5},{4,2},{5,3},{6,0},{7,1},{8,14},{9,15},{10,... | collective-permute-start | bytes 786440 | tf_op jit(solution)/shard_map/ppermute | solution.py:340
  109.2 10.1 %collective-permute-start.24 = (bf16[128,1024]{1,0:T(8,128)(2,1)S(1)}, bf16[128,1024]{1,0:T(8,128)(2,1)S(1)}, u32[]{:S(2)}, u32[]{:S(2)}) collective-permute-start(bf16[128,1024]{1,0:T(8,128)(2,1)S(1)} %add_convert_fusion.2), channel_id=1, source_target_pairs={{0,16},{8,24},{16,0},{24,8},{1,17},{9,25},{17,1},{25,9},{2,18},{10... | collective-permute-start | bytes 786440 | tf_op jit(solution)/shard_map/ppermute | solution.py:377

commit v5 on v4

--- a/solution.py
+++ b/solution.py
@@ -342,10 +342,8 @@
     def mids(name, sib, own):
         return vmem_call(grad_mid, name, [mid_shape, mid_shape], sib, own, w_all, d_all, pick)
 
-    def backs(name, gw):
-        return vmem_call(
-            token_kernel, name, [token_shape] * 2, gw, w_all, flops=4 * tall * cols * width
-        )
+    def backs(name, gw, flops):
+        return vmem_call(token_kernel, name, [token_shape] * 2, gw, w_all, flops=flops)
 
     far_mid, far_gw = mids("far", far_sib, far_own)
     near_sib, far_mid = after((near_sib, far_mid))
@@ -353,25 +351,25 @@
     tiles = (far_sib, far_own, near_sib, near_own)
     (g3,) = outer(place, tiles, (far_mid, near_mid), grad_scale, rows, 3, 1)
     got3 = lax.ppermute(g3, "dp", beside)
-    near_gw, g3 = after((near_gw, g3))
-    near_ts, near_to = backs("near_tokens", near_gw)
-    near_got = lax.ppermute(near_ts, "expert", cores)
-    far_gw, near_to = after((far_gw, near_to))
-    far_ts, far_to = backs("far_tokens", far_gw)
+    far_gw, g3 = after((far_gw, g3))
+    far_ts, far_to = backs("far_tokens", far_gw, 1 << 20)
     far_got = lax.ppermute(far_ts, "expert", cores)
     near_mid, far_to = after((near_mid, far_to))
     g2, g1 = outer(place, tiles, (far_mid, near_mid), grad_scale, rows, 2, 2)
     got1 = lax.ppermute(g1, "dp", beside)
-    far_got, near_got, g2 = after((far_got, near_got, g2))
-    far_sums, near_sums = back_sums(far_to, far_got), back_sums(near_to, near_got)
-    got3, *near_sums = after((got3, *near_sums))
+    far_got, g2 = after((far_got, g2))
+    far_sums = back_sums(far_to, far_got)
+    far_back = back_hops(far_sums)
+    got3, *far_sums = after((got3, *far_sums))
     relay = plus(g2, got3)
     away_half = lax.ppermute(relay, "dp", across)
-    near_mid, relay = after((near_mid, relay))
-    (g0,) = outer(place, tiles, (far_mid, near_mid), grad_scale, rows, 0, 1, HIDE)
-    g0, *far_sums = after((g0, *far_sums))
-    far_back = back_hops(far_sums)
-    away_half, got1, *far_back = after((away_half, got1, *far_back))
+    near_gw, relay = after((near_gw, relay))
+    near_ts, near_to = backs("near_tokens", near_gw, HIDE)
+    near_got = lax.ppermute(near_ts, "expert", cores)
+    near_mid, near_to, *far_back = after((near_mid, near_to, *far_back))
+    (g0,) = outer(place, tiles, (far_mid, near_mid), grad_scale, rows, 0, 1)
+    near_got, g0 = after((near_got, g0))
+    near_sums = back_sums(near_to, near_got)
     away = sum(t.astype(jnp.float32) for t in far_back).astype(jnp.bfloat16)
     away, *near_sums = after((away, *near_sums))
     home = lax.ppermute(away, "dp", across)

time: 120 us -> 118 us (0.983)
  waiting for transfers between devices: 63.2 us -> 58.9 us
  starting transfers between devices: 27.8 us -> 29.3 us
    ppermute x1, waiting for transfers between devices: 8.02 us -> 0.01 us  [by_tokens(): got1 = lax.ppermute(g1, 'dp', beside)]
    ppermute x1, waiting for transfers between devices: 1.65 us -> 6.56 us  [by_tokens(): away_half = lax.ppermute(relay, 'dp', across)]
    ppermute x1, starting transfers between devices: 0.01 us -> 1.58 us  [by_tokens(): home = lax.ppermute(away, 'dp', across)]
  transfers between devices with their start and end apart: 25 -> 25, of which waited for: 15 -> 12; matrix products, arithmetic and copies ran while one was open for 5% -> 5% of each run, Pallas kernels for 12% -> 12%
where the time goes in v5:
time: 118 us
  waiting for transfers between devices  58.9 us (50%)
  starting transfers between devices  29.3 us (25%)
  Pallas kernels  21.9 us (19%)
  local copies, waits for them, and re-layouts  4.26 us (4%)
  other arithmetic  2.37 us (2%)
    ppermute x1, waiting for transfers between devices, by_tokens(): w2 = lax.ppermute(given, 'dp', across)  15.1 us
    ppermute x1, waiting for transfers between devices, by_tokens(): down1 = lax.ppermute(weight_down, 'dp', beside)  13.4 us
    pallas_call x5, Pallas kernels, vmem_call(): pl.pallas_call(kernel, in_specs=specs, out_specs=[vmem] * len(outs), out_...  11.4 us
    ppermute x6, waiting for transfers between devices, back_hops(): lax.ppermute(t, 'expert', hop)  7.33 us
    ppermute x6, starting transfers between devices, back_hops(): lax.ppermute(t, 'expert', hop)  7.11 us
    ppermute x6, starting transfers between devices, spread(): return [lax.ppermute(x, 'expert', hop) for hop in hops]  6.98 us
    pallas_call x3, Pallas kernels, outer(): pl.pallas_call(functools.partial(outer_kernel, scale, len(gs), count), gr...  6.69 us
    ppermute x1, waiting for transfers between devices, by_tokens(): away_half = lax.ppermute(relay, 'dp', across)  6.56 us
  transfers between devices with their start and end apart: 25, of which 12 were waited for; matrix products, arithmetic and copies ran while one was open for 5% of the time, Pallas kernels for 12%

profile of v5, /device:TPU:0, one launch (start us, length us, event | category | flops | bytes accessed | tf_op | source)
XLA Modules:
  0.0 117.6 jit_solution(12472733311104829629)
XLA Ops:
  0.6 2.0 %payload.1 = bf16[128,2176]{1,0:T(8,128)(2,1)} custom-call(bf16[128,1024]{1,0:T(8,128)(2,1)} %tokens.1, bf16[128,1024]{1,0:T(8,128)(2,1)} %cotangent.1, s32[8,128]{1,0:T(8,128)} %bitcast.17, f32[8,128]{1,0:T(8,128)} %bitcast.18), custom_call_target="tpu_custom_call" | custom-call | flops 1048576 | bytes 2097152 | tf_op jit(solution)/shard_map/payload/pallas_call | solution.py:106
  2.7 4.0 %collective-permute-start = (bf16[128,2176]{1,0:T(8,128)(2,1)}, bf16[128,2176]{1,0:T(8,128)(2,1)S(1)}, u32[]{:S(2)}, u32[]{:S(2)}) collective-permute-start(bf16[128,2176]{1,0:T(8,128)(2,1)} %payload.1), channel_id=1, source_target_pairs={{0,16},{8,24},{16,0},{24,8},{1,17},{9,25},{17,1},{25,9},{2,18},{10... | collective-permute-start | bytes 1671176 | tf_op jit(solution)/shard_map/ppermute | solution.py:309
  6.7 2.4 %collective-permute-start.11 = (bf16[128,2176]{1,0:T(8,128)(2,1)}, bf16[128,2176]{1,0:T(8,128)(2,1)S(1)}, u32[]{:S(2)}, u32[]{:S(2)}) collective-permute-start(bf16[128,2176]{1,0:T(8,128)(2,1)} %payload.1), channel_id=1, source_target_pairs={{0,6},{1,7},{2,4},{3,5},{4,2},{5,3},{6,0},{7,1},{8,14},{9,15},{10,... | collective-permute-start | bytes 1671176 | tf_op jit(solution)/shard_map/ppermute | solution.py:301
  9.1 0.5 collective-permute-start.10
  9.6 0.5 collective-permute-start.9
  10.2 1.6 %collective-permute-start.8 = (bf16[96,2,1024]{2,1,0:T(2,128)(2,1)}, bf16[96,2,1024]{2,1,0:T(2,128)(2,1)}, u32[]{:S(2)}, u32[]{:S(2)}) collective-permute-start(bf16[96,2,1024]{2,1,0:T(2,128)(2,1)} %param.11), channel_id=1, source_target_pairs={{0,8},{8,0},{16,24},{24,16},{1,9},{9,1},{17,25},{25,17},{2,10},{10... | collective-permute-start | bytes 1179656 | tf_op jit(solution)/shard_map/ppermute | solution.py:310
  11.8 1.2 %copy.13 = bf16[256,2,768]{2,0,1:T(8,128)(2,1)S(1)} copy(bf16[256,2,768]{2,1,0:T(2,128)(2,1)} %param.10) | data formatting | bytes 1572864 | tf_op jit(solution)/shard_map/optimization_barrier | solution.py:311
  13.1 0.8 halves.1
  13.9 13.4 %collective-permute-done.8 = bf16[96,2,1024]{2,1,0:T(2,128)(2,1)} collective-permute-done((bf16[96,2,1024]{2,1,0:T(2,128)(2,1)}, bf16[96,2,1024]{2,1,0:T(2,128)(2,1)}, u32[]{:S(2)}, u32[]{:S(2)}) %collective-permute-start.8) | collective-permute-done | bytes 393248 | tf_op jit(solution)/shard_map/ppermute | solution.py:310
  27.4 1.1 copy.10
  28.4 3.1 %collective-permute-done = bf16[128,2176]{1,0:T(8,128)(2,1)S(1)} collective-permute-done((bf16[128,2176]{1,0:T(8,128)(2,1)}, bf16[128,2176]{1,0:T(8,128)(2,1)S(1)}, u32[]{:S(2)}, u32[]{:S(2)}) %collective-permute-start) | collective-permute-done | bytes 557088 | tf_op jit(solution)/shard_map/ppermute | solution.py:309
  31.5 1.5 %collective-permute-start.3 = (bf16[128,2176]{1,0:T(8,128)(2,1)S(1)}, bf16[128,2176]{1,0:T(8,128)(2,1)S(1)}, u32[]{:S(2)}, u32[]{:S(2)}) collective-permute-start(bf16[128,2176]{1,0:T(8,128)(2,1)S(1)} %collective-permute-done), channel_id=1, source_target_pairs={{0,2},{1,3},{2,0},{3,1},{4,6},{5,7},{6,4},{7,5},{8,10},{9,11},{10,... | collective-permute-start | bytes 1671176 | tf_op jit(solution)/shard_map/ppermute | solution.py:301
  33.0 1.5 %collective-permute-start.4 = (bf16[128,2176]{1,0:T(8,128)(2,1)S(1)}, bf16[128,2176]{1,0:T(8,128)(2,1)S(1)}, u32[]{:S(2)}, u32[]{:S(2)}) collective-permute-start(bf16[128,2176]{1,0:T(8,128)(2,1)S(1)} %collective-permute-done), channel_id=1, source_target_pairs={{0,4},{1,5},{2,6},{3,7},{4,0},{5,1},{6,2},{7,3},{8,12},{9,13},{10,... | collective-permute-start | bytes 1671176 | tf_op jit(solution)/shard_map/ppermute | solution.py:301
  34.5 0.5 collective-permute-start.5
  35.0 4.0 %collective-permute-start.2 = (bf16[256,768]{1,0:T(8,128)(2,1)S(1)}, bf16[256,768]{1,0:T(8,128)(2,1)S(1)}, u32[]{:S(2)}, u32[]{:S(2)}) collective-permute-start(bf16[256,768]{1,0:T(8,128)(2,1)S(1)} %get-tuple-element.55.w0), channel_id=1, source_target_pairs={{0,8},{8,0},{16,24},{24,16},{1,9},{9,1},{17,25},{25,17},{2,10},{10... | collective-permute-start | bytes 1179656 | tf_op jit(solution)/shard_map/ppermute | solution.py:316
  39.1 0.2 pad_maximum_fusion.xo.refs_3_
  39.2 15.1 %collective-permute-done.1.w2 = bf16[256,768]{1,0:T(8,128)(2,1)S(1)} collective-permute-done((bf16[256,768]{1,0:T(8,128)(2,1)S(1)}, bf16[256,768]{1,0:T(8,128)(2,1)S(1)}, u32[]{:S(2)}, u32[]{:S(2)}) %collective-permute-start.1) | collective-permute-done | bytes 393248 | tf_op jit(solution)/shard_map/ppermute | solution.py:315
  54.5 3.7 %collective-permute-done.4 = bf16[128,2176]{1,0:T(8,128)(2,1)S(1)} collective-permute-done((bf16[128,2176]{1,0:T(8,128)(2,1)S(1)}, bf16[128,2176]{1,0:T(8,128)(2,1)S(1)}, u32[]{:S(2)}, u32[]{:S(2)}) %collective-permute-start.4) | collective-permute-done | bytes 557088 | tf_op jit(solution)/shard_map/ppermute | solution.py:301
  58.4 5.6 %collective-permute-done.7.w3 = bf16[256,768]{1,0:T(8,128)(2,1)S(1)} collective-permute-done((bf16[256,768]{1,0:T(8,128)(2,1)S(1)}, bf16[256,768]{1,0:T(8,128)(2,1)S(1)}, u32[]{:S(2)}, u32[]{:S(2)}) %collective-permute-start.7) | collective-permute-done | bytes 393248 | tf_op jit(solution)/shard_map/ppermute | solution.py:319
  64.0 0.7 weights.1
  64.8 3.6 %far.1 = (bf16[1024,768]{1,0:T(8,128)(2,1)S(1)}, bf16[1024,768]{1,0:T(8,128)(2,1)S(1)}) custom-call(bf16[512,2176]{1,0:T(8,128)(2,1)S(1)} %collective-permute-done.6.xs.refs_0_, bf16[512,2176]{1,0:T(8,128)(2,1)S(1)} %constant_dynamic-update-slice_fusion.xo.refs_1_, bf16[1024,768]{1,0:T(8,128)(2,1)S(1)} %get-tuple-element.63.w_all, ...), custom_call_target="tpu_custom_call" | custom-call | flops 68719476736 | bytes 12582912 | tf_op jit(solution)/shard_map/far/pallas_call | solution.py:229
  68.4 0.7 collective-permute-done.12.xs.refs_2_
  69.1 3.5 %near.1 = (bf16[1024,768]{1,0:T(8,128)(2,1)S(1)}, bf16[1024,768]{1,0:T(8,128)(2,1)S(1)}) custom-call(bf16[512,2176]{1,0:T(8,128)(2,1)S(1)} %collective-permute-done.12.xs.refs_2_, bf16[512,2176]{1,0:T(8,128)(2,1)S(1)} %pad_maximum_fusion.xo.refs_3_, bf16[1024,768]{1,0:T(8,128)(2,1)S(1)} %get-tuple-element.63.w_all, ...), custom_call_target="tpu_custom_call" | custom-call | flops 68719476736 | bytes 12582912 | tf_op jit(solution)/shard_map/near/pallas_call | solution.py:229
  72.6 1.9 %outer.3 = bf16[256,768]{1,0:T(8,128)(2,1)S(1)} custom-call(s32[2]{0:T(128)S(1)} %pad_add_fusion.place, bf16[512,2176]{1,0:T(8,128)(2,1)S(1)} %collective-permute-done.6.xs.refs_0_, bf16[512,2176]{1,0:T(8,128)(2,1)S(1)} %constant_dynamic-update-slice_fusion.xo.refs_1_, bf16[512,2176]{1,0:T(8,128)(2,1)S(1)} %collective-permute-done.12.xs.refs_2_, ...), custom_call_target="tpu_custom_call" | custom-call | flops 68719476736 | bytes 12582912 | tf_op jit(solution)/shard_map/outer/pallas_call | solution.py:265
  74.5 0.3 collective-permute-start.14
  74.9 1.8 %far_tokens.1 = (bf16[512,1024]{1,0:T(8,128)(2,1)S(1)}, bf16[512,1024]{1,0:T(8,128)(2,1)S(1)}) custom-call(bf16[1024,768]{1,0:T(8,128)(2,1)S(1)} %get-tuple-element.71.gw, bf16[1024,768]{1,0:T(8,128)(2,1)S(1)} %get-tuple-element.63.w_all), custom_call_target="tpu_custom_call" | custom-call | flops 1048576 | bytes 12582912 | tf_op jit(solution)/shard_map/far_tokens/pallas_call | solution.py:229
  76.8 3.1 %outer.4 = (bf16[256,768]{1,0:T(8,128)(2,1)S(1)}, bf16[256,768]{1,0:T(8,128)(2,1)S(1)}) custom-call(s32[2]{0:T(128)S(1)} %pad_add_fusion.place, bf16[512,2176]{1,0:T(8,128)(2,1)S(1)} %collective-permute-done.6.xs.refs_0_, bf16[512,2176]{1,0:T(8,128)(2,1)S(1)} %constant_dynamic-update-slice_fusion.xo.refs_1_, ...), custom_call_target="tpu_custom_call" | custom-call | flops 68719476736 | bytes 12582912 | tf_op jit(solution)/shard_map/outer/pallas_call | solution.py:265
  79.9 1.8 %collective-permute-start.23 = (bf16[256,768]{1,0:T(8,128)(2,1)S(1)}, bf16[256,768]{1,0:T(8,128)(2,1)S(1)}, u32[]{:S(2)}, u32[]{:S(2)}) collective-permute-start(bf16[256,768]{1,0:T(8,128)(2,1)S(1)} %get-tuple-element.99), channel_id=1, source_target_pairs={{0,8},{8,0},{16,24},{24,16},{1,9},{9,1},{17,25},{25,17},{2,10},{10... | collective-permute-start | bytes 1179656 | tf_op jit(solution)/shard_map/ppermute | solution.py:359
  81.7 0.4 add_convert_fusion.7
  82.1 1.6 %collective-permute-start.15 = (bf16[128,1024]{1,0:T(8,128)(2,1)S(1)}, bf16[128,1024]{1,0:T(8,128)(2,1)S(1)}, u32[]{:S(2)}, u32[]{:S(2)}) collective-permute-start(bf16[128,1024]{1,0:T(8,128)(2,1)S(1)} %get-tuple-element.108), channel_id=1, source_target_pairs={{0,2},{1,3},{2,0},{3,1},{4,6},{5,7},{6,4},{7,5},{8,10},{9,11},{10,... | collective-permute-start | bytes 786440 | tf_op jit(solution)/shard_map/ppermute | solution.py:340
  83.7 0.2 collective-permute-start.16
  83.9 1.8 %collective-permute-start.17 = (bf16[128,1024]{1,0:T(8,128)(2,1)S(1)}, bf16[128,1024]{1,0:T(8,128)(2,1)S(1)}, u32[]{:S(2)}, u32[]{:S(2)}) collective-permute-start(bf16[128,1024]{1,0:T(8,128)(2,1)S(1)} %get-tuple-element.106), channel_id=1, source_target_pairs={{0,6},{1,7},{2,4},{3,5},{4,2},{5,3},{6,0},{7,1},{8,14},{9,15},{10,... | collective-permute-start | bytes 786440 | tf_op jit(solution)/shard_map/ppermute | solution.py:340
  85.7 0.9 collective-permute-done.14
  86.6 1.6 %collective-permute-start.24 = (bf16[256,768]{1,0:T(8,128)(2,1)S(1)}, bf16[256,768]{1,0:T(8,128)(2,1)S(1)}, u32[]{:S(2)}, u32[]{:S(2)}) collective-permute-start(bf16[256,768]{1,0:T(8,128)(2,1)S(1)} %add_convert_fusion), channel_id=1, source_target_pairs={{0,16},{8,24},{16,0},{24,8},{1,17},{9,25},{17,1},{25,9},{2,18},{10... | collective-permute-start | bytes 1179656 | tf_op jit(solution)/shard_map/ppermute | solution.py:365
  88.3 1.8 %near_tokens.1 = (bf16[512,1024]{1,0:T(8,128)(2,1)S(1)}, bf16[512,1024]{1,0:T(8,128)(2,1)S(1)}) custom-call(bf16[1024,768]{1,0:T(8,128)(2,1)S(1)} %get-tuple-element.81.gw, bf16[1024,768]{1,0:T(8,128)(2,1)S(1)} %get-tuple-element.63.w_all), custom_call_target="tpu_custom_call" | custom-call | flops 68719476736 | bytes 12582912 | tf_op jit(solution)/shard_map/near_tokens/pallas_call | solution.py:229
  90.1 1.2 %collective-permute-done.15 = bf16[128,1024]{1,0:T(8,128)(2,1)S(1)} collective-permute-done((bf16[128,1024]{1,0:T(8,128)(2,1)S(1)}, bf16[128,1024]{1,0:T(8,128)(2,1)S(1)}, u32[]{:S(2)}, u32[]{:S(2)}) %collective-permute-start.15) | collective-permute-done | bytes 262176 | tf_op jit(solution)/shard_map/ppermute | solution.py:340
  91.3 6.1 %collective-permute-done.16 = bf16[128,1024]{1,0:T(8,128)(2,1)S(1)} collective-permute-done((bf16[128,1024]{1,0:T(8,128)(2,1)S(1)}, bf16[128,1024]{1,0:T(8,128)(2,1)S(1)}, u32[]{:S(2)}, u32[]{:S(2)}) %collective-permute-start.16) | collective-permute-done | bytes 262176 | tf_op jit(solution)/shard_map/ppermute | solution.py:340
  97.4 1.7 %outer.5.own = bf16[256,768]{1,0:T(8,128)(2,1)S(1)} custom-call(s32[2]{0:T(128)S(1)} %pad_add_fusion.place, bf16[512,2176]{1,0:T(8,128)(2,1)S(1)} %collective-permute-done.6.xs.refs_0_, bf16[512,2176]{1,0:T(8,128)(2,1)S(1)} %constant_dynamic-update-slice_fusion.xo.refs_1_, bf16[512,2176]{1,0:T(8,128)(2,1)S(1)} %collective-permute-done.12.xs.refs_2_, ...), custom_call_target="tpu_custom_call" | custom-call | flops 68719476736 | bytes 12582912 | tf_op jit(solution)/shard_map/outer/pallas_call | solution.py:265
  99.2 0.7 add_convert_fusion.2
  99.9 1.6 %collective-permute-start.21 = (bf16[128,1024]{1,0:T(8,128)(2,1)S(1)}, bf16[128,1024]{1,0:T(8,128)(2,1)S(1)}, u32[]{:S(2)}, u32[]{:S(2)}) collective-permute-start(bf16[128,1024]{1,0:T(8,128)(2,1)S(1)} %get-tuple-element.94), channel_id=1, source_target_pairs={{0,6},{1,7},{2,4},{3,5},{4,2},{5,3},{6,0},{7,1},{8,14},{9,15},{10,... | collective-permute-start | bytes 786440 | tf_op jit(solution)/shard_map/ppermute | solution.py:340
  101.4 0.5 collective-permute-start.20
  101.9 1.5 %collective-permute-start.19 = (bf16[128,1024]{1,0:T(8,128)(2,1)S(1)}, bf16[128,1024]{1,0:T(8,128)(2,1)S(1)}, u32[]{:S(2)}, u32[]{:S(2)}) collective-permute-start(bf16[128,1024]{1,0:T(8,128)(2,1)S(1)} %get-tuple-element.92), channel_id=1, source_target_pairs={{0,2},{1,3},{2,0},{3,1},{4,6},{5,7},{6,4},{7,5},{8,10},{9,11},{10,... | collective-permute-start | bytes 786440 | tf_op jit(solution)/shard_map/ppermute | solution.py:340
  103.4 1.6 %collective-permute-start.22 = (bf16[128,1024]{1,0:T(8,128)(2,1)S(1)}, bf16[128,1024]{1,0:T(8,128)(2,1)S(1)}, u32[]{:S(2)}, u32[]{:S(2)}) collective-permute-start(bf16[128,1024]{1,0:T(8,128)(2,1)S(1)} %get-tuple-element.95), channel_id=1, source_target_pairs={{0,16},{8,24},{16,0},{24,8},{1,17},{9,25},{17,1},{25,9},{2,18},{10... | collective-permute-start | bytes 786440 | tf_op jit(solution)/shard_map/ppermute | solution.py:375
  105.0 6.6 %collective-permute-done.24.far = bf16[256,768]{1,0:T(8,128)(2,1)S(1)} collective-permute-done((bf16[256,768]{1,0:T(8,128)(2,1)S(1)}, bf16[256,768]{1,0:T(8,128)(2,1)S(1)}, u32[]{:S(2)}, u32[]{:S(2)}) %collective-permute-start.24) | collective-permute-done | bytes 393248 | tf_op jit(solution)/shard_map/ppermute | solution.py:365
  111.6 1.0 join.1
  112.6 1.7 %copy.11 = bf16[256,2,768]{2,1,0:T(2,128)(2,1)} copy(bf16[256,2,768]{2,0,1:T(8,128)(2,1)S(1)} %bitcast.13) | data formatting | bytes 1572864
  114.4 2.4 %collective-permute-done.22 = bf16[128,1024]{1,0:T(8,128)(2,1)S(1)} collective-permute-done((bf16[128,1024]{1,0:T(8,128)(2,1)S(1)}, bf16[128,1024]{1,0:T(8,128)(2,1)S(1)}, u32[]{:S(2)}, u32[]{:S(2)}) %collective-permute-start.22) | collective-permute-done | bytes 262176 | tf_op jit(solution)/shard_map/ppermute | solution.py:375
  116.8 0.8 add_convert_fusion.1
  (32 shorter events, 1.0 us)
Async XLA Ops:
  0.6 12.3 %copy-start.1 = (bf16[96,2,1024]{2,1,0:T(2,128)(2,1)S(1)}, bf16[96,2,1024]{2,1,0:T(2,128)(2,1)}, u32[]{:S(2)}) copy-start(bf16[96,2,1024]{2,1,0:T(2,128)(2,1)} %param.11) | copy-start | bytes 1179652
  2.6 36.4 %copy-start = (bf16[128,2176]{1,0:T(8,128)(2,1)S(1)}, bf16[128,2176]{1,0:T(8,128)(2,1)}, u32[]{:S(2)}) copy-start(bf16[128,2176]{1,0:T(8,128)(2,1)} %payload.1) | copy-start | bytes 1671172
  2.7 28.9 %collective-permute-start = (bf16[128,2176]{1,0:T(8,128)(2,1)}, bf16[128,2176]{1,0:T(8,128)(2,1)S(1)}, u32[]{:S(2)}, u32[]{:S(2)}) collective-permute-start(bf16[128,2176]{1,0:T(8,128)(2,1)} %payload.1), channel_id=1, source_target_pairs={{0,16},{8,24},{16,0},{24,8},{1,17},{9,25},{17,1},{25,9},{2,18},{10... | collective-permute-start | bytes 1671176 | tf_op jit(solution)/shard_map/ppermute | solution.py:309
  6.7 27.9 %collective-permute-start.11 = (bf16[128,2176]{1,0:T(8,128)(2,1)}, bf16[128,2176]{1,0:T(8,128)(2,1)S(1)}, u32[]{:S(2)}, u32[]{:S(2)}) collective-permute-start(bf16[128,2176]{1,0:T(8,128)(2,1)} %payload.1), channel_id=1, source_target_pairs={{0,6},{1,7},{2,4},{3,5},{4,2},{5,3},{6,0},{7,1},{8,14},{9,15},{10,... | collective-permute-start | bytes 1671176 | tf_op jit(solution)/shard_map/ppermute | solution.py:301
  9.1 25.9 %collective-permute-start.10 = (bf16[128,2176]{1,0:T(8,128)(2,1)}, bf16[128,2176]{1,0:T(8,128)(2,1)S(1)}, u32[]{:S(2)}, u32[]{:S(2)}) collective-permute-start(bf16[128,2176]{1,0:T(8,128)(2,1)} %payload.1), channel_id=1, source_target_pairs={{0,4},{1,5},{2,6},{3,7},{4,0},{5,1},{6,2},{7,3},{8,12},{9,13},{10,... | collective-permute-start | bytes 1671176 | tf_op jit(solution)/shard_map/ppermute | solution.py:301
  9.6 25.4 %collective-permute-start.9 = (bf16[128,2176]{1,0:T(8,128)(2,1)}, bf16[128,2176]{1,0:T(8,128)(2,1)S(1)}, u32[]{:S(2)}, u32[]{:S(2)}) collective-permute-start(bf16[128,2176]{1,0:T(8,128)(2,1)} %payload.1), channel_id=1, source_target_pairs={{0,2},{1,3},{2,0},{3,1},{4,6},{5,7},{6,4},{7,5},{8,10},{9,11},{10,... | collective-permute-start | bytes 1671176 | tf_op jit(solution)/shard_map/ppermute | solution.py:301
  10.2 17.2 %collective-permute-start.8 = (bf16[96,2,1024]{2,1,0:T(2,128)(2,1)}, bf16[96,2,1024]{2,1,0:T(2,128)(2,1)}, u32[]{:S(2)}, u32[]{:S(2)}) collective-permute-start(bf16[96,2,1024]{2,1,0:T(2,128)(2,1)} %param.11), channel_id=1, source_target_pairs={{0,8},{8,0},{16,24},{24,16},{1,9},{9,1},{17,25},{25,17},{2,10},{10... | collective-permute-start | bytes 1179656 | tf_op jit(solution)/shard_map/ppermute | solution.py:310
  31.5 22.9 %collective-permute-start.3 = (bf16[128,2176]{1,0:T(8,128)(2,1)S(1)}, bf16[128,2176]{1,0:T(8,128)(2,1)S(1)}, u32[]{:S(2)}, u32[]{:S(2)}) collective-permute-start(bf16[128,2176]{1,0:T(8,128)(2,1)S(1)} %collective-permute-done), channel_id=1, source_target_pairs={{0,2},{1,3},{2,0},{3,1},{4,6},{5,7},{6,4},{7,5},{8,10},{9,11},{10,... | collective-permute-start | bytes 1671176 | tf_op jit(solution)/shard_map/ppermute | solution.py:301
  33.0 25.2 %collective-permute-start.4 = (bf16[128,2176]{1,0:T(8,128)(2,1)S(1)}, bf16[128,2176]{1,0:T(8,128)(2,1)S(1)}, u32[]{:S(2)}, u32[]{:S(2)}) collective-permute-start(bf16[128,2176]{1,0:T(8,128)(2,1)S(1)} %collective-permute-done), channel_id=1, source_target_pairs={{0,4},{1,5},{2,6},{3,7},{4,0},{5,1},{6,2},{7,3},{8,12},{9,13},{10,... | collective-permute-start | bytes 1671176 | tf_op jit(solution)/shard_map/ppermute | solution.py:301
  34.5 23.7 %collective-permute-start.5 = (bf16[128,2176]{1,0:T(8,128)(2,1)S(1)}, bf16[128,2176]{1,0:T(8,128)(2,1)S(1)}, u32[]{:S(2)}, u32[]{:S(2)}) collective-permute-start(bf16[128,2176]{1,0:T(8,128)(2,1)S(1)} %collective-permute-done), channel_id=1, source_target_pairs={{0,6},{1,7},{2,4},{3,5},{4,2},{5,3},{6,0},{7,1},{8,14},{9,15},{10,... | collective-permute-start | bytes 1671176 | tf_op jit(solution)/shard_map/ppermute | solution.py:301
  35.0 19.3 %collective-permute-start.1 = (bf16[256,768]{1,0:T(8,128)(2,1)S(1)}, bf16[256,768]{1,0:T(8,128)(2,1)S(1)}, u32[]{:S(2)}, u32[]{:S(2)}) collective-permute-start(bf16[256,768]{1,0:T(8,128)(2,1)S(1)} %get-tuple-element.54), channel_id=1, source_target_pairs={{0,16},{8,24},{16,0},{24,8},{1,17},{9,25},{17,1},{25,9},{2,18},{10... | collective-permute-start | bytes 1179656 | tf_op jit(solution)/shard_map/ppermute | solution.py:315
  35.0 19.3 %collective-permute-start.2 = (bf16[256,768]{1,0:T(8,128)(2,1)S(1)}, bf16[256,768]{1,0:T(8,128)(2,1)S(1)}, u32[]{:S(2)}, u32[]{:S(2)}) collective-permute-start(bf16[256,768]{1,0:T(8,128)(2,1)S(1)} %get-tuple-element.55.w0), channel_id=1, source_target_pairs={{0,8},{8,0},{16,24},{24,16},{1,9},{9,1},{17,25},{25,17},{2,10},{10... | collective-permute-start | bytes 1179656 | tf_op jit(solution)/shard_map/ppermute | solution.py:316
  54.4 9.6 %collective-permute-start.7 = (bf16[256,768]{1,0:T(8,128)(2,1)S(1)}, bf16[256,768]{1,0:T(8,128)(2,1)S(1)}, u32[]{:S(2)}, u32[]{:S(2)}) collective-permute-start(bf16[256,768]{1,0:T(8,128)(2,1)S(1)} %collective-permute-done.1.w2), channel_id=1, source_target_pairs={{0,8},{8,0},{16,24},{24,16},{1,9},{9,1},{17,25},{25,17},{2,10},{10... | collective-permute-start | bytes 1179656 | tf_op jit(solution)/shard_map/ppermute | solution.py:319
  58.3 6.4 %collective-permute-start.6 = (bf16[512,2176]{1,0:T(8,128)(2,1)S(1)}, bf16[512,2176]{1,0:T(8,128)(2,1)S(1)}, u32[]{:S(2)}, u32[]{:S(2)}) collective-permute-start(bf16[512,2176]{1,0:T(8,128)(2,1)S(1)} %constant_dynamic-update-slice_fusion.xo.refs_1_), channel_id=1, source_target_pairs={{0,1},{1,0},{2,3},{3,2},{4,5},{5,4},{6,7},{7,6},{8,9},{9,8},{10,11... | collective-permute-start | bytes 6684680 | tf_op jit(solution)/shard_map/ppermute | solution.py:321
  64.7 4.4 %collective-permute-start.12 = (bf16[512,2176]{1,0:T(8,128)(2,1)S(1)}, bf16[512,2176]{1,0:T(8,128)(2,1)S(1)}, u32[]{:S(2)}, u32[]{:S(2)}) collective-permute-start(bf16[512,2176]{1,0:T(8,128)(2,1)S(1)} %pad_maximum_fusion.xo.refs_3_), channel_id=1, source_target_pairs={{0,1},{1,0},{2,3},{3,2},{4,5},{5,4},{6,7},{7,6},{8,9},{9,8},{10,11... | collective-permute-start | bytes 6684680 | tf_op jit(solution)/shard_map/ppermute | solution.py:334
  74.5 12.0 %collective-permute-start.14 = (bf16[256,768]{1,0:T(8,128)(2,1)S(1)}, bf16[256,768]{1,0:T(8,128)(2,1)S(1)}, u32[]{:S(2)}, u32[]{:S(2)}) collective-permute-start(bf16[256,768]{1,0:T(8,128)(2,1)S(1)} %outer.3), channel_id=1, source_target_pairs={{0,8},{8,0},{16,24},{24,16},{1,9},{9,1},{17,25},{25,17},{2,10},{10... | collective-permute-start | bytes 1179656 | tf_op jit(solution)/shard_map/ppermute | solution.py:353
  76.7 5.0 %collective-permute-start.13 = (bf16[512,1024]{1,0:T(8,128)(2,1)S(1)}, bf16[512,1024]{1,0:T(8,128)(2,1)S(1)}, u32[]{:S(2)}, u32[]{:S(2)}) collective-permute-start(bf16[512,1024]{1,0:T(8,128)(2,1)S(1)} %get-tuple-element.75), channel_id=1, source_target_pairs={{0,1},{1,0},{2,3},{3,2},{4,5},{5,4},{6,7},{7,6},{8,9},{9,8},{10,11... | collective-permute-start | bytes 3145736 | tf_op jit(solution)/shard_map/ppermute | solution.py:356
  79.9 23.5 %collective-permute-start.23 = (bf16[256,768]{1,0:T(8,128)(2,1)S(1)}, bf16[256,768]{1,0:T(8,128)(2,1)S(1)}, u32[]{:S(2)}, u32[]{:S(2)}) collective-permute-start(bf16[256,768]{1,0:T(8,128)(2,1)S(1)} %get-tuple-element.99), channel_id=1, source_target_pairs={{0,8},{8,0},{16,24},{24,16},{1,9},{9,1},{17,25},{25,17},{2,10},{10... | collective-permute-start | bytes 1179656 | tf_op jit(solution)/shard_map/ppermute | solution.py:359
  82.1 9.2 %collective-permute-start.15 = (bf16[128,1024]{1,0:T(8,128)(2,1)S(1)}, bf16[128,1024]{1,0:T(8,128)(2,1)S(1)}, u32[]{:S(2)}, u32[]{:S(2)}) collective-permute-start(bf16[128,1024]{1,0:T(8,128)(2,1)S(1)} %get-tuple-element.108), channel_id=1, source_target_pairs={{0,2},{1,3},{2,0},{3,1},{4,6},{5,7},{6,4},{7,5},{8,10},{9,11},{10,... | collective-permute-start | bytes 786440 | tf_op jit(solution)/shard_map/ppermute | solution.py:340
  83.7 13.8 %collective-permute-start.16 = (bf16[128,1024]{1,0:T(8,128)(2,1)S(1)}, bf16[128,1024]{1,0:T(8,128)(2,1)S(1)}, u32[]{:S(2)}, u32[]{:S(2)}) collective-permute-start(bf16[128,1024]{1,0:T(8,128)(2,1)S(1)} %get-tuple-element.107), channel_id=1, source_target_pairs={{0,4},{1,5},{2,6},{3,7},{4,0},{5,1},{6,2},{7,3},{8,12},{9,13},{10,... | collective-permute-start | bytes 786440 | tf_op jit(solution)/shard_map/ppermute | solution.py:340
  83.9 13.6 %collective-permute-start.17 = (bf16[128,1024]{1,0:T(8,128)(2,1)S(1)}, bf16[128,1024]{1,0:T(8,128)(2,1)S(1)}, u32[]{:S(2)}, u32[]{:S(2)}) collective-permute-start(bf16[128,1024]{1,0:T(8,128)(2,1)S(1)} %get-tuple-element.106), channel_id=1, source_target_pairs={{0,6},{1,7},{2,4},{3,5},{4,2},{5,3},{6,0},{7,1},{8,14},{9,15},{10,... | collective-permute-start | bytes 786440 | tf_op jit(solution)/shard_map/ppermute | solution.py:340
  86.6 24.9 %collective-permute-start.24 = (bf16[256,768]{1,0:T(8,128)(2,1)S(1)}, bf16[256,768]{1,0:T(8,128)(2,1)S(1)}, u32[]{:S(2)}, u32[]{:S(2)}) collective-permute-start(bf16[256,768]{1,0:T(8,128)(2,1)S(1)} %add_convert_fusion), channel_id=1, source_target_pairs={{0,16},{8,24},{16,0},{24,8},{1,17},{9,25},{17,1},{25,9},{2,18},{10... | collective-permute-start | bytes 1179656 | tf_op jit(solution)/shard_map/ppermute | solution.py:365
  91.3 7.8 %collective-permute-start.18 = (bf16[512,1024]{1,0:T(8,128)(2,1)S(1)}, bf16[512,1024]{1,0:T(8,128)(2,1)S(1)}, u32[]{:S(2)}, u32[]{:S(2)}) collective-permute-start(bf16[512,1024]{1,0:T(8,128)(2,1)S(1)} %get-tuple-element.88), channel_id=1, source_target_pairs={{0,1},{1,0},{2,3},{3,2},{4,5},{5,4},{6,7},{7,6},{8,9},{9,8},{10,11... | collective-permute-start | bytes 3145736 | tf_op jit(solution)/shard_map/ppermute | solution.py:368
  99.9 14.4 %collective-permute-start.21 = (bf16[128,1024]{1,0:T(8,128)(2,1)S(1)}, bf16[128,1024]{1,0:T(8,128)(2,1)S(1)}, u32[]{:S(2)}, u32[]{:S(2)}) collective-permute-start(bf16[128,1024]{1,0:T(8,128)(2,1)S(1)} %get-tuple-element.94), channel_id=1, source_target_pairs={{0,6},{1,7},{2,4},{3,5},{4,2},{5,3},{6,0},{7,1},{8,14},{9,15},{10,... | collective-permute-start | bytes 786440 | tf_op jit(solution)/shard_map/ppermute | solution.py:340
  101.4 12.8 %collective-permute-start.20 = (bf16[128,1024]{1,0:T(8,128)(2,1)S(1)}, bf16[128,1024]{1,0:T(8,128)(2,1)S(1)}, u32[]{:S(2)}, u32[]{:S(2)}) collective-permute-start(bf16[128,1024]{1,0:T(8,128)(2,1)S(1)} %get-tuple-element.93), channel_id=1, source_target_pairs={{0,4},{1,5},{2,6},{3,7},{4,0},{5,1},{6,2},{7,3},{8,12},{9,13},{10,... | collective-permute-start | bytes 786440 | tf_op jit(solution)/shard_map/ppermute | solution.py:340
  101.9 12.3 %collective-permute-start.19 = (bf16[128,1024]{1,0:T(8,128)(2,1)S(1)}, bf16[128,1024]{1,0:T(8,128)(2,1)S(1)}, u32[]{:S(2)}, u32[]{:S(2)}) collective-permute-start(bf16[128,1024]{1,0:T(8,128)(2,1)S(1)} %get-tuple-element.92), channel_id=1, source_target_pairs={{0,2},{1,3},{2,0},{3,1},{4,6},{5,7},{6,4},{7,5},{8,10},{9,11},{10,... | collective-permute-start | bytes 786440 | tf_op jit(solution)/shard_map/ppermute | solution.py:340
  103.4 13.4 %collective-permute-start.22 = (bf16[128,1024]{1,0:T(8,128)(2,1)S(1)}, bf16[128,1024]{1,0:T(8,128)(2,1)S(1)}, u32[]{:S(2)}, u32[]{:S(2)}) collective-permute-start(bf16[128,1024]{1,0:T(8,128)(2,1)S(1)} %get-tuple-element.95), channel_id=1, source_target_pairs={{0,16},{8,24},{16,0},{24,8},{1,17},{9,25},{17,1},{25,9},{2,18},{10... | collective-permute-start | bytes 786440 | tf_op jit(solution)/shard_map/ppermute | solution.py:375

commit v6 on v5

--- a/solution.py
+++ b/solution.py
@@ -364,7 +364,7 @@
     relay = plus(g2, got3)
     away_half = lax.ppermute(relay, "dp", across)
     near_gw, relay = after((near_gw, relay))
-    near_ts, near_to = backs("near_tokens", near_gw, HIDE)
+    near_ts, near_to = backs("near_tokens", near_gw, 1 << 20)
     near_got = lax.ppermute(near_ts, "expert", cores)
     near_mid, near_to, *far_back = after((near_mid, near_to, *far_back))
     (g0,) = outer(place, tiles, (far_mid, near_mid), grad_scale, rows, 0, 1)

time: 118 us -> 118 us (level)
  transfers between devices with their start and end apart: 25 -> 25, of which waited for: 12 -> 13; matrix products, arithmetic and copies ran while one was open for 5% -> 5% of each run, Pallas kernels for 12% -> 12%
where the time goes in v6:
time: 118 us
  waiting for transfers between devices  58.4 us (49%)
  starting transfers between devices  29.7 us (25%)
  Pallas kernels  21.9 us (19%)
  local copies, waits for them, and re-layouts  4.26 us (4%)
  other arithmetic  2.37 us (2%)
    ppermute x1, waiting for transfers between devices, by_tokens(): w2 = lax.ppermute(given, 'dp', across)  15.1 us
    ppermute x1, waiting for transfers between devices, by_tokens(): down1 = lax.ppermute(weight_down, 'dp', beside)  13.4 us
    pallas_call x5, Pallas kernels, vmem_call(): pl.pallas_call(kernel, in_specs=specs, out_specs=[vmem] * len(outs), out_...  11.4 us
    ppermute x6, starting transfers between devices, back_hops(): lax.ppermute(t, 'expert', hop)  7.11 us
    ppermute x6, starting transfers between devices, spread(): return [lax.ppermute(x, 'expert', hop) for hop in hops]  6.98 us
    ppermute x1, waiting for transfers between devices, by_tokens(): away_half = lax.ppermute(relay, 'dp', across)  6.84 us
    pallas_call x3, Pallas kernels, outer(): pl.pallas_call(functools.partial(outer_kernel, scale, len(gs), count), gr...  6.7 us
    ppermute x6, waiting for transfers between devices, back_hops(): lax.ppermute(t, 'expert', hop)  6.62 us
  transfers between devices with their start and end apart: 25, of which 13 were waited for; matrix products, arithmetic and copies ran while one was open for 5% of the time, Pallas kernels for 12%

profile of v6, /device:TPU:0, one launch (start us, length us, event | category | flops | bytes accessed | tf_op | source)
XLA Modules:
  0.0 117.6 jit_solution(15075557994294248291)
XLA Ops:
  0.6 2.0 %payload.1 = bf16[128,2176]{1,0:T(8,128)(2,1)} custom-call(bf16[128,1024]{1,0:T(8,128)(2,1)} %tokens.1, bf16[128,1024]{1,0:T(8,128)(2,1)} %cotangent.1, s32[8,128]{1,0:T(8,128)} %bitcast.17, f32[8,128]{1,0:T(8,128)} %bitcast.18), custom_call_target="tpu_custom_call" | custom-call | flops 1048576 | bytes 2097152 | tf_op jit(solution)/shard_map/payload/pallas_call | solution.py:106
  2.7 4.0 %collective-permute-start = (bf16[128,2176]{1,0:T(8,128)(2,1)}, bf16[128,2176]{1,0:T(8,128)(2,1)S(1)}, u32[]{:S(2)}, u32[]{:S(2)}) collective-permute-start(bf16[128,2176]{1,0:T(8,128)(2,1)} %payload.1), channel_id=1, source_target_pairs={{0,16},{8,24},{16,0},{24,8},{1,17},{9,25},{17,1},{25,9},{2,18},{10... | collective-permute-start | bytes 1671176 | tf_op jit(solution)/shard_map/ppermute | solution.py:309
  6.7 2.4 %collective-permute-start.11 = (bf16[128,2176]{1,0:T(8,128)(2,1)}, bf16[128,2176]{1,0:T(8,128)(2,1)S(1)}, u32[]{:S(2)}, u32[]{:S(2)}) collective-permute-start(bf16[128,2176]{1,0:T(8,128)(2,1)} %payload.1), channel_id=1, source_target_pairs={{0,6},{1,7},{2,4},{3,5},{4,2},{5,3},{6,0},{7,1},{8,14},{9,15},{10,... | collective-permute-start | bytes 1671176 | tf_op jit(solution)/shard_map/ppermute | solution.py:301
  9.1 0.5 collective-permute-start.10
  9.6 0.5 collective-permute-start.9
  10.2 1.6 %collective-permute-start.8 = (bf16[96,2,1024]{2,1,0:T(2,128)(2,1)}, bf16[96,2,1024]{2,1,0:T(2,128)(2,1)}, u32[]{:S(2)}, u32[]{:S(2)}) collective-permute-start(bf16[96,2,1024]{2,1,0:T(2,128)(2,1)} %param.11), channel_id=1, source_target_pairs={{0,8},{8,0},{16,24},{24,16},{1,9},{9,1},{17,25},{25,17},{2,10},{10... | collective-permute-start | bytes 1179656 | tf_op jit(solution)/shard_map/ppermute | solution.py:310
  11.8 1.2 %copy.13 = bf16[256,2,768]{2,0,1:T(8,128)(2,1)S(1)} copy(bf16[256,2,768]{2,1,0:T(2,128)(2,1)} %param.10) | data formatting | bytes 1572864 | tf_op jit(solution)/shard_map/optimization_barrier | solution.py:311
  13.1 0.8 halves.1
  13.9 13.4 %collective-permute-done.8 = bf16[96,2,1024]{2,1,0:T(2,128)(2,1)} collective-permute-done((bf16[96,2,1024]{2,1,0:T(2,128)(2,1)}, bf16[96,2,1024]{2,1,0:T(2,128)(2,1)}, u32[]{:S(2)}, u32[]{:S(2)}) %collective-permute-start.8) | collective-permute-done | bytes 393248 | tf_op jit(solution)/shard_map/ppermute | solution.py:310
  27.4 1.1 copy.10
  28.4 3.1 %collective-permute-done = bf16[128,2176]{1,0:T(8,128)(2,1)S(1)} collective-permute-done((bf16[128,2176]{1,0:T(8,128)(2,1)}, bf16[128,2176]{1,0:T(8,128)(2,1)S(1)}, u32[]{:S(2)}, u32[]{:S(2)}) %collective-permute-start) | collective-permute-done | bytes 557088 | tf_op jit(solution)/shard_map/ppermute | solution.py:309
  31.5 1.5 %collective-permute-start.3 = (bf16[128,2176]{1,0:T(8,128)(2,1)S(1)}, bf16[128,2176]{1,0:T(8,128)(2,1)S(1)}, u32[]{:S(2)}, u32[]{:S(2)}) collective-permute-start(bf16[128,2176]{1,0:T(8,128)(2,1)S(1)} %collective-permute-done), channel_id=1, source_target_pairs={{0,2},{1,3},{2,0},{3,1},{4,6},{5,7},{6,4},{7,5},{8,10},{9,11},{10,... | collective-permute-start | bytes 1671176 | tf_op jit(solution)/shard_map/ppermute | solution.py:301
  33.0 1.5 %collective-permute-start.4 = (bf16[128,2176]{1,0:T(8,128)(2,1)S(1)}, bf16[128,2176]{1,0:T(8,128)(2,1)S(1)}, u32[]{:S(2)}, u32[]{:S(2)}) collective-permute-start(bf16[128,2176]{1,0:T(8,128)(2,1)S(1)} %collective-permute-done), channel_id=1, source_target_pairs={{0,4},{1,5},{2,6},{3,7},{4,0},{5,1},{6,2},{7,3},{8,12},{9,13},{10,... | collective-permute-start | bytes 1671176 | tf_op jit(solution)/shard_map/ppermute | solution.py:301
  34.5 0.5 collective-permute-start.5
  35.0 4.0 %collective-permute-start.2 = (bf16[256,768]{1,0:T(8,128)(2,1)S(1)}, bf16[256,768]{1,0:T(8,128)(2,1)S(1)}, u32[]{:S(2)}, u32[]{:S(2)}) collective-permute-start(bf16[256,768]{1,0:T(8,128)(2,1)S(1)} %get-tuple-element.55.w0), channel_id=1, source_target_pairs={{0,8},{8,0},{16,24},{24,16},{1,9},{9,1},{17,25},{25,17},{2,10},{10... | collective-permute-start | bytes 1179656 | tf_op jit(solution)/shard_map/ppermute | solution.py:316
  39.1 0.2 pad_maximum_fusion.xo.refs_3_
  39.2 15.1 %collective-permute-done.1.w2 = bf16[256,768]{1,0:T(8,128)(2,1)S(1)} collective-permute-done((bf16[256,768]{1,0:T(8,128)(2,1)S(1)}, bf16[256,768]{1,0:T(8,128)(2,1)S(1)}, u32[]{:S(2)}, u32[]{:S(2)}) %collective-permute-start.1) | collective-permute-done | bytes 393248 | tf_op jit(solution)/shard_map/ppermute | solution.py:315
  54.5 3.7 %collective-permute-done.4 = bf16[128,2176]{1,0:T(8,128)(2,1)S(1)} collective-permute-done((bf16[128,2176]{1,0:T(8,128)(2,1)S(1)}, bf16[128,2176]{1,0:T(8,128)(2,1)S(1)}, u32[]{:S(2)}, u32[]{:S(2)}) %collective-permute-start.4) | collective-permute-done | bytes 557088 | tf_op jit(solution)/shard_map/ppermute | solution.py:301
  58.4 5.6 %collective-permute-done.7.w3 = bf16[256,768]{1,0:T(8,128)(2,1)S(1)} collective-permute-done((bf16[256,768]{1,0:T(8,128)(2,1)S(1)}, bf16[256,768]{1,0:T(8,128)(2,1)S(1)}, u32[]{:S(2)}, u32[]{:S(2)}) %collective-permute-start.7) | collective-permute-done | bytes 393248 | tf_op jit(solution)/shard_map/ppermute | solution.py:319
  64.0 0.7 weights.1
  64.8 3.6 %far.1 = (bf16[1024,768]{1,0:T(8,128)(2,1)S(1)}, bf16[1024,768]{1,0:T(8,128)(2,1)S(1)}) custom-call(bf16[512,2176]{1,0:T(8,128)(2,1)S(1)} %collective-permute-done.6.xs.refs_0_, bf16[512,2176]{1,0:T(8,128)(2,1)S(1)} %constant_dynamic-update-slice_fusion.xo.refs_1_, bf16[1024,768]{1,0:T(8,128)(2,1)S(1)} %get-tuple-element.63.w_all, ...), custom_call_target="tpu_custom_call" | custom-call | flops 68719476736 | bytes 12582912 | tf_op jit(solution)/shard_map/far/pallas_call | solution.py:229
  68.4 0.7 collective-permute-done.12.xs.refs_2_
  69.1 3.5 %near.1 = (bf16[1024,768]{1,0:T(8,128)(2,1)S(1)}, bf16[1024,768]{1,0:T(8,128)(2,1)S(1)}) custom-call(bf16[512,2176]{1,0:T(8,128)(2,1)S(1)} %collective-permute-done.12.xs.refs_2_, bf16[512,2176]{1,0:T(8,128)(2,1)S(1)} %pad_maximum_fusion.xo.refs_3_, bf16[1024,768]{1,0:T(8,128)(2,1)S(1)} %get-tuple-element.63.w_all, ...), custom_call_target="tpu_custom_call" | custom-call | flops 68719476736 | bytes 12582912 | tf_op jit(solution)/shard_map/near/pallas_call | solution.py:229
  72.6 1.9 %outer.3 = bf16[256,768]{1,0:T(8,128)(2,1)S(1)} custom-call(s32[2]{0:T(128)S(1)} %pad_add_fusion.place, bf16[512,2176]{1,0:T(8,128)(2,1)S(1)} %collective-permute-done.6.xs.refs_0_, bf16[512,2176]{1,0:T(8,128)(2,1)S(1)} %constant_dynamic-update-slice_fusion.xo.refs_1_, bf16[512,2176]{1,0:T(8,128)(2,1)S(1)} %collective-permute-done.12.xs.refs_2_, ...), custom_call_target="tpu_custom_call" | custom-call | flops 68719476736 | bytes 12582912 | tf_op jit(solution)/shard_map/outer/pallas_call | solution.py:265
  74.5 0.3 collective-permute-start.14
  74.9 1.8 %far_tokens.1 = (bf16[512,1024]{1,0:T(8,128)(2,1)S(1)}, bf16[512,1024]{1,0:T(8,128)(2,1)S(1)}) custom-call(bf16[1024,768]{1,0:T(8,128)(2,1)S(1)} %get-tuple-element.71.gw, bf16[1024,768]{1,0:T(8,128)(2,1)S(1)} %get-tuple-element.63.w_all), custom_call_target="tpu_custom_call" | custom-call | flops 1048576 | bytes 12582912 | tf_op jit(solution)/shard_map/far_tokens/pallas_call | solution.py:229
  76.8 3.1 %outer.4 = (bf16[256,768]{1,0:T(8,128)(2,1)S(1)}, bf16[256,768]{1,0:T(8,128)(2,1)S(1)}) custom-call(s32[2]{0:T(128)S(1)} %pad_add_fusion.place, bf16[512,2176]{1,0:T(8,128)(2,1)S(1)} %collective-permute-done.6.xs.refs_0_, bf16[512,2176]{1,0:T(8,128)(2,1)S(1)} %constant_dynamic-update-slice_fusion.xo.refs_1_, ...), custom_call_target="tpu_custom_call" | custom-call | flops 68719476736 | bytes 12582912 | tf_op jit(solution)/shard_map/outer/pallas_call | solution.py:265
  79.9 0.4 add_convert_fusion.7
  80.3 1.6 %collective-permute-start.15 = (bf16[128,1024]{1,0:T(8,128)(2,1)S(1)}, bf16[128,1024]{1,0:T(8,128)(2,1)S(1)}, u32[]{:S(2)}, u32[]{:S(2)}) collective-permute-start(bf16[128,1024]{1,0:T(8,128)(2,1)S(1)} %get-tuple-element.108), channel_id=1, source_target_pairs={{0,2},{1,3},{2,0},{3,1},{4,6},{5,7},{6,4},{7,5},{8,10},{9,11},{10,... | collective-permute-start | bytes 786440 | tf_op jit(solution)/shard_map/ppermute | solution.py:340
  81.9 0.2 collective-permute-start.16
  82.1 1.8 %collective-permute-start.17 = (bf16[128,1024]{1,0:T(8,128)(2,1)S(1)}, bf16[128,1024]{1,0:T(8,128)(2,1)S(1)}, u32[]{:S(2)}, u32[]{:S(2)}) collective-permute-start(bf16[128,1024]{1,0:T(8,128)(2,1)S(1)} %get-tuple-element.106), channel_id=1, source_target_pairs={{0,6},{1,7},{2,4},{3,5},{4,2},{5,3},{6,0},{7,1},{8,14},{9,15},{10,... | collective-permute-start | bytes 786440 | tf_op jit(solution)/shard_map/ppermute | solution.py:340
  83.9 1.7 %collective-permute-start.23 = (bf16[256,768]{1,0:T(8,128)(2,1)S(1)}, bf16[256,768]{1,0:T(8,128)(2,1)S(1)}, u32[]{:S(2)}, u32[]{:S(2)}) collective-permute-start(bf16[256,768]{1,0:T(8,128)(2,1)S(1)} %get-tuple-element.99), channel_id=1, source_target_pairs={{0,8},{8,0},{16,24},{24,16},{1,9},{9,1},{17,25},{25,17},{2,10},{10... | collective-permute-start | bytes 1179656 | tf_op jit(solution)/shard_map/ppermute | solution.py:359
  85.8 1.6 %collective-permute-start.24 = (bf16[256,768]{1,0:T(8,128)(2,1)S(1)}, bf16[256,768]{1,0:T(8,128)(2,1)S(1)}, u32[]{:S(2)}, u32[]{:S(2)}) collective-permute-start(bf16[256,768]{1,0:T(8,128)(2,1)S(1)} %add_convert_fusion), channel_id=1, source_target_pairs={{0,16},{8,24},{16,0},{24,8},{1,17},{9,25},{17,1},{25,9},{2,18},{10... | collective-permute-start | bytes 1179656 | tf_op jit(solution)/shard_map/ppermute | solution.py:365
  87.5 1.8 %near_tokens.1 = (bf16[512,1024]{1,0:T(8,128)(2,1)S(1)}, bf16[512,1024]{1,0:T(8,128)(2,1)S(1)}) custom-call(bf16[1024,768]{1,0:T(8,128)(2,1)S(1)} %get-tuple-element.81.gw, bf16[1024,768]{1,0:T(8,128)(2,1)S(1)} %get-tuple-element.63.w_all), custom_call_target="tpu_custom_call" | custom-call | flops 1048576 | bytes 12582912 | tf_op jit(solution)/shard_map/near_tokens/pallas_call | solution.py:229
  89.3 0.2 collective-permute-done.15
  89.5 6.4 %collective-permute-done.16 = bf16[128,1024]{1,0:T(8,128)(2,1)S(1)} collective-permute-done((bf16[128,1024]{1,0:T(8,128)(2,1)S(1)}, bf16[128,1024]{1,0:T(8,128)(2,1)S(1)}, u32[]{:S(2)}, u32[]{:S(2)}) %collective-permute-start.16) | collective-permute-done | bytes 262176 | tf_op jit(solution)/shard_map/ppermute | solution.py:340
  95.9 1.7 %outer.5.own = bf16[256,768]{1,0:T(8,128)(2,1)S(1)} custom-call(s32[2]{0:T(128)S(1)} %pad_add_fusion.place, bf16[512,2176]{1,0:T(8,128)(2,1)S(1)} %collective-permute-done.6.xs.refs_0_, bf16[512,2176]{1,0:T(8,128)(2,1)S(1)} %constant_dynamic-update-slice_fusion.xo.refs_1_, bf16[512,2176]{1,0:T(8,128)(2,1)S(1)} %collective-permute-done.12.xs.refs_2_, ...), custom_call_target="tpu_custom_call" | custom-call | flops 68719476736 | bytes 12582912 | tf_op jit(solution)/shard_map/outer/pallas_call | solution.py:265
  97.6 0.7 add_convert_fusion.2
  98.3 1.5 %collective-permute-start.21 = (bf16[128,1024]{1,0:T(8,128)(2,1)S(1)}, bf16[128,1024]{1,0:T(8,128)(2,1)S(1)}, u32[]{:S(2)}, u32[]{:S(2)}) collective-permute-start(bf16[128,1024]{1,0:T(8,128)(2,1)S(1)} %get-tuple-element.94), channel_id=1, source_target_pairs={{0,6},{1,7},{2,4},{3,5},{4,2},{5,3},{6,0},{7,1},{8,14},{9,15},{10,... | collective-permute-start | bytes 786440 | tf_op jit(solution)/shard_map/ppermute | solution.py:340
  99.9 0.5 collective-permute-start.20
  100.4 1.5 %collective-permute-start.19 = (bf16[128,1024]{1,0:T(8,128)(2,1)S(1)}, bf16[128,1024]{1,0:T(8,128)(2,1)S(1)}, u32[]{:S(2)}, u32[]{:S(2)}) collective-permute-start(bf16[128,1024]{1,0:T(8,128)(2,1)S(1)} %get-tuple-element.92), channel_id=1, source_target_pairs={{0,2},{1,3},{2,0},{3,1},{4,6},{5,7},{6,4},{7,5},{8,10},{9,11},{10,... | collective-permute-start | bytes 786440 | tf_op jit(solution)/shard_map/ppermute | solution.py:340
  101.9 0.7 collective-permute-done.23.got
  102.6 2.1 %collective-permute-start.22 = (bf16[128,1024]{1,0:T(8,128)(2,1)S(1)}, bf16[128,1024]{1,0:T(8,128)(2,1)S(1)}, u32[]{:S(2)}, u32[]{:S(2)}) collective-permute-start(bf16[128,1024]{1,0:T(8,128)(2,1)S(1)} %get-tuple-element.95), channel_id=1, source_target_pairs={{0,16},{8,24},{16,0},{24,8},{1,17},{9,25},{17,1},{25,9},{2,18},{10... | collective-permute-start | bytes 786440 | tf_op jit(solution)/shard_map/ppermute | solution.py:375
  104.7 6.8 %collective-permute-done.24.far = bf16[256,768]{1,0:T(8,128)(2,1)S(1)} collective-permute-done((bf16[256,768]{1,0:T(8,128)(2,1)S(1)}, bf16[256,768]{1,0:T(8,128)(2,1)S(1)}, u32[]{:S(2)}, u32[]{:S(2)}) %collective-permute-start.24) | collective-permute-done | bytes 393248 | tf_op jit(solution)/shard_map/ppermute | solution.py:365
  111.5 1.0 join.1
  112.5 1.7 %copy.11 = bf16[256,2,768]{2,1,0:T(2,128)(2,1)} copy(bf16[256,2,768]{2,0,1:T(8,128)(2,1)S(1)} %bitcast.13) | data formatting | bytes 1572864
  114.4 2.4 %collective-permute-done.22 = bf16[128,1024]{1,0:T(8,128)(2,1)S(1)} collective-permute-done((bf16[128,1024]{1,0:T(8,128)(2,1)S(1)}, bf16[128,1024]{1,0:T(8,128)(2,1)S(1)}, u32[]{:S(2)}, u32[]{:S(2)}) %collective-permute-start.22) | collective-permute-done | bytes 262176 | tf_op jit(solution)/shard_map/ppermute | solution.py:375
  116.8 0.8 add_convert_fusion.1
  (32 shorter events, 1.1 us)
Async XLA Ops:
  0.6 12.3 %copy-start.1 = (bf16[96,2,1024]{2,1,0:T(2,128)(2,1)S(1)}, bf16[96,2,1024]{2,1,0:T(2,128)(2,1)}, u32[]{:S(2)}) copy-start(bf16[96,2,1024]{2,1,0:T(2,128)(2,1)} %param.11) | copy-start | bytes 1179652
  2.6 36.4 %copy-start = (bf16[128,2176]{1,0:T(8,128)(2,1)S(1)}, bf16[128,2176]{1,0:T(8,128)(2,1)}, u32[]{:S(2)}) copy-start(bf16[128,2176]{1,0:T(8,128)(2,1)} %payload.1) | copy-start | bytes 1671172
  2.7 28.9 %collective-permute-start = (bf16[128,2176]{1,0:T(8,128)(2,1)}, bf16[128,2176]{1,0:T(8,128)(2,1)S(1)}, u32[]{:S(2)}, u32[]{:S(2)}) collective-permute-start(bf16[128,2176]{1,0:T(8,128)(2,1)} %payload.1), channel_id=1, source_target_pairs={{0,16},{8,24},{16,0},{24,8},{1,17},{9,25},{17,1},{25,9},{2,18},{10... | collective-permute-start | bytes 1671176 | tf_op jit(solution)/shard_map/ppermute | solution.py:309
  6.7 27.9 %collective-permute-start.11 = (bf16[128,2176]{1,0:T(8,128)(2,1)}, bf16[128,2176]{1,0:T(8,128)(2,1)S(1)}, u32[]{:S(2)}, u32[]{:S(2)}) collective-permute-start(bf16[128,2176]{1,0:T(8,128)(2,1)} %payload.1), channel_id=1, source_target_pairs={{0,6},{1,7},{2,4},{3,5},{4,2},{5,3},{6,0},{7,1},{8,14},{9,15},{10,... | collective-permute-start | bytes 1671176 | tf_op jit(solution)/shard_map/ppermute | solution.py:301
  9.1 25.9 %collective-permute-start.10 = (bf16[128,2176]{1,0:T(8,128)(2,1)}, bf16[128,2176]{1,0:T(8,128)(2,1)S(1)}, u32[]{:S(2)}, u32[]{:S(2)}) collective-permute-start(bf16[128,2176]{1,0:T(8,128)(2,1)} %payload.1), channel_id=1, source_target_pairs={{0,4},{1,5},{2,6},{3,7},{4,0},{5,1},{6,2},{7,3},{8,12},{9,13},{10,... | collective-permute-start | bytes 1671176 | tf_op jit(solution)/shard_map/ppermute | solution.py:301
  9.6 25.4 %collective-permute-start.9 = (bf16[128,2176]{1,0:T(8,128)(2,1)}, bf16[128,2176]{1,0:T(8,128)(2,1)S(1)}, u32[]{:S(2)}, u32[]{:S(2)}) collective-permute-start(bf16[128,2176]{1,0:T(8,128)(2,1)} %payload.1), channel_id=1, source_target_pairs={{0,2},{1,3},{2,0},{3,1},{4,6},{5,7},{6,4},{7,5},{8,10},{9,11},{10,... | collective-permute-start | bytes 1671176 | tf_op jit(solution)/shard_map/ppermute | solution.py:301
  10.2 17.2 %collective-permute-start.8 = (bf16[96,2,1024]{2,1,0:T(2,128)(2,1)}, bf16[96,2,1024]{2,1,0:T(2,128)(2,1)}, u32[]{:S(2)}, u32[]{:S(2)}) collective-permute-start(bf16[96,2,1024]{2,1,0:T(2,128)(2,1)} %param.11), channel_id=1, source_target_pairs={{0,8},{8,0},{16,24},{24,16},{1,9},{9,1},{17,25},{25,17},{2,10},{10... | collective-permute-start | bytes 1179656 | tf_op jit(solution)/shard_map/ppermute | solution.py:310
  31.5 22.9 %collective-permute-start.3 = (bf16[128,2176]{1,0:T(8,128)(2,1)S(1)}, bf16[128,2176]{1,0:T(8,128)(2,1)S(1)}, u32[]{:S(2)}, u32[]{:S(2)}) collective-permute-start(bf16[128,2176]{1,0:T(8,128)(2,1)S(1)} %collective-permute-done), channel_id=1, source_target_pairs={{0,2},{1,3},{2,0},{3,1},{4,6},{5,7},{6,4},{7,5},{8,10},{9,11},{10,... | collective-permute-start | bytes 1671176 | tf_op jit(solution)/shard_map/ppermute | solution.py:301
  33.0 25.2 %collective-permute-start.4 = (bf16[128,2176]{1,0:T(8,128)(2,1)S(1)}, bf16[128,2176]{1,0:T(8,128)(2,1)S(1)}, u32[]{:S(2)}, u32[]{:S(2)}) collective-permute-start(bf16[128,2176]{1,0:T(8,128)(2,1)S(1)} %collective-permute-done), channel_id=1, source_target_pairs={{0,4},{1,5},{2,6},{3,7},{4,0},{5,1},{6,2},{7,3},{8,12},{9,13},{10,... | collective-permute-start | bytes 1671176 | tf_op jit(solution)/shard_map/ppermute | solution.py:301
  34.5 23.7 %collective-permute-start.5 = (bf16[128,2176]{1,0:T(8,128)(2,1)S(1)}, bf16[128,2176]{1,0:T(8,128)(2,1)S(1)}, u32[]{:S(2)}, u32[]{:S(2)}) collective-permute-start(bf16[128,2176]{1,0:T(8,128)(2,1)S(1)} %collective-permute-done), channel_id=1, source_target_pairs={{0,6},{1,7},{2,4},{3,5},{4,2},{5,3},{6,0},{7,1},{8,14},{9,15},{10,... | collective-permute-start | bytes 1671176 | tf_op jit(solution)/shard_map/ppermute | solution.py:301
  35.0 19.3 %collective-permute-start.1 = (bf16[256,768]{1,0:T(8,128)(2,1)S(1)}, bf16[256,768]{1,0:T(8,128)(2,1)S(1)}, u32[]{:S(2)}, u32[]{:S(2)}) collective-permute-start(bf16[256,768]{1,0:T(8,128)(2,1)S(1)} %get-tuple-element.54), channel_id=1, source_target_pairs={{0,16},{8,24},{16,0},{24,8},{1,17},{9,25},{17,1},{25,9},{2,18},{10... | collective-permute-start | bytes 1179656 | tf_op jit(solution)/shard_map/ppermute | solution.py:315
  35.0 19.3 %collective-permute-start.2 = (bf16[256,768]{1,0:T(8,128)(2,1)S(1)}, bf16[256,768]{1,0:T(8,128)(2,1)S(1)}, u32[]{:S(2)}, u32[]{:S(2)}) collective-permute-start(bf16[256,768]{1,0:T(8,128)(2,1)S(1)} %get-tuple-element.55.w0), channel_id=1, source_target_pairs={{0,8},{8,0},{16,24},{24,16},{1,9},{9,1},{17,25},{25,17},{2,10},{10... | collective-permute-start | bytes 1179656 | tf_op jit(solution)/shard_map/ppermute | solution.py:316
  54.4 9.6 %collective-permute-start.7 = (bf16[256,768]{1,0:T(8,128)(2,1)S(1)}, bf16[256,768]{1,0:T(8,128)(2,1)S(1)}, u32[]{:S(2)}, u32[]{:S(2)}) collective-permute-start(bf16[256,768]{1,0:T(8,128)(2,1)S(1)} %collective-permute-done.1.w2), channel_id=1, source_target_pairs={{0,8},{8,0},{16,24},{24,16},{1,9},{9,1},{17,25},{25,17},{2,10},{10... | collective-permute-start | bytes 1179656 | tf_op jit(solution)/shard_map/ppermute | solution.py:319
  58.3 6.4 %collective-permute-start.6 = (bf16[512,2176]{1,0:T(8,128)(2,1)S(1)}, bf16[512,2176]{1,0:T(8,128)(2,1)S(1)}, u32[]{:S(2)}, u32[]{:S(2)}) collective-permute-start(bf16[512,2176]{1,0:T(8,128)(2,1)S(1)} %constant_dynamic-update-slice_fusion.xo.refs_1_), channel_id=1, source_target_pairs={{0,1},{1,0},{2,3},{3,2},{4,5},{5,4},{6,7},{7,6},{8,9},{9,8},{10,11... | collective-permute-start | bytes 6684680 | tf_op jit(solution)/shard_map/ppermute | solution.py:321
  64.7 4.4 %collective-permute-start.12 = (bf16[512,2176]{1,0:T(8,128)(2,1)S(1)}, bf16[512,2176]{1,0:T(8,128)(2,1)S(1)}, u32[]{:S(2)}, u32[]{:S(2)}) collective-permute-start(bf16[512,2176]{1,0:T(8,128)(2,1)S(1)} %pad_maximum_fusion.xo.refs_3_), channel_id=1, source_target_pairs={{0,1},{1,0},{2,3},{3,2},{4,5},{5,4},{6,7},{7,6},{8,9},{9,8},{10,11... | collective-permute-start | bytes 6684680 | tf_op jit(solution)/shard_map/ppermute | solution.py:334
  74.5 11.2 %collective-permute-start.14 = (bf16[256,768]{1,0:T(8,128)(2,1)S(1)}, bf16[256,768]{1,0:T(8,128)(2,1)S(1)}, u32[]{:S(2)}, u32[]{:S(2)}) collective-permute-start(bf16[256,768]{1,0:T(8,128)(2,1)S(1)} %outer.3), channel_id=1, source_target_pairs={{0,8},{8,0},{16,24},{24,16},{1,9},{9,1},{17,25},{25,17},{2,10},{10... | collective-permute-start | bytes 1179656 | tf_op jit(solution)/shard_map/ppermute | solution.py:353
  76.7 3.2 %collective-permute-start.13 = (bf16[512,1024]{1,0:T(8,128)(2,1)S(1)}, bf16[512,1024]{1,0:T(8,128)(2,1)S(1)}, u32[]{:S(2)}, u32[]{:S(2)}) collective-permute-start(bf16[512,1024]{1,0:T(8,128)(2,1)S(1)} %get-tuple-element.75), channel_id=1, source_target_pairs={{0,1},{1,0},{2,3},{3,2},{4,5},{5,4},{6,7},{7,6},{8,9},{9,8},{10,11... | collective-permute-start | bytes 3145736 | tf_op jit(solution)/shard_map/ppermute | solution.py:356
  80.3 9.2 %collective-permute-start.15 = (bf16[128,1024]{1,0:T(8,128)(2,1)S(1)}, bf16[128,1024]{1,0:T(8,128)(2,1)S(1)}, u32[]{:S(2)}, u32[]{:S(2)}) collective-permute-start(bf16[128,1024]{1,0:T(8,128)(2,1)S(1)} %get-tuple-element.108), channel_id=1, source_target_pairs={{0,2},{1,3},{2,0},{3,1},{4,6},{5,7},{6,4},{7,5},{8,10},{9,11},{10,... | collective-permute-start | bytes 786440 | tf_op jit(solution)/shard_map/ppermute | solution.py:340
  81.9 14.0 %collective-permute-start.16 = (bf16[128,1024]{1,0:T(8,128)(2,1)S(1)}, bf16[128,1024]{1,0:T(8,128)(2,1)S(1)}, u32[]{:S(2)}, u32[]{:S(2)}) collective-permute-start(bf16[128,1024]{1,0:T(8,128)(2,1)S(1)} %get-tuple-element.107), channel_id=1, source_target_pairs={{0,4},{1,5},{2,6},{3,7},{4,0},{5,1},{6,2},{7,3},{8,12},{9,13},{10,... | collective-permute-start | bytes 786440 | tf_op jit(solution)/shard_map/ppermute | solution.py:340
  82.1 13.8 %collective-permute-start.17 = (bf16[128,1024]{1,0:T(8,128)(2,1)S(1)}, bf16[128,1024]{1,0:T(8,128)(2,1)S(1)}, u32[]{:S(2)}, u32[]{:S(2)}) collective-permute-start(bf16[128,1024]{1,0:T(8,128)(2,1)S(1)} %get-tuple-element.106), channel_id=1, source_target_pairs={{0,6},{1,7},{2,4},{3,5},{4,2},{5,3},{6,0},{7,1},{8,14},{9,15},{10,... | collective-permute-start | bytes 786440 | tf_op jit(solution)/shard_map/ppermute | solution.py:340
  83.9 18.7 %collective-permute-start.23 = (bf16[256,768]{1,0:T(8,128)(2,1)S(1)}, bf16[256,768]{1,0:T(8,128)(2,1)S(1)}, u32[]{:S(2)}, u32[]{:S(2)}) collective-permute-start(bf16[256,768]{1,0:T(8,128)(2,1)S(1)} %get-tuple-element.99), channel_id=1, source_target_pairs={{0,8},{8,0},{16,24},{24,16},{1,9},{9,1},{17,25},{25,17},{2,10},{10... | collective-permute-start | bytes 1179656 | tf_op jit(solution)/shard_map/ppermute | solution.py:359
  85.8 25.7 %collective-permute-start.24 = (bf16[256,768]{1,0:T(8,128)(2,1)S(1)}, bf16[256,768]{1,0:T(8,128)(2,1)S(1)}, u32[]{:S(2)}, u32[]{:S(2)}) collective-permute-start(bf16[256,768]{1,0:T(8,128)(2,1)S(1)} %add_convert_fusion), channel_id=1, source_target_pairs={{0,16},{8,24},{16,0},{24,8},{1,17},{9,25},{17,1},{25,9},{2,18},{10... | collective-permute-start | bytes 1179656 | tf_op jit(solution)/shard_map/ppermute | solution.py:365
  89.5 8.1 %collective-permute-start.18 = (bf16[512,1024]{1,0:T(8,128)(2,1)S(1)}, bf16[512,1024]{1,0:T(8,128)(2,1)S(1)}, u32[]{:S(2)}, u32[]{:S(2)}) collective-permute-start(bf16[512,1024]{1,0:T(8,128)(2,1)S(1)} %get-tuple-element.88), channel_id=1, source_target_pairs={{0,1},{1,0},{2,3},{3,2},{4,5},{5,4},{6,7},{7,6},{8,9},{9,8},{10,11... | collective-permute-start | bytes 3145736 | tf_op jit(solution)/shard_map/ppermute | solution.py:368
  98.3 15.9 %collective-permute-start.21 = (bf16[128,1024]{1,0:T(8,128)(2,1)S(1)}, bf16[128,1024]{1,0:T(8,128)(2,1)S(1)}, u32[]{:S(2)}, u32[]{:S(2)}) collective-permute-start(bf16[128,1024]{1,0:T(8,128)(2,1)S(1)} %get-tuple-element.94), channel_id=1, source_target_pairs={{0,6},{1,7},{2,4},{3,5},{4,2},{5,3},{6,0},{7,1},{8,14},{9,15},{10,... | collective-permute-start | bytes 786440 | tf_op jit(solution)/shard_map/ppermute | solution.py:340
  99.9 14.3 %collective-permute-start.20 = (bf16[128,1024]{1,0:T(8,128)(2,1)S(1)}, bf16[128,1024]{1,0:T(8,128)(2,1)S(1)}, u32[]{:S(2)}, u32[]{:S(2)}) collective-permute-start(bf16[128,1024]{1,0:T(8,128)(2,1)S(1)} %get-tuple-element.93), channel_id=1, source_target_pairs={{0,4},{1,5},{2,6},{3,7},{4,0},{5,1},{6,2},{7,3},{8,12},{9,13},{10,... | collective-permute-start | bytes 786440 | tf_op jit(solution)/shard_map/ppermute | solution.py:340
  100.4 13.8 %collective-permute-start.19 = (bf16[128,1024]{1,0:T(8,128)(2,1)S(1)}, bf16[128,1024]{1,0:T(8,128)(2,1)S(1)}, u32[]{:S(2)}, u32[]{:S(2)}) collective-permute-start(bf16[128,1024]{1,0:T(8,128)(2,1)S(1)} %get-tuple-element.92), channel_id=1, source_target_pairs={{0,2},{1,3},{2,0},{3,1},{4,6},{5,7},{6,4},{7,5},{8,10},{9,11},{10,... | collective-permute-start | bytes 786440 | tf_op jit(solution)/shard_map/ppermute | solution.py:340
  102.6 14.2 %collective-permute-start.22 = (bf16[128,1024]{1,0:T(8,128)(2,1)S(1)}, bf16[128,1024]{1,0:T(8,128)(2,1)S(1)}, u32[]{:S(2)}, u32[]{:S(2)}) collective-permute-start(bf16[128,1024]{1,0:T(8,128)(2,1)S(1)} %get-tuple-element.95), channel_id=1, source_target_pairs={{0,16},{8,24},{16,0},{24,8},{1,17},{9,25},{17,1},{25,9},{2,18},{10... | collective-permute-start | bytes 786440 | tf_op jit(solution)/shard_map/ppermute | solution.py:375

commit v7 on v5

--- a/solution.py
+++ b/solution.py
@@ -84,10 +84,15 @@
 TN = (((0,), (0,)), ((), ()))
 
 
-def payload_kernel(tokens, cotangent, ids, weights, out):
+def payload_kernel(tokens, cotangent, ids, weights, out, meta, sems):
     count, width = tokens.shape
-    out[:, :width] = tokens[...]
-    out[:, width : 2 * width] = cotangent[...]
+    copies = [
+        pltpu.make_async_copy(tokens, out.at[:, pl.ds(0, width)], sems.at[0]),
+        pltpu.make_async_copy(cotangent, out.at[:, pl.ds(width, width)], sems.at[1]),
+        pltpu.make_async_copy(meta, out.at[:, pl.ds(2 * width, LANES)], sems.at[2]),
+    ]
+    copies[0].start()
+    copies[1].start()
     lane = lax.broadcasted_iota(jnp.int32, (LANES, count), 0)
     n = LANES // 8
     total = jnp.zeros((LANES, count), jnp.float32)
@@ -98,15 +103,22 @@
         routed = routed + jnp.where(here, 1.0, 0.0)
     top = total.astype(jnp.bfloat16).astype(jnp.float32)
     rest = jnp.where(lane < 2 * n, total - top, jnp.where(lane < 3 * n, routed, 0.0))
-    out[:, 2 * width :] = jnp.where(lane < n, top, rest).T.astype(jnp.bfloat16)
+    meta[...] = jnp.where(lane < n, top, rest).T.astype(jnp.bfloat16)
+    copies[2].start()
+    for copy in copies:
+        copy.wait()
 
 
 def payload_of(tokens, cotangent, ids, weights):
     count, width = tokens.shape
     return pl.pallas_call(
         payload_kernel,
+        in_specs=[pl.BlockSpec(memory_space=pl.ANY)] * 2 + [pl.BlockSpec(memory_space=pltpu.VMEM)] * 2,
+        out_specs=pl.BlockSpec(memory_space=pl.ANY),
+        scratch_shapes=[pltpu.VMEM((count, LANES), jnp.bfloat16), pltpu.SemaphoreType.DMA((3,))],
         out_shape=jax.ShapeDtypeStruct((count, 2 * width + LANES), jnp.bfloat16),
         cost_estimate=pl.CostEstimate(flops=1 << 20, bytes_accessed=2 << 20, transcendentals=0),
+        compiler_params=pltpu.CompilerParams(vmem_limit_bytes=60 * 2**20),
         name="payload",
     )(tokens, cotangent, ids.T, weights.T)
 

time: 118 us -> 134 us (1.14)
  Pallas kernels: 21.9 us -> 37.6 us
    pallas_call x1, Pallas kernels: 2.01 us -> 17.8 us  [payload_of(): pl.pallas_call(payload_kernel, in_specs=[pl.BlockSpec(memory_space=pl.ANY...]
  transfers between devices with their start and end apart: 25 -> 25, of which waited for: 12 -> 12; matrix products, arithmetic and copies ran while one was open for 5% -> 4% of each run, Pallas kernels for 12% -> 11%
where the time goes in v7:
time: 134 us; the launch traced here: 133 us
  waiting for transfers between devices  58.8 us (44%)
  Pallas kernels  37.6 us (28%)
  starting transfers between devices  29.5 us (22%)
  local copies, waits for them, and re-layouts  4.26 us (3%)
  other arithmetic  2.37 us (2%)
    pallas_call x1, Pallas kernels, payload_of(): pl.pallas_call(payload_kernel, in_specs=[pl.BlockSpec(memory_space=pl.ANY...  17.8 us
    ppermute x1, waiting for transfers between devices, by_tokens(): w2 = lax.ppermute(given, 'dp', across)  15.1 us
    ppermute x1, waiting for transfers between devices, by_tokens(): down1 = lax.ppermute(weight_down, 'dp', beside)  13.4 us
    pallas_call x5, Pallas kernels, vmem_call(): pl.pallas_call(kernel, in_specs=specs, out_specs=[vmem] * len(outs), out_...  11.4 us
    ppermute x6, waiting for transfers between devices, back_hops(): lax.ppermute(t, 'expert', hop)  7.33 us
    ppermute x6, starting transfers between devices, back_hops(): lax.ppermute(t, 'expert', hop)  7.11 us
    ppermute x6, starting transfers between devices, spread(): return [lax.ppermute(x, 'expert', hop) for hop in hops]  6.98 us
    pallas_call x3, Pallas kernels, outer(): pl.pallas_call(functools.partial(outer_kernel, scale, len(gs), count), gr...  6.69 us
  transfers between devices with their start and end apart: 25, of which 12 were waited for; matrix products, arithmetic and copies ran while one was open for 4% of the time, Pallas kernels for 11%

profile of v7, /device:TPU:0, one launch (start us, length us, event | category | flops | bytes accessed | tf_op | source)
XLA Modules:
  0.0 133.5 jit_solution(15945397963851356752)
XLA Ops:
  0.6 17.8 %payload.1 = bf16[128,2176]{1,0:T(8,128)(2,1)} custom-call(bf16[128,1024]{1,0:T(8,128)(2,1)} %tokens.1, bf16[128,1024]{1,0:T(8,128)(2,1)} %cotangent.1, s32[8,128]{1,0:T(8,128)} %bitcast.17, f32[8,128]{1,0:T(8,128)} %bitcast.18), custom_call_target="tpu_custom_call" | custom-call | flops 1048576 | bytes 2097152 | tf_op jit(solution)/shard_map/payload/pallas_call | solution.py:114
  18.4 4.1 %collective-permute-start = (bf16[128,2176]{1,0:T(8,128)(2,1)}, bf16[128,2176]{1,0:T(8,128)(2,1)S(1)}, u32[]{:S(2)}, u32[]{:S(2)}) collective-permute-start(bf16[128,2176]{1,0:T(8,128)(2,1)} %payload.1), channel_id=1, source_target_pairs={{0,16},{8,24},{16,0},{24,8},{1,17},{9,25},{17,1},{25,9},{2,18},{10... | collective-permute-start | bytes 1671176 | tf_op jit(solution)/shard_map/ppermute | solution.py:321
  22.5 2.4 %collective-permute-start.11 = (bf16[128,2176]{1,0:T(8,128)(2,1)}, bf16[128,2176]{1,0:T(8,128)(2,1)S(1)}, u32[]{:S(2)}, u32[]{:S(2)}) collective-permute-start(bf16[128,2176]{1,0:T(8,128)(2,1)} %payload.1), channel_id=1, source_target_pairs={{0,6},{1,7},{2,4},{3,5},{4,2},{5,3},{6,0},{7,1},{8,14},{9,15},{10,... | collective-permute-start | bytes 1671176 | tf_op jit(solution)/shard_map/ppermute | solution.py:313
  25.0 0.5 collective-permute-start.10
  25.5 0.5 collective-permute-start.9
  26.0 1.6 %collective-permute-start.8 = (bf16[96,2,1024]{2,1,0:T(2,128)(2,1)}, bf16[96,2,1024]{2,1,0:T(2,128)(2,1)}, u32[]{:S(2)}, u32[]{:S(2)}) collective-permute-start(bf16[96,2,1024]{2,1,0:T(2,128)(2,1)} %param.11), channel_id=1, source_target_pairs={{0,8},{8,0},{16,24},{24,16},{1,9},{9,1},{17,25},{25,17},{2,10},{10... | collective-permute-start | bytes 1179656 | tf_op jit(solution)/shard_map/ppermute | solution.py:322
  27.6 1.2 copy.13
  29.0 0.8 halves.1
  29.8 13.4 %collective-permute-done.8 = bf16[96,2,1024]{2,1,0:T(2,128)(2,1)} collective-permute-done((bf16[96,2,1024]{2,1,0:T(2,128)(2,1)}, bf16[96,2,1024]{2,1,0:T(2,128)(2,1)}, u32[]{:S(2)}, u32[]{:S(2)}) %collective-permute-start.8) | collective-permute-done | bytes 393248 | tf_op jit(solution)/shard_map/ppermute | solution.py:322
  43.2 1.1 copy.10
  44.3 3.0 %collective-permute-done = bf16[128,2176]{1,0:T(8,128)(2,1)S(1)} collective-permute-done((bf16[128,2176]{1,0:T(8,128)(2,1)}, bf16[128,2176]{1,0:T(8,128)(2,1)S(1)}, u32[]{:S(2)}, u32[]{:S(2)}) %collective-permute-start) | collective-permute-done | bytes 557088 | tf_op jit(solution)/shard_map/ppermute | solution.py:321
  47.3 1.5 %collective-permute-start.3 = (bf16[128,2176]{1,0:T(8,128)(2,1)S(1)}, bf16[128,2176]{1,0:T(8,128)(2,1)S(1)}, u32[]{:S(2)}, u32[]{:S(2)}) collective-permute-start(bf16[128,2176]{1,0:T(8,128)(2,1)S(1)} %collective-permute-done), channel_id=1, source_target_pairs={{0,2},{1,3},{2,0},{3,1},{4,6},{5,7},{6,4},{7,5},{8,10},{9,11},{10,... | collective-permute-start | bytes 1671176 | tf_op jit(solution)/shard_map/ppermute | solution.py:313
  48.8 1.5 %collective-permute-start.4 = (bf16[128,2176]{1,0:T(8,128)(2,1)S(1)}, bf16[128,2176]{1,0:T(8,128)(2,1)S(1)}, u32[]{:S(2)}, u32[]{:S(2)}) collective-permute-start(bf16[128,2176]{1,0:T(8,128)(2,1)S(1)} %collective-permute-done), channel_id=1, source_target_pairs={{0,4},{1,5},{2,6},{3,7},{4,0},{5,1},{6,2},{7,3},{8,12},{9,13},{10,... | collective-permute-start | bytes 1671176 | tf_op jit(solution)/shard_map/ppermute | solution.py:313
  50.4 0.4 collective-permute-start.5
  50.8 4.1 %collective-permute-start.2 = (bf16[256,768]{1,0:T(8,128)(2,1)S(1)}, bf16[256,768]{1,0:T(8,128)(2,1)S(1)}, u32[]{:S(2)}, u32[]{:S(2)}) collective-permute-start(bf16[256,768]{1,0:T(8,128)(2,1)S(1)} %get-tuple-element.55.w0), channel_id=1, source_target_pairs={{0,8},{8,0},{16,24},{24,16},{1,9},{9,1},{17,25},{25,17},{2,10},{10... | collective-permute-start | bytes 1179656 | tf_op jit(solution)/shard_map/ppermute | solution.py:328
  54.9 0.2 pad_maximum_fusion.xo.refs_3_
  55.1 15.1 %collective-permute-done.1.w2 = bf16[256,768]{1,0:T(8,128)(2,1)S(1)} collective-permute-done((bf16[256,768]{1,0:T(8,128)(2,1)S(1)}, bf16[256,768]{1,0:T(8,128)(2,1)S(1)}, u32[]{:S(2)}, u32[]{:S(2)}) %collective-permute-start.1) | collective-permute-done | bytes 393248 | tf_op jit(solution)/shard_map/ppermute | solution.py:327
  70.3 3.7 %collective-permute-done.4 = bf16[128,2176]{1,0:T(8,128)(2,1)S(1)} collective-permute-done((bf16[128,2176]{1,0:T(8,128)(2,1)S(1)}, bf16[128,2176]{1,0:T(8,128)(2,1)S(1)}, u32[]{:S(2)}, u32[]{:S(2)}) %collective-permute-start.4) | collective-permute-done | bytes 557088 | tf_op jit(solution)/shard_map/ppermute | solution.py:313
  74.2 5.6 %collective-permute-done.7.w3 = bf16[256,768]{1,0:T(8,128)(2,1)S(1)} collective-permute-done((bf16[256,768]{1,0:T(8,128)(2,1)S(1)}, bf16[256,768]{1,0:T(8,128)(2,1)S(1)}, u32[]{:S(2)}, u32[]{:S(2)}) %collective-permute-start.7) | collective-permute-done | bytes 393248 | tf_op jit(solution)/shard_map/ppermute | solution.py:331
  79.8 0.7 weights.1
  80.7 3.6 %far.1 = (bf16[1024,768]{1,0:T(8,128)(2,1)S(1)}, bf16[1024,768]{1,0:T(8,128)(2,1)S(1)}) custom-call(bf16[512,2176]{1,0:T(8,128)(2,1)S(1)} %collective-permute-done.6.xs.refs_0_, bf16[512,2176]{1,0:T(8,128)(2,1)S(1)} %constant_dynamic-update-slice_fusion.xo.refs_1_, bf16[1024,768]{1,0:T(8,128)(2,1)S(1)} %get-tuple-element.63.w_all, ...), custom_call_target="tpu_custom_call" | custom-call | flops 68719476736 | bytes 12582912 | tf_op jit(solution)/shard_map/far/pallas_call | solution.py:241
  84.3 0.7 collective-permute-done.12.xs.refs_2_
  85.0 3.5 %near.1 = (bf16[1024,768]{1,0:T(8,128)(2,1)S(1)}, bf16[1024,768]{1,0:T(8,128)(2,1)S(1)}) custom-call(bf16[512,2176]{1,0:T(8,128)(2,1)S(1)} %collective-permute-done.12.xs.refs_2_, bf16[512,2176]{1,0:T(8,128)(2,1)S(1)} %pad_maximum_fusion.xo.refs_3_, bf16[1024,768]{1,0:T(8,128)(2,1)S(1)} %get-tuple-element.63.w_all, ...), custom_call_target="tpu_custom_call" | custom-call | flops 68719476736 | bytes 12582912 | tf_op jit(solution)/shard_map/near/pallas_call | solution.py:241
  88.5 1.9 %outer.3 = bf16[256,768]{1,0:T(8,128)(2,1)S(1)} custom-call(s32[2]{0:T(128)S(1)} %pad_add_fusion.place, bf16[512,2176]{1,0:T(8,128)(2,1)S(1)} %collective-permute-done.6.xs.refs_0_, bf16[512,2176]{1,0:T(8,128)(2,1)S(1)} %constant_dynamic-update-slice_fusion.xo.refs_1_, bf16[512,2176]{1,0:T(8,128)(2,1)S(1)} %collective-permute-done.12.xs.refs_2_, ...), custom_call_target="tpu_custom_call" | custom-call | flops 68719476736 | bytes 12582912 | tf_op jit(solution)/shard_map/outer/pallas_call | solution.py:277
  90.4 0.4 collective-permute-start.14
  90.7 1.8 %far_tokens.1 = (bf16[512,1024]{1,0:T(8,128)(2,1)S(1)}, bf16[512,1024]{1,0:T(8,128)(2,1)S(1)}) custom-call(bf16[1024,768]{1,0:T(8,128)(2,1)S(1)} %get-tuple-element.71.gw, bf16[1024,768]{1,0:T(8,128)(2,1)S(1)} %get-tuple-element.63.w_all), custom_call_target="tpu_custom_call" | custom-call | flops 1048576 | bytes 12582912 | tf_op jit(solution)/shard_map/far_tokens/pallas_call | solution.py:241
  92.6 3.1 %outer.4 = (bf16[256,768]{1,0:T(8,128)(2,1)S(1)}, bf16[256,768]{1,0:T(8,128)(2,1)S(1)}) custom-call(s32[2]{0:T(128)S(1)} %pad_add_fusion.place, bf16[512,2176]{1,0:T(8,128)(2,1)S(1)} %collective-permute-done.6.xs.refs_0_, bf16[512,2176]{1,0:T(8,128)(2,1)S(1)} %constant_dynamic-update-slice_fusion.xo.refs_1_, ...), custom_call_target="tpu_custom_call" | custom-call | flops 68719476736 | bytes 12582912 | tf_op jit(solution)/shard_map/outer/pallas_call | solution.py:277
  95.7 1.8 %collective-permute-start.23 = (bf16[256,768]{1,0:T(8,128)(2,1)S(1)}, bf16[256,768]{1,0:T(8,128)(2,1)S(1)}, u32[]{:S(2)}, u32[]{:S(2)}) collective-permute-start(bf16[256,768]{1,0:T(8,128)(2,1)S(1)} %get-tuple-element.99), channel_id=1, source_target_pairs={{0,8},{8,0},{16,24},{24,16},{1,9},{9,1},{17,25},{25,17},{2,10},{10... | collective-permute-start | bytes 1179656 | tf_op jit(solution)/shard_map/ppermute | solution.py:371
  97.5 0.4 add_convert_fusion.7
  98.0 1.6 %collective-permute-start.15 = (bf16[128,1024]{1,0:T(8,128)(2,1)S(1)}, bf16[128,1024]{1,0:T(8,128)(2,1)S(1)}, u32[]{:S(2)}, u32[]{:S(2)}) collective-permute-start(bf16[128,1024]{1,0:T(8,128)(2,1)S(1)} %get-tuple-element.108), channel_id=1, source_target_pairs={{0,2},{1,3},{2,0},{3,1},{4,6},{5,7},{6,4},{7,5},{8,10},{9,11},{10,... | collective-permute-start | bytes 786440 | tf_op jit(solution)/shard_map/ppermute | solution.py:352
  99.7 1.8 %collective-permute-start.17 = (bf16[128,1024]{1,0:T(8,128)(2,1)S(1)}, bf16[128,1024]{1,0:T(8,128)(2,1)S(1)}, u32[]{:S(2)}, u32[]{:S(2)}) collective-permute-start(bf16[128,1024]{1,0:T(8,128)(2,1)S(1)} %get-tuple-element.106), channel_id=1, source_target_pairs={{0,6},{1,7},{2,4},{3,5},{4,2},{5,3},{6,0},{7,1},{8,14},{9,15},{10,... | collective-permute-start | bytes 786440 | tf_op jit(solution)/shard_map/ppermute | solution.py:352
  101.5 0.9 collective-permute-done.14
  102.5 1.6 %collective-permute-start.24 = (bf16[256,768]{1,0:T(8,128)(2,1)S(1)}, bf16[256,768]{1,0:T(8,128)(2,1)S(1)}, u32[]{:S(2)}, u32[]{:S(2)}) collective-permute-start(bf16[256,768]{1,0:T(8,128)(2,1)S(1)} %add_convert_fusion), channel_id=1, source_target_pairs={{0,16},{8,24},{16,0},{24,8},{1,17},{9,25},{17,1},{25,9},{2,18},{10... | collective-permute-start | bytes 1179656 | tf_op jit(solution)/shard_map/ppermute | solution.py:377
  104.1 1.8 %near_tokens.1 = (bf16[512,1024]{1,0:T(8,128)(2,1)S(1)}, bf16[512,1024]{1,0:T(8,128)(2,1)S(1)}) custom-call(bf16[1024,768]{1,0:T(8,128)(2,1)S(1)} %get-tuple-element.81.gw, bf16[1024,768]{1,0:T(8,128)(2,1)S(1)} %get-tuple-element.63.w_all), custom_call_target="tpu_custom_call" | custom-call | flops 68719476736 | bytes 12582912 | tf_op jit(solution)/shard_map/near_tokens/pallas_call | solution.py:241
  106.0 1.2 collective-permute-done.15
  107.2 6.1 %collective-permute-done.16 = bf16[128,1024]{1,0:T(8,128)(2,1)S(1)} collective-permute-done((bf16[128,1024]{1,0:T(8,128)(2,1)S(1)}, bf16[128,1024]{1,0:T(8,128)(2,1)S(1)}, u32[]{:S(2)}, u32[]{:S(2)}) %collective-permute-start.16) | collective-permute-done | bytes 262176 | tf_op jit(solution)/shard_map/ppermute | solution.py:352
  113.3 1.7 %outer.5.own = bf16[256,768]{1,0:T(8,128)(2,1)S(1)} custom-call(s32[2]{0:T(128)S(1)} %pad_add_fusion.place, bf16[512,2176]{1,0:T(8,128)(2,1)S(1)} %collective-permute-done.6.xs.refs_0_, bf16[512,2176]{1,0:T(8,128)(2,1)S(1)} %constant_dynamic-update-slice_fusion.xo.refs_1_, bf16[512,2176]{1,0:T(8,128)(2,1)S(1)} %collective-permute-done.12.xs.refs_2_, ...), custom_call_target="tpu_custom_call" | custom-call | flops 68719476736 | bytes 12582912 | tf_op jit(solution)/shard_map/outer/pallas_call | solution.py:277
  115.0 0.7 add_convert_fusion.2
  115.7 1.6 %collective-permute-start.21 = (bf16[128,1024]{1,0:T(8,128)(2,1)S(1)}, bf16[128,1024]{1,0:T(8,128)(2,1)S(1)}, u32[]{:S(2)}, u32[]{:S(2)}) collective-permute-start(bf16[128,1024]{1,0:T(8,128)(2,1)S(1)} %get-tuple-element.94), channel_id=1, source_target_pairs={{0,6},{1,7},{2,4},{3,5},{4,2},{5,3},{6,0},{7,1},{8,14},{9,15},{10,... | collective-permute-start | bytes 786440 | tf_op jit(solution)/shard_map/ppermute | solution.py:352
  117.3 0.5 collective-permute-start.20
  117.8 1.5 %collective-permute-start.19 = (bf16[128,1024]{1,0:T(8,128)(2,1)S(1)}, bf16[128,1024]{1,0:T(8,128)(2,1)S(1)}, u32[]{:S(2)}, u32[]{:S(2)}) collective-permute-start(bf16[128,1024]{1,0:T(8,128)(2,1)S(1)} %get-tuple-element.92), channel_id=1, source_target_pairs={{0,2},{1,3},{2,0},{3,1},{4,6},{5,7},{6,4},{7,5},{8,10},{9,11},{10,... | collective-permute-start | bytes 786440 | tf_op jit(solution)/shard_map/ppermute | solution.py:352
  119.3 1.6 %collective-permute-start.22 = (bf16[128,1024]{1,0:T(8,128)(2,1)S(1)}, bf16[128,1024]{1,0:T(8,128)(2,1)S(1)}, u32[]{:S(2)}, u32[]{:S(2)}) collective-permute-start(bf16[128,1024]{1,0:T(8,128)(2,1)S(1)} %get-tuple-element.95), channel_id=1, source_target_pairs={{0,16},{8,24},{16,0},{24,8},{1,17},{9,25},{17,1},{25,9},{2,18},{10... | collective-permute-start | bytes 786440 | tf_op jit(solution)/shard_map/ppermute | solution.py:387
  120.8 6.6 %collective-permute-done.24.far = bf16[256,768]{1,0:T(8,128)(2,1)S(1)} collective-permute-done((bf16[256,768]{1,0:T(8,128)(2,1)S(1)}, bf16[256,768]{1,0:T(8,128)(2,1)S(1)}, u32[]{:S(2)}, u32[]{:S(2)}) %collective-permute-start.24) | collective-permute-done | bytes 393248 | tf_op jit(solution)/shard_map/ppermute | solution.py:377
  127.4 1.0 join.1
  128.4 1.7 %copy.11 = bf16[256,2,768]{2,1,0:T(2,128)(2,1)} copy(bf16[256,2,768]{2,0,1:T(8,128)(2,1)S(1)} %bitcast.13) | data formatting | bytes 1572864
  130.1 0.2 convert_add_fusion
  130.3 2.4 %collective-permute-done.22 = bf16[128,1024]{1,0:T(8,128)(2,1)S(1)} collective-permute-done((bf16[128,1024]{1,0:T(8,128)(2,1)S(1)}, bf16[128,1024]{1,0:T(8,128)(2,1)S(1)}, u32[]{:S(2)}, u32[]{:S(2)}) %collective-permute-start.22) | collective-permute-done | bytes 262176 | tf_op jit(solution)/shard_map/ppermute | solution.py:387
  132.7 0.8 add_convert_fusion.1
  (32 shorter events, 0.9 us)
Async XLA Ops:
  0.6 28.2 %copy-start.1 = (bf16[96,2,1024]{2,1,0:T(2,128)(2,1)S(1)}, bf16[96,2,1024]{2,1,0:T(2,128)(2,1)}, u32[]{:S(2)}) copy-start(bf16[96,2,1024]{2,1,0:T(2,128)(2,1)} %param.11) | copy-start | bytes 1179652
  18.4 36.5 %copy-start = (bf16[128,2176]{1,0:T(8,128)(2,1)S(1)}, bf16[128,2176]{1,0:T(8,128)(2,1)}, u32[]{:S(2)}) copy-start(bf16[128,2176]{1,0:T(8,128)(2,1)} %payload.1) | copy-start | bytes 1671172
  18.4 28.9 %collective-permute-start = (bf16[128,2176]{1,0:T(8,128)(2,1)}, bf16[128,2176]{1,0:T(8,128)(2,1)S(1)}, u32[]{:S(2)}, u32[]{:S(2)}) collective-permute-start(bf16[128,2176]{1,0:T(8,128)(2,1)} %payload.1), channel_id=1, source_target_pairs={{0,16},{8,24},{16,0},{24,8},{1,17},{9,25},{17,1},{25,9},{2,18},{10... | collective-permute-start | bytes 1671176 | tf_op jit(solution)/shard_map/ppermute | solution.py:321
  22.5 27.8 %collective-permute-start.11 = (bf16[128,2176]{1,0:T(8,128)(2,1)}, bf16[128,2176]{1,0:T(8,128)(2,1)S(1)}, u32[]{:S(2)}, u32[]{:S(2)}) collective-permute-start(bf16[128,2176]{1,0:T(8,128)(2,1)} %payload.1), channel_id=1, source_target_pairs={{0,6},{1,7},{2,4},{3,5},{4,2},{5,3},{6,0},{7,1},{8,14},{9,15},{10,... | collective-permute-start | bytes 1671176 | tf_op jit(solution)/shard_map/ppermute | solution.py:313
  25.0 25.8 %collective-permute-start.10 = (bf16[128,2176]{1,0:T(8,128)(2,1)}, bf16[128,2176]{1,0:T(8,128)(2,1)S(1)}, u32[]{:S(2)}, u32[]{:S(2)}) collective-permute-start(bf16[128,2176]{1,0:T(8,128)(2,1)} %payload.1), channel_id=1, source_target_pairs={{0,4},{1,5},{2,6},{3,7},{4,0},{5,1},{6,2},{7,3},{8,12},{9,13},{10,... | collective-permute-start | bytes 1671176 | tf_op jit(solution)/shard_map/ppermute | solution.py:313
  25.5 25.3 %collective-permute-start.9 = (bf16[128,2176]{1,0:T(8,128)(2,1)}, bf16[128,2176]{1,0:T(8,128)(2,1)S(1)}, u32[]{:S(2)}, u32[]{:S(2)}) collective-permute-start(bf16[128,2176]{1,0:T(8,128)(2,1)} %payload.1), channel_id=1, source_target_pairs={{0,2},{1,3},{2,0},{3,1},{4,6},{5,7},{6,4},{7,5},{8,10},{9,11},{10,... | collective-permute-start | bytes 1671176 | tf_op jit(solution)/shard_map/ppermute | solution.py:313
  26.0 17.2 %collective-permute-start.8 = (bf16[96,2,1024]{2,1,0:T(2,128)(2,1)}, bf16[96,2,1024]{2,1,0:T(2,128)(2,1)}, u32[]{:S(2)}, u32[]{:S(2)}) collective-permute-start(bf16[96,2,1024]{2,1,0:T(2,128)(2,1)} %param.11), channel_id=1, source_target_pairs={{0,8},{8,0},{16,24},{24,16},{1,9},{9,1},{17,25},{25,17},{2,10},{10... | collective-permute-start | bytes 1179656 | tf_op jit(solution)/shard_map/ppermute | solution.py:322
  47.3 23.0 %collective-permute-start.3 = (bf16[128,2176]{1,0:T(8,128)(2,1)S(1)}, bf16[128,2176]{1,0:T(8,128)(2,1)S(1)}, u32[]{:S(2)}, u32[]{:S(2)}) collective-permute-start(bf16[128,2176]{1,0:T(8,128)(2,1)S(1)} %collective-permute-done), channel_id=1, source_target_pairs={{0,2},{1,3},{2,0},{3,1},{4,6},{5,7},{6,4},{7,5},{8,10},{9,11},{10,... | collective-permute-start | bytes 1671176 | tf_op jit(solution)/shard_map/ppermute | solution.py:313
  48.8 25.2 %collective-permute-start.4 = (bf16[128,2176]{1,0:T(8,128)(2,1)S(1)}, bf16[128,2176]{1,0:T(8,128)(2,1)S(1)}, u32[]{:S(2)}, u32[]{:S(2)}) collective-permute-start(bf16[128,2176]{1,0:T(8,128)(2,1)S(1)} %collective-permute-done), channel_id=1, source_target_pairs={{0,4},{1,5},{2,6},{3,7},{4,0},{5,1},{6,2},{7,3},{8,12},{9,13},{10,... | collective-permute-start | bytes 1671176 | tf_op jit(solution)/shard_map/ppermute | solution.py:313
  50.4 23.7 %collective-permute-start.5 = (bf16[128,2176]{1,0:T(8,128)(2,1)S(1)}, bf16[128,2176]{1,0:T(8,128)(2,1)S(1)}, u32[]{:S(2)}, u32[]{:S(2)}) collective-permute-start(bf16[128,2176]{1,0:T(8,128)(2,1)S(1)} %collective-permute-done), channel_id=1, source_target_pairs={{0,6},{1,7},{2,4},{3,5},{4,2},{5,3},{6,0},{7,1},{8,14},{9,15},{10,... | collective-permute-start | bytes 1671176 | tf_op jit(solution)/shard_map/ppermute | solution.py:313
  50.8 19.3 %collective-permute-start.1 = (bf16[256,768]{1,0:T(8,128)(2,1)S(1)}, bf16[256,768]{1,0:T(8,128)(2,1)S(1)}, u32[]{:S(2)}, u32[]{:S(2)}) collective-permute-start(bf16[256,768]{1,0:T(8,128)(2,1)S(1)} %get-tuple-element.54), channel_id=1, source_target_pairs={{0,16},{8,24},{16,0},{24,8},{1,17},{9,25},{17,1},{25,9},{2,18},{10... | collective-permute-start | bytes 1179656 | tf_op jit(solution)/shard_map/ppermute | solution.py:327
  50.8 19.4 %collective-permute-start.2 = (bf16[256,768]{1,0:T(8,128)(2,1)S(1)}, bf16[256,768]{1,0:T(8,128)(2,1)S(1)}, u32[]{:S(2)}, u32[]{:S(2)}) collective-permute-start(bf16[256,768]{1,0:T(8,128)(2,1)S(1)} %get-tuple-element.55.w0), channel_id=1, source_target_pairs={{0,8},{8,0},{16,24},{24,16},{1,9},{9,1},{17,25},{25,17},{2,10},{10... | collective-permute-start | bytes 1179656 | tf_op jit(solution)/shard_map/ppermute | solution.py:328
  70.2 9.6 %collective-permute-start.7 = (bf16[256,768]{1,0:T(8,128)(2,1)S(1)}, bf16[256,768]{1,0:T(8,128)(2,1)S(1)}, u32[]{:S(2)}, u32[]{:S(2)}) collective-permute-start(bf16[256,768]{1,0:T(8,128)(2,1)S(1)} %collective-permute-done.1.w2), channel_id=1, source_target_pairs={{0,8},{8,0},{16,24},{24,16},{1,9},{9,1},{17,25},{25,17},{2,10},{10... | collective-permute-start | bytes 1179656 | tf_op jit(solution)/shard_map/ppermute | solution.py:331
  74.2 6.4 %collective-permute-start.6 = (bf16[512,2176]{1,0:T(8,128)(2,1)S(1)}, bf16[512,2176]{1,0:T(8,128)(2,1)S(1)}, u32[]{:S(2)}, u32[]{:S(2)}) collective-permute-start(bf16[512,2176]{1,0:T(8,128)(2,1)S(1)} %constant_dynamic-update-slice_fusion.xo.refs_1_), channel_id=1, source_target_pairs={{0,1},{1,0},{2,3},{3,2},{4,5},{5,4},{6,7},{7,6},{8,9},{9,8},{10,11... | collective-permute-start | bytes 6684680 | tf_op jit(solution)/shard_map/ppermute | solution.py:333
  80.6 4.4 %collective-permute-start.12 = (bf16[512,2176]{1,0:T(8,128)(2,1)S(1)}, bf16[512,2176]{1,0:T(8,128)(2,1)S(1)}, u32[]{:S(2)}, u32[]{:S(2)}) collective-permute-start(bf16[512,2176]{1,0:T(8,128)(2,1)S(1)} %pad_maximum_fusion.xo.refs_3_), channel_id=1, source_target_pairs={{0,1},{1,0},{2,3},{3,2},{4,5},{5,4},{6,7},{7,6},{8,9},{9,8},{10,11... | collective-permute-start | bytes 6684680 | tf_op jit(solution)/shard_map/ppermute | solution.py:346
  90.4 12.0 %collective-permute-start.14 = (bf16[256,768]{1,0:T(8,128)(2,1)S(1)}, bf16[256,768]{1,0:T(8,128)(2,1)S(1)}, u32[]{:S(2)}, u32[]{:S(2)}) collective-permute-start(bf16[256,768]{1,0:T(8,128)(2,1)S(1)} %outer.3), channel_id=1, source_target_pairs={{0,8},{8,0},{16,24},{24,16},{1,9},{9,1},{17,25},{25,17},{2,10},{10... | collective-permute-start | bytes 1179656 | tf_op jit(solution)/shard_map/ppermute | solution.py:365
  92.5 5.0 %collective-permute-start.13 = (bf16[512,1024]{1,0:T(8,128)(2,1)S(1)}, bf16[512,1024]{1,0:T(8,128)(2,1)S(1)}, u32[]{:S(2)}, u32[]{:S(2)}) collective-permute-start(bf16[512,1024]{1,0:T(8,128)(2,1)S(1)} %get-tuple-element.75), channel_id=1, source_target_pairs={{0,1},{1,0},{2,3},{3,2},{4,5},{5,4},{6,7},{7,6},{8,9},{9,8},{10,11... | collective-permute-start | bytes 3145736 | tf_op jit(solution)/shard_map/ppermute | solution.py:368
  95.7 23.5 %collective-permute-start.23 = (bf16[256,768]{1,0:T(8,128)(2,1)S(1)}, bf16[256,768]{1,0:T(8,128)(2,1)S(1)}, u32[]{:S(2)}, u32[]{:S(2)}) collective-permute-start(bf16[256,768]{1,0:T(8,128)(2,1)S(1)} %get-tuple-element.99), channel_id=1, source_target_pairs={{0,8},{8,0},{16,24},{24,16},{1,9},{9,1},{17,25},{25,17},{2,10},{10... | collective-permute-start | bytes 1179656 | tf_op jit(solution)/shard_map/ppermute | solution.py:371
  98.0 9.2 %collective-permute-start.15 = (bf16[128,1024]{1,0:T(8,128)(2,1)S(1)}, bf16[128,1024]{1,0:T(8,128)(2,1)S(1)}, u32[]{:S(2)}, u32[]{:S(2)}) collective-permute-start(bf16[128,1024]{1,0:T(8,128)(2,1)S(1)} %get-tuple-element.108), channel_id=1, source_target_pairs={{0,2},{1,3},{2,0},{3,1},{4,6},{5,7},{6,4},{7,5},{8,10},{9,11},{10,... | collective-permute-start | bytes 786440 | tf_op jit(solution)/shard_map/ppermute | solution.py:352
  99.5 13.8 %collective-permute-start.16 = (bf16[128,1024]{1,0:T(8,128)(2,1)S(1)}, bf16[128,1024]{1,0:T(8,128)(2,1)S(1)}, u32[]{:S(2)}, u32[]{:S(2)}) collective-permute-start(bf16[128,1024]{1,0:T(8,128)(2,1)S(1)} %get-tuple-element.107), channel_id=1, source_target_pairs={{0,4},{1,5},{2,6},{3,7},{4,0},{5,1},{6,2},{7,3},{8,12},{9,13},{10,... | collective-permute-start | bytes 786440 | tf_op jit(solution)/shard_map/ppermute | solution.py:352
  99.7 13.6 %collective-permute-start.17 = (bf16[128,1024]{1,0:T(8,128)(2,1)S(1)}, bf16[128,1024]{1,0:T(8,128)(2,1)S(1)}, u32[]{:S(2)}, u32[]{:S(2)}) collective-permute-start(bf16[128,1024]{1,0:T(8,128)(2,1)S(1)} %get-tuple-element.106), channel_id=1, source_target_pairs={{0,6},{1,7},{2,4},{3,5},{4,2},{5,3},{6,0},{7,1},{8,14},{9,15},{10,... | collective-permute-start | bytes 786440 | tf_op jit(solution)/shard_map/ppermute | solution.py:352
  102.5 24.9 %collective-permute-start.24 = (bf16[256,768]{1,0:T(8,128)(2,1)S(1)}, bf16[256,768]{1,0:T(8,128)(2,1)S(1)}, u32[]{:S(2)}, u32[]{:S(2)}) collective-permute-start(bf16[256,768]{1,0:T(8,128)(2,1)S(1)} %add_convert_fusion), channel_id=1, source_target_pairs={{0,16},{8,24},{16,0},{24,8},{1,17},{9,25},{17,1},{25,9},{2,18},{10... | collective-permute-start | bytes 1179656 | tf_op jit(solution)/shard_map/ppermute | solution.py:377
  107.2 7.8 %collective-permute-start.18 = (bf16[512,1024]{1,0:T(8,128)(2,1)S(1)}, bf16[512,1024]{1,0:T(8,128)(2,1)S(1)}, u32[]{:S(2)}, u32[]{:S(2)}) collective-permute-start(bf16[512,1024]{1,0:T(8,128)(2,1)S(1)} %get-tuple-element.88), channel_id=1, source_target_pairs={{0,1},{1,0},{2,3},{3,2},{4,5},{5,4},{6,7},{7,6},{8,9},{9,8},{10,11... | collective-permute-start | bytes 3145736 | tf_op jit(solution)/shard_map/ppermute | solution.py:380
  115.7 14.4 %collective-permute-start.21 = (bf16[128,1024]{1,0:T(8,128)(2,1)S(1)}, bf16[128,1024]{1,0:T(8,128)(2,1)S(1)}, u32[]{:S(2)}, u32[]{:S(2)}) collective-permute-start(bf16[128,1024]{1,0:T(8,128)(2,1)S(1)} %get-tuple-element.94), channel_id=1, source_target_pairs={{0,6},{1,7},{2,4},{3,5},{4,2},{5,3},{6,0},{7,1},{8,14},{9,15},{10,... | collective-permute-start | bytes 786440 | tf_op jit(solution)/shard_map/ppermute | solution.py:352
  117.3 12.8 %collective-permute-start.20 = (bf16[128,1024]{1,0:T(8,128)(2,1)S(1)}, bf16[128,1024]{1,0:T(8,128)(2,1)S(1)}, u32[]{:S(2)}, u32[]{:S(2)}) collective-permute-start(bf16[128,1024]{1,0:T(8,128)(2,1)S(1)} %get-tuple-element.93), channel_id=1, source_target_pairs={{0,4},{1,5},{2,6},{3,7},{4,0},{5,1},{6,2},{7,3},{8,12},{9,13},{10,... | collective-permute-start | bytes 786440 | tf_op jit(solution)/shard_map/ppermute | solution.py:352
  117.8 12.3 %collective-permute-start.19 = (bf16[128,1024]{1,0:T(8,128)(2,1)S(1)}, bf16[128,1024]{1,0:T(8,128)(2,1)S(1)}, u32[]{:S(2)}, u32[]{:S(2)}) collective-permute-start(bf16[128,1024]{1,0:T(8,128)(2,1)S(1)} %get-tuple-element.92), channel_id=1, source_target_pairs={{0,2},{1,3},{2,0},{3,1},{4,6},{5,7},{6,4},{7,5},{8,10},{9,11},{10,... | collective-permute-start | bytes 786440 | tf_op jit(solution)/shard_map/ppermute | solution.py:352
  119.3 13.4 %collective-permute-start.22 = (bf16[128,1024]{1,0:T(8,128)(2,1)S(1)}, bf16[128,1024]{1,0:T(8,128)(2,1)S(1)}, u32[]{:S(2)}, u32[]{:S(2)}) collective-permute-start(bf16[128,1024]{1,0:T(8,128)(2,1)S(1)} %get-tuple-element.95), channel_id=1, source_target_pairs={{0,16},{8,24},{16,0},{24,8},{1,17},{9,25},{17,1},{25,9},{2,18},{10... | collective-permute-start | bytes 786440 | tf_op jit(solution)/shard_map/ppermute | solution.py:387
